TPU v7x, 32 devices: a whole 2x2x4 slice. The times are simulated.
32 devices in a mesh: ctx: 2 (over x), exp: 16 (over z, y, core).
Axes of the slice: x: 2, y: 2, z: 4, core: 2. Of those that a mesh axis runs over, the one named last changes fastest.
Arguments:
- q_input: bfloat16 [1024, 8192], P('ctx', 'exp'), may hold values from -8 to 8
- k_input: bfloat16 [1024, 8192], P('ctx', 'exp'), may hold values from -8 to 8
- v_input: bfloat16 [1024, 8192], P('ctx', 'exp'), may hold values from -6 to 6
- segment_ids: int32 [1024], P('ctx'), may hold values from 0 to 5, never falling along the last dimension, each value on 1 to 512 neighbouring positions
- tokens: bfloat16 [1024, 5120], P('exp'), may hold values from -6 to 6
- expert_ids: int32 [1024, 6], P('exp'), may hold values from 0 to 15, all different within a row; in each aligned block of 64 rows (0 to 63, 64 to 127, ...) at most 32 rows name the same one
- route_weight: float32 [1024, 6], P('exp'), may hold values from 0.2 to 1
- w_in: bfloat16 [16, 2, 5120, 1536], P('exp', None, None, 'ctx'), may hold values from -0.078125 to 0.078125
- w_down: bfloat16 [16, 1536, 5120], P('exp', 'ctx'), may hold values from -0.15625 to 0.15625
Outputs:
- attn_out: bfloat16 [1024, 8192], P('ctx', 'exp')
- moe_out: bfloat16 [1024, 5120], P('exp', 'ctx')
Inputs may be any that keep to these rules, and one draw needn't show every extreme that they name: `segment_ids`: never falling along the sequence; each document has 1 to 512 tokens, one exactly 512. `expert_ids`: each row names 6 different experts; in each aligned block of 64 rows no expert is named by more than 32 rows, a bound that some block reaches.
All inputs are finite; a program needn't handle non-finite values.
Results may differ from a plain program's by a relative error of at most 0.0066.
Values may be sent and summed in bfloat16 or wider, within the bound.
No kernel may reach another device: no remote copies, remote signals or barrier semaphores. Data moves between devices by JAX's collectives and lax.ppermute only.
A program may use at most 192 MiB of HBM per device.

v0:
```python
import jax
import jax.numpy as jnp
from jax import lax
from jax.sharding import PartitionSpec as P

HD = 128
TOP = 6


def on_device(
    q_input, k_input, v_input, segment_ids, tokens, expert_ids, route_weight, w_in, w_down
):
    scale = HD ** (-0.5)
    query_rows = q_input.shape[0]
    heads_here = q_input.shape[1] // HD
    query_place = lax.axis_index("ctx") * query_rows + jnp.arange(query_rows, dtype=jnp.int32)
    queries = q_input.reshape(query_rows, heads_here, HD)
    running = jnp.full((query_rows, heads_here), -1e30, jnp.float32)
    keys = lax.all_gather(k_input, "ctx", axis=0, tiled=True)
    values = lax.all_gather(v_input, "ctx", axis=0, tiled=True)
    key_docs = lax.all_gather(segment_ids, "ctx", axis=0, tiled=True)
    count = keys.shape[0]
    key_place = jnp.arange(count, dtype=jnp.int32)
    visible = (key_place[None, :] <= query_place[:, None]) & (
        key_docs[None, :] == segment_ids[:, None]
    )
    scores = (
        jnp.einsum(
            "qhd,khd->qhk",
            queries,
            keys.reshape(count, heads_here, HD),
            preferred_element_type=jnp.float32,
        )
        * scale
    )
    scores = jnp.where(visible[:, None, :], scores, -1e30)
    newest = jnp.maximum(running, jnp.max(scores, axis=2))
    probs = jnp.where(visible[:, None, :], jnp.exp(scores - newest[:, :, None]), 0.0)
    total = jnp.sum(probs, axis=2)
    summed = jnp.einsum(
        "qhk,khd->qhd",
        probs.astype(jnp.bfloat16),
        values.reshape(count, heads_here, HD),
        preferred_element_type=jnp.float32,
    )
    running, total, summed = (newest, total, summed)
    attn_out = (
        (summed / total[:, :, None]).reshape(query_rows, heads_here * HD).astype(jnp.bfloat16)
    )
    rows = tokens.shape[0]
    experts = lax.axis_size("exp")
    cap = rows * 8 // experts
    slots = experts * cap
    flat = expert_ids.reshape(rows * TOP)
    onehot = (flat[:, None] == jnp.arange(experts, dtype=jnp.int32)[None, :]).astype(jnp.int32)
    rank = jnp.sum((jnp.cumsum(onehot, axis=0) - onehot) * onehot, axis=1)
    dest = (flat * cap + rank).reshape(rows, TOP)
    matches = jnp.arange(slots, dtype=jnp.int32)[:, None, None] == dest[None, :, :]
    placing = jnp.any(matches, axis=2).astype(jnp.bfloat16)
    weighting = jnp.sum(jnp.where(matches, route_weight[None, :, :], 0.0), axis=2)
    gate_proj = w_in[0, 0]
    up_proj = w_in[0, 1]
    outgoing = jnp.dot(placing, tokens, preferred_element_type=jnp.float32).astype(jnp.bfloat16)
    arrived = lax.all_to_all(outgoing, "exp", split_axis=0, concat_axis=0, tiled=True)
    gate = jnp.dot(arrived, gate_proj, preferred_element_type=jnp.float32)
    up = jnp.dot(arrived, up_proj, preferred_element_type=jnp.float32)
    hidden = (jax.nn.silu(gate) * up).astype(jnp.bfloat16)
    down_proj = w_down[0]
    summed_out = lax.psum_scatter(
        lax.dot_general(
            down_proj, hidden, (((0,), (1,)), ((), ())), preferred_element_type=jnp.float32
        ).astype(jnp.bfloat16),
        "ctx",
        scatter_dimension=0,
        tiled=True,
    )
    returned = lax.all_to_all(summed_out, "exp", split_axis=1, concat_axis=1, tiled=True)
    mixed = lax.dot_general(
        weighting,
        returned.astype(jnp.float32),
        (((0,), (1,)), ((), ())),
        precision=lax.Precision.HIGHEST,
        preferred_element_type=jnp.float32,
    )
    return (attn_out, mixed.astype(jnp.bfloat16))


def solution(mesh):
    in_specs = (
        P("ctx", "exp"),
        P("ctx", "exp"),
        P("ctx", "exp"),
        P("ctx"),
        P("exp", None),
        P("exp", None),
        P("exp", None),
        P("exp", None, None, "ctx"),
        P("exp", "ctx", None),
    )
    out_specs = (P("ctx", "exp"), P("exp", "ctx"))
    return jax.shard_map(
        on_device, mesh=mesh, in_specs=in_specs, out_specs=out_specs, check_vma=False
    )
```

profile of v0, /device:TPU:0, one launch (start us, length us, event | category | flops | bytes accessed | tf_op | source)
XLA Modules:
  0.0 298.6 jit_solution(13402072255765026008)
XLA Ops:
  7.2 0.8 copy.58
  8.1 0.1 eq.63
  8.2 0.1 eq.59
  8.4 0.9 reduce-window.6
  9.2 0.2 slice_reduce_fusion
  9.5 0.1 fusion.37
  9.6 0.1 reduce_sum.31
  9.7 0.1 copy.61
  9.8 0.7 multiply_add_fusion
  10.5 0.2 fusion.31
  10.7 1.6 convolution_convert_fusion
  12.3 122.2 %all_to_all.24 = bf16[16,32,5120]{2,1,0:T(8,128)(2,1)S(1)} all-to-all(bf16[16,32,5120]{2,1,0:T(8,128)(2,1)S(1)} %bitcast.84), channel_id=1, replica_groups=mesh['ctx'=2,'exp'=16] {'exp'}, dimensions={0} | all-to-all | bytes 10485760 | tf_op jit(solution)/shard_map/all_to_all | solution.py:64
  134.4 2.3 copy-done.1
  136.8 4.3 %fusion.4 = f32[512,768]{1,0:T(8,128)S(1)} fusion(bf16[512,5120]{1,0:T(8,128)(2,1)S(1)} %bitcast.86, bf16[1,2,5120,768]{3,2,1,0:T(8,128)(2,1)S(1)} %copy-done.6), kind=kOutput, calls=%fused_computation.6 | convolution fusion | flops 4026531840 | bytes 14680064 | tf_op jit(solution)/shard_map/dot_general | solution.py:65
  141.1 18.6 %fusion.12 = bf16[5120,512]{0,1:T(8,128)(2,1)} fusion(bf16[1,768,5120]{2,1,0:T(8,128)(2,1)} %param.17, f32[512,768]{1,0:T(8,128)S(1)} %fusion.4, bf16[512,5120]{1,0:T(8,128)(2,1)} %bitcast.87, bf16[1,2,5120,768]{3,2,1,0:T(8,128)(2,1)} %param.16), kind=kOutput, calls=%fused_computation.13 | convolution fusion | flops 8058044416 | bytes 27787264 | tf_op jit(solution)/shard_map/dot_general | solution.py:70
  159.7 66.5 %reduce-scatter.2.cloned.1.call-done = bf16[2560,512]{0,1:T(8,128)(2,1)} async-done(((bf16[5120,512]{0,1:T(8,128)(2,1)}), bf16[2560,512]{0,1:T(8,128)(2,1)}) %reduce-scatter.2.cloned.1.call-update) | async-done | bytes 2621456 | tf_op jit(solution)/shard_map/reduce_scatter | solution.py:69
  226.2 5.6 %all-to-all-start.1 = ((bf16[2560,16,32]{0,2,1:T(8,128)(2,1)}), bf16[2560,16,32]{0,2,1:T(8,128)(2,1)S(1)}, u32[]{:S(2)}, u32[]{:S(2)}) async-start(bf16[2560,16,32]{0,2,1:T(8,128)(2,1)} %bitcast.88), calls=%async_computation.2 | async-start | bytes 5242880 | tf_op jit(solution)/shard_map/all_to_all | solution.py:77
  231.8 0.0 all-gather.6.cloned.1.call-start
  231.9 0.7 all-gather.6.cloned.1.call-update
  232.6 0.0 all-gather.4.cloned.1.call-start
  232.6 2.0 copy.53
  234.7 4.5 %all-gather = s32[2,1,512]{2,1,0:T(1,128)S(1)} all-gather(s32[1,1,512]{2,1,0:T(1,128)S(1)} %bitcast.93), channel_id=1, replica_groups=mesh['ctx'=2,'exp'=16] {'ctx'}, dimensions={0}, use_global_device_ids=true | all-gather | bytes 6144 | tf_op jit(solution)/shard_map/all_gather | solution.py:21
  239.3 0.2 select_reduce_fusion
  239.4 1.3 fusion.20
  240.7 15.3 %all-gather.6.cloned.1.call-done = bf16[1024,512]{1,0:T(8,128)(2,1)} async-done(((bf16[512,512]{1,0:T(8,128)(2,1)}), bf16[1024,512]{1,0:T(8,128)(2,1)}) %all-gather.6.cloned.1.call-update) | async-done | bytes 1048592 | tf_op jit(solution)/shard_map/all_gather | solution.py:20
  256.0 2.3 copy.56
  258.3 20.7 %all-gather.4.cloned.1.call-done = bf16[1024,512]{0,1:T(8,128)(2,1)} async-done(((bf16[512,512]{0,1:T(8,128)(2,1)}), bf16[1024,512]{0,1:T(8,128)(2,1)}) %all-gather.4.cloned.1.call-update) | async-done | bytes 1048592 | tf_op jit(solution)/shard_map/all_gather | solution.py:19
  279.0 3.4 %fusion.11 = (f32[512,4]{0,1:T(4,128)S(1)}, f32[4,1024,512]{2,1,0:T(8,128)S(1)}) fusion(pred[512,1024]{0,1:T(8,128)(4,1)} %fusion.20, bf16[1024,4,128]{0,2,1:T(8,128)(2,1)} %bitcast.89, bf16[512,512]{1,0:T(8,128)(2,1)} %param.9), kind=kOutput, calls=%fused_computation.12 | convolution fusion | flops 543160320 | bytes 10493952 | tf_op jit(solution)/shard_map/qhd,khd->qhk/dot_general | solution.py:28
  282.5 2.1 fusion.15
  284.6 3.2 %divide_convert_fusion = bf16[512,4,128]{0,2,1:T(8,128)(2,1)} fusion(bf16[1024,4,128]{0,2,1:T(8,128)(2,1)S(1)} %bitcast.90, f32[4,1024,512]{2,1,0:T(8,128)S(1)} %get-tuple-element.13, f32[512,4]{0,1:T(4,128)S(1)} %broadcast_maximum_fusion, pred[512,1024]{0,1:T(8,128)(4,1)S(1)} %copy-done.2, f32[512,4]{0,1:T(4,128)S(1)} %fusion.15), kind=kOutput, calls=%fused_computation.23 | convolution fusion | flops 547880960 | bytes 10502144 | tf_op jit(solution)/shard_map/qhk,khd->qhd/dot_general | solution.py:40
  287.8 2.0 copy.62
  289.9 2.2 convolution_convert_fusion.1
  (21 shorter events, 0.2 us)
Async XLA Ops:
  7.2 3.5 %copy-start = (bf16[64,5120]{1,0:T(8,128)(2,1)S(1)}, bf16[64,5120]{1,0:T(8,128)(2,1)}, u32[]{:S(2)}) copy-start(bf16[64,5120]{1,0:T(8,128)(2,1)} %param.13) | copy-start | bytes 1966084
  7.2 219.0 %reduce-scatter.2.cloned.1.call-start = ((), (), s32[]{:S(2)}) async-start(), calls=%async_computation.5 | async-start | bytes 7864320 | tf_op jit(solution)/shard_map/reduce_scatter | solution.py:69
  10.7 126.1 %copy-start.6 = (bf16[1,2,5120,768]{3,2,1,0:T(8,128)(2,1)S(1)}, bf16[1,2,5120,768]{3,2,1,0:T(8,128)(2,1)}, u32[]{:S(2)}) copy-start(bf16[1,2,5120,768]{3,2,1,0:T(8,128)(2,1)} %param.16) | copy-start | bytes 47185924
  134.4 2.3 copy-start.1
  159.7 75.0 %copy-start.4 = (s32[512]{0:T(512)S(1)}, s32[512]{0:T(512)}, u32[]{:S(2)}) copy-start(s32[512]{0:T(512)} %param.12) | copy-start | bytes 6148
  159.7 79.6 %copy-start.5 = (f32[64,6]{0,1:T(8,128)S(1)}, f32[64,6]{0,1:T(8,128)}, u32[]{:S(2)}) copy-start(f32[64,6]{0,1:T(8,128)} %param.15) | copy-start | bytes 4612
  226.2 63.7 %all-to-all-start.1 = ((bf16[2560,16,32]{0,2,1:T(8,128)(2,1)}), bf16[2560,16,32]{0,2,1:T(8,128)(2,1)S(1)}, u32[]{:S(2)}, u32[]{:S(2)}) async-start(bf16[2560,16,32]{0,2,1:T(8,128)(2,1)} %bitcast.88), calls=%async_computation.2 | async-start | bytes 5242880 | tf_op jit(solution)/shard_map/all_to_all | solution.py:77
  231.8 24.2 %all-gather.6.cloned.1.call-start = ((), (), s32[]{:S(2)}) async-start(), calls=%async_computation.4 | async-start | bytes 1572864 | tf_op jit(solution)/shard_map/all_gather | solution.py:20
  232.6 46.4 %all-gather.4.cloned.1.call-start = ((), (), s32[]{:S(2)}) async-start(), calls=%async_computation.3 | async-start | bytes 1572864 | tf_op jit(solution)/shard_map/all_gather | solution.py:19
  279.0 3.5 %copy-start.2 = (pred[512,1024]{0,1:T(8,128)(4,1)S(1)}, pred[512,1024]{0,1:T(8,128)(4,1)}, u32[]{:S(2)}) copy-start(pred[512,1024]{0,1:T(8,128)(4,1)} %fusion.20) | copy-start | bytes 1572868
  279.0 5.6 %copy-start.3 = (bf16[1024,512]{0,1:T(8,128)(2,1)S(1)}, bf16[1024,512]{0,1:T(8,128)(2,1)}, u32[]{:S(2)}) copy-start(bf16[1024,512]{0,1:T(8,128)(2,1)} %copy.56) | copy-start | bytes 3145732
Sparse Core Ops, SparseCore 0:
  159.8 66.3 reduce-scatter.1
  234.3 21.6 all-gather.5
  257.7 21.2 all-gather.3
where the time goes:
time: 299 us
  blocking collectives  127 us (42%)
  waiting for transfers between devices  103 us (34%)
  matrix products  33.3 us (11%)
  between operations  13.9 us (5%)
  local copies, waits for them, and re-layouts  10.3 us (3%)
  starting transfers between devices  5.75 us (2%)
  other arithmetic  5.45 us (2%)
    all_to_all x1, blocking collectives, on_device(): lax.all_to_all(outgoing, 'exp', split_axis=0, concat_axis=0, tiled=True)  122 us
    reduce_scatter x1, waiting for transfers between devices, on_device(): lax.psum_scatter(lax.dot_general(down_proj, hidden, (((0,), (1,)), ((), (...  66.5 us
    all_gather x1, waiting for transfers between devices, on_device(): keys = lax.all_gather(k_input, 'ctx', axis=0, tiled=True)  20.7 us
    dot_general x1, matrix products, on_device(): lax.dot_general(down_proj, hidden, (((0,), (1,)), ((), ())), preferred_el...  18.6 us
    all_gather x1, waiting for transfers between devices, on_device(): values = lax.all_gather(v_input, 'ctx', axis=0, tiled=True)  15.3 us
    unnamed x17, local copies, waits for them, and re-layouts  7.3 us
  transfers between devices with their start and end apart: 4, of which 3 were waited for; matrix products, arithmetic and copies ran while one was open for 6% of the time, Pallas kernels for 0%

commit v1 on v0

v1 whole, which is shorter than its diff:
```python
import jax
import jax.numpy as jnp
from jax import lax
from jax.sharding import PartitionSpec as P

HD = 128
TOP = 6
BF16 = jnp.bfloat16
F32 = jnp.float32


def attend(q_input, k_input, v_input, segment_ids, n_ctx):
    scale = HD ** (-0.5)
    rows = q_input.shape[0]
    heads = q_input.shape[1] // HD
    place = lax.axis_index("ctx") * rows + jnp.arange(rows, dtype=jnp.int32)
    if n_ctx == 2:
        ahead = [(0, 1)]
        keys = jnp.concatenate([lax.ppermute(k_input, "ctx", ahead), k_input], axis=0)
        values = jnp.concatenate([lax.ppermute(v_input, "ctx", ahead), v_input], axis=0)
        docs = jnp.concatenate([lax.ppermute(segment_ids, "ctx", ahead), segment_ids], axis=0)
        first = (lax.axis_index("ctx") - 1) * rows
    else:
        keys = lax.all_gather(k_input, "ctx", axis=0, tiled=True)
        values = lax.all_gather(v_input, "ctx", axis=0, tiled=True)
        docs = lax.all_gather(segment_ids, "ctx", axis=0, tiled=True)
        first = 0
    count = keys.shape[0]
    key_place = first + jnp.arange(count, dtype=jnp.int32)
    visible = (
        (key_place[None, :] <= place[:, None])
        & (key_place[None, :] >= 0)
        & (docs[None, :] == segment_ids[:, None])
    )
    queries = q_input.reshape(rows, heads, HD)
    scores = (
        jnp.einsum(
            "qhd,khd->qhk", queries, keys.reshape(count, heads, HD), preferred_element_type=F32
        )
        * scale
    )
    scores = jnp.where(visible[:, None, :], scores, -1e30)
    newest = jnp.max(scores, axis=2)
    probs = jnp.where(visible[:, None, :], jnp.exp(scores - newest[:, :, None]), 0.0)
    total = jnp.sum(probs, axis=2)
    summed = jnp.einsum(
        "qhk,khd->qhd",
        probs.astype(BF16),
        values.reshape(count, heads, HD),
        preferred_element_type=F32,
    )
    return (summed / total[:, :, None]).reshape(rows, heads * HD).astype(BF16)


def spread(onehot):
    blocks, cap, rows = onehot.shape
    same = jnp.eye(blocks, dtype=jnp.bool_)
    wide = onehot[:, :, None, :] & same[:, None, :, None]
    return wide.reshape(blocks * cap, blocks * rows).astype(BF16)


def solution(mesh):
    n_ctx = mesh.shape["ctx"]
    n_exp = mesh.shape["exp"]
    nz = n_exp // 4

    def pairs(move):
        out = []
        for i in range(n_exp):
            z, y, c = i // 4, (i // 2) % 2, i % 2
            z, y, c = move(z, y, c)
            out.append((i, (z % nz * 2 + y) * 2 + c))
        return out

    def z_shift(x, d):
        return lax.ppermute(x, "exp", pairs(lambda z, y, c: (z + d, y, c)))

    def y_swap(x):
        return lax.ppermute(x, "exp", pairs(lambda z, y, c: (z, 1 - y, c)))

    def core_swap(x):
        return lax.ppermute(x, "exp", pairs(lambda z, y, c: (z, y, 1 - c)))

    def x_swap(x):
        return lax.ppermute(x, "ctx", [(0, 1), (1, 0)])

    def on_device(
        q_input, k_input, v_input, segment_ids, tokens, expert_ids, route_weight, w_in, w_down
    ):
        me = lax.axis_index("exp")
        at_x = lax.axis_index("ctx")
        rows, width = tokens.shape
        cap = rows * 8 // n_exp
        half = width // 2
        near = n_exp // 2
        slots = near * cap

        if n_ctx == 2:
            plan = [("x", 1024), ("x", 1024), ("", 1024), ("x", 1024), ("", 1024)]
        else:
            plan = [("", width)]
        arrived = []
        start = 0
        for kind, size in plan:
            if kind == "x":
                block = lax.dynamic_slice_in_dim(tokens, start + at_x * (size // 2), size // 2, 1)
            else:
                block = tokens[:, start : start + size]
            line = jnp.concatenate([block] + [z_shift(block, d) for d in range(1, nz)], axis=0)
            both = jnp.concatenate([line, y_swap(line)], axis=0)
            if kind == "x":
                other = x_swap(both)
                both = jnp.concatenate(
                    [jnp.where(at_x == 0, both, other), jnp.where(at_x == 0, other, both)], axis=1
                )
            arrived.append((start, size, both))
            start += size

        meta = jnp.concatenate([expert_ids.astype(F32), route_weight], axis=1)
        meta = lax.all_gather(meta, "exp", axis=0, tiled=False)
        z, y, c = me // 4, (me // 2) % 2, me % 2
        order = jnp.stack(
            [
                ((z - d + nz) % nz * 2 + (y + yr) % 2) * 2 + (c + cr) % 2
                for cr in range(2)
                for yr in range(2)
                for d in range(nz)
            ]
        )
        meta = meta[order]
        ids, weights = meta[:, :, :TOP].astype(jnp.int32), meta[:, :, TOP:]

        def placing(ids, expert):
            named = ids == expert
            hit = jnp.any(named, axis=2)
            count = hit.astype(jnp.int32)
            rank = jnp.cumsum(count, axis=1) - count
            slot = jnp.arange(cap, dtype=jnp.int32)
            return named, hit[:, None, :] & (rank[:, None, :] == slot[None, :, None])

        named, mine = placing(ids, me)
        _, others = placing(ids[:near], me + 1 - 2 * c)
        weight = jnp.sum(jnp.where(named, weights, 0.0), axis=2)
        weight = jnp.sum(jnp.where(mine, weight[:, None, :], 0.0), axis=2).reshape(2 * slots, 1)
        place = jnp.concatenate([spread(mine[:near]), spread(others)], axis=0)

        gate = up = None
        for start, size, both in arrived:
            placed = jnp.dot(place, both, preferred_element_type=F32).astype(BF16)
            block = jnp.concatenate([placed[:slots], core_swap(placed[slots:])], axis=0)
            g = jnp.dot(block, w_in[0, 0, start : start + size], preferred_element_type=F32)
            u = jnp.dot(block, w_in[0, 1, start : start + size], preferred_element_type=F32)
            gate = g if gate is None else gate + g
            up = u if up is None else up + u
        hidden = (jax.nn.silu(gate) * up).astype(BF16)

        if n_ctx == 2:
            back = [("x", 512), ("x", 512), ("", 512), ("x", 512), ("", 512)]
        else:
            back = [("", half)]
        down = w_down[0]
        pieces = []
        start = 0
        for kind, size in back:
            if n_ctx == 2:
                cols = jnp.concatenate(
                    [down[:, start : start + size], down[:, half + start : half + start + size]],
                    axis=1,
                )
            else:
                cols = down
            part = jnp.dot(hidden, cols, preferred_element_type=F32)
            part = (part * weight).astype(BF16)
            part = jnp.concatenate([part[:slots], core_swap(part[slots:])], axis=0)
            summed = lax.dot_general(
                place, part, (((0,), (0,)), ((), ())), preferred_element_type=F32
            )

            def over_x(summed):
                first, second = summed[:, :size].astype(BF16), summed[:, size:].astype(BF16)
                other = x_swap(jnp.where(at_x == 0, second, first))
                own = jnp.where(at_x == 0, summed[:, :size], summed[:, size:])
                return own + other.astype(F32)

            if kind == "x":
                summed = over_x(summed)
            count = nz * rows
            summed = summed[:count] + y_swap(summed[count:].astype(BF16)).astype(F32)
            total = summed[:rows]
            for d in range(1, nz):
                block = summed[d * rows : (d + 1) * rows].astype(BF16)
                total = total + z_shift(block, -d).astype(F32)
            if kind != "x":
                if n_ctx == 2:
                    total = over_x(total)
                else:
                    total = lax.psum_scatter(
                        total.astype(BF16), "ctx", scatter_dimension=1, tiled=True
                    )
            pieces.append(total.astype(BF16))
            start += size
        moe_out = jnp.concatenate(pieces, axis=1)
        attn_out = attend(q_input, k_input, v_input, segment_ids, n_ctx)
        return attn_out, moe_out

    in_specs = (
        P("ctx", "exp"),
        P("ctx", "exp"),
        P("ctx", "exp"),
        P("ctx"),
        P("exp", None),
        P("exp", None),
        P("exp", None),
        P("exp", None, None, "ctx"),
        P("exp", "ctx", None),
    )
    out_specs = (P("ctx", "exp"), P("exp", "ctx"))
    return jax.shard_map(
        on_device, mesh=mesh, in_specs=in_specs, out_specs=out_specs, check_vma=False
    )
```

time: 299 us -> 272 us (0.910); the launches traced: 299 us -> 268 us
  blocking collectives: 127 us -> 20.6 us
  starting transfers between devices: 5.75 us -> 75.5 us
  waiting for transfers between devices: 103 us -> 60.8 us
  local copies, waits for them, and re-layouts: 10.3 us -> 35.1 us
  matrix products: 33.3 us -> 52 us
  other arithmetic: 5.45 us -> 22.2 us
  between operations: 13.9 us -> 1.96 us
    all_to_all x1 -> x0, blocking collectives: 122 us -> none  [on_device(): lax.all_to_all(outgoing, 'exp', split_axis=0, concat_axis=0, tiled=True)]
    ppermute x0 -> x61, starting transfers between devices: none -> 75.5 us  [the longest x30 52.4 us: z_shift(): return lax.ppermute(x, 'exp', pairs(lambda z, y, c: (z + d, y, c)))]
    reduce_scatter x1 -> x0, waiting for transfers between devices: 66.5 us -> none  [on_device(): lax.psum_scatter(lax.dot_general(down_proj, hidden, (((0,), (1,)), ((), (...]
    ppermute x0 -> x61, waiting for transfers between devices: none -> 60.8 us  [the longest x30 25.1 us: z_shift(): return lax.ppermute(x, 'exp', pairs(lambda z, y, c: (z + d, y, c)))]
    all_gather x2 -> x0, waiting for transfers between devices: 36 us -> none  [the longest x1 20.7 us: on_device(): keys = lax.all_gather(k_input, 'ctx', axis=0, tiled=True)]
    dot_general x6 -> x27, matrix products: 33.3 us -> 52 us  [the longest x5 22.3 us: on_device(): jnp.dot(block, w_in[0, 1, start:start + size], preferred_element_type=F32)]
    all_gather x1, blocking collectives: 4.52 us -> 20.6 us  [on_device(): meta = lax.all_gather(meta, 'exp', axis=0, tiled=False)]
    unnamed x17 -> x57, local copies, waits for them, and re-layouts: 7.3 us -> 19.5 us
  transfers between devices with their start and end apart: 4 -> 61, of which waited for: 3 -> 21; matrix products, arithmetic and copies ran while one was open for 6% -> 31% of each run, Pallas kernels for 0% -> 0%
where the time goes in v1:
time: 272 us; the launch traced here: 268 us
  starting transfers between devices  75.5 us (28%)
  waiting for transfers between devices  60.8 us (22%)
  matrix products  52 us (19%)
  local copies, waits for them, and re-layouts  35.1 us (13%)
  other arithmetic  22.2 us (8%)
  blocking collectives  20.6 us (8%)
    ppermute x30, starting transfers between devices, z_shift(): return lax.ppermute(x, 'exp', pairs(lambda z, y, c: (z + d, y, c)))  52.4 us
    ppermute x30, waiting for transfers between devices, z_shift(): return lax.ppermute(x, 'exp', pairs(lambda z, y, c: (z + d, y, c)))  25.1 us
    ppermute x10, waiting for transfers between devices, y_swap(): return lax.ppermute(x, 'exp', pairs(lambda z, y, c: (z, 1 - y, c)))  22.8 us
    dot_general x5, matrix products, on_device(): jnp.dot(block, w_in[0, 1, start:start + size], preferred_element_type=F32)  22.3 us
    all_gather x1, blocking collectives, on_device(): meta = lax.all_gather(meta, 'exp', axis=0, tiled=False)  20.6 us
    unnamed x57, local copies, waits for them, and re-layouts  19.5 us
    ppermute x8, waiting for transfers between devices, x_swap(): return lax.ppermute(x, 'ctx', [(0, 1), (1, 0)])  12.8 us
    dot_general x5, matrix products, on_device(): jnp.dot(block, w_in[0, 0, start:start + size], preferred_element_type=F32)  12 us
  transfers between devices with their start and end apart: 61, of which 21 were waited for; matrix products, arithmetic and copies ran while one was open for 31% of the time, Pallas kernels for 0%

profile of v1, /device:TPU:0, one launch (start us, length us, event | category | flops | bytes accessed | tf_op | source)
XLA Modules:
  0.0 268.1 jit_solution(6111879407805451038)
XLA Ops:
  2.4 4.0 %collective-permute-start.10 = (bf16[64,512]{1,0:T(8,128)(2,1)}, bf16[64,512]{1,0:T(8,128)(2,1)}, u32[]{:S(2)}, u32[]{:S(2)}) collective-permute-start(bf16[64,512]{1,0:T(8,128)(2,1)} %get-tuple-element.23), channel_id=1, source_target_pairs={{0,8},{1,9},{2,10},{3,11},{4,12},{5,13},{6,14},{7,15},{8,0},{9,1},... | collective-permute-start | bytes 196616 | tf_op jit(solution)/shard_map/ppermute | solution.py:76
  10.0 4.0 %collective-permute-start.1 = (s32[512]{0:T(512)}, s32[512]{0:T(512)}, u32[]{:S(2)}, u32[]{:S(2)}) collective-permute-start(s32[512]{0:T(512)} %param.12), channel_id=1, source_target_pairs={{0,16},{1,17},{2,18},{3,19},{4,20},{5,21},{6,22},{7,23},{8,24},{9,... | collective-permute-start | bytes 6152 | tf_op jit(solution)/shard_map/ppermute | solution.py:21
  17.3 20.6 %all-gather.1 = f32[16,64,12]{1,2,0:T(8,128)S(1)} all-gather(f32[1,64,12]{1,2,0:T(8,128)S(1)} %maximum_bitcast_fusion), channel_id=2, replica_groups=mesh['ctx'=2,'exp'=16] {'exp'}, dimensions={0}, use_global_device_ids=true | all-gather | bytes 52224 | tf_op jit(solution)/shard_map/all_gather | solution.py:120
  40.8 5.8 %fusion.153 = (bf16[768,512]{1,0:T(8,128)(2,1)}, bf16[768,512]{1,0:T(8,128)(2,1)}, bf16[768,512]{1,0:T(8,128)(2,1)}, bf16[768,512]{1,0:T(8,128)(2,1)}, bf16[768,...) fusion(bf16[768,5120]{1,0:T(8,128)(2,1)} %bitcast.104), kind=kLoop, calls=%fused_computation.257 | loop fusion | bytes 15728640 | tf_op jit(solution)/shard_map/slice | solution.py:167
  53.9 2.8 %collective-permute-start.4 = (bf16[64,512]{1,0:T(8,128)(2,1)}, bf16[64,512]{1,0:T(8,128)(2,1)S(1)}, u32[]{:S(2)}, u32[]{:S(2)}) collective-permute-start(bf16[64,512]{1,0:T(8,128)(2,1)} %get-tuple-element.69), channel_id=1, source_target_pairs={{0,8},{1,9},{2,10},{3,11},{4,12},{5,13},{6,14},{7,15},{8,0},{9,1},... | collective-permute-start | bytes 196616 | tf_op jit(solution)/shard_map/ppermute | solution.py:76
  66.3 2.8 %collective-permute-start.17 = (bf16[64,1024]{1,0:T(8,128)(2,1)}, bf16[64,1024]{1,0:T(8,128)(2,1)S(1)}, u32[]{:S(2)}, u32[]{:S(2)}) collective-permute-start(bf16[64,1024]{1,0:T(8,128)(2,1)} %get-tuple-element.67), channel_id=1, source_target_pairs={{0,12},{1,13},{2,14},{3,15},{4,0},{5,1},{6,2},{7,3},{8,4},{9,5},{1... | collective-permute-start | bytes 393224 | tf_op jit(solution)/shard_map/ppermute | solution.py:76
  72.2 2.8 %collective-permute-start.28 = (bf16[64,1024]{1,0:T(8,128)(2,1)S(1)}, bf16[64,1024]{1,0:T(8,128)(2,1)S(1)}, u32[]{:S(2)}, u32[]{:S(2)}) collective-permute-start(bf16[64,1024]{1,0:T(8,128)(2,1)S(1)} %get-tuple-element.64), channel_id=1, source_target_pairs={{0,12},{1,13},{2,14},{3,15},{4,0},{5,1},{6,2},{7,3},{8,4},{9,5},{1... | collective-permute-start | bytes 393224 | tf_op jit(solution)/shard_map/ppermute | solution.py:76
  75.6 3.8 %collective-permute-done.16 = bf16[64,1024]{1,0:T(8,128)(2,1)S(1)} collective-permute-done((bf16[64,1024]{1,0:T(8,128)(2,1)}, bf16[64,1024]{1,0:T(8,128)(2,1)S(1)}, u32[]{:S(2)}, u32[]{:S(2)}) %collective-permute-start.16) | collective-permute-done | bytes 131104 | tf_op jit(solution)/shard_map/ppermute | solution.py:76
  91.5 2.6 collective-permute-done.12
  94.9 4.9 %collective-permute-done.23 = bf16[256,512]{1,0:T(8,128)(2,1)S(1)} collective-permute-done((bf16[256,512]{1,0:T(8,128)(2,1)S(1)}, bf16[256,512]{1,0:T(8,128)(2,1)S(1)}, u32[]{:S(2)}, u32[]{:S(2)}) %collective-permute-start.23) | collective-permute-done | bytes 262176 | tf_op jit(solution)/shard_map/ppermute | solution.py:79
  100.5 4.9 %collective-permute-done.6 = bf16[256,512]{1,0:T(8,128)(2,1)S(1)} collective-permute-done((bf16[256,512]{1,0:T(8,128)(2,1)S(1)}, bf16[256,512]{1,0:T(8,128)(2,1)S(1)}, u32[]{:S(2)}, u32[]{:S(2)}) %collective-permute-start.6) | collective-permute-done | bytes 262176 | tf_op jit(solution)/shard_map/ppermute | solution.py:79
  108.9 5.9 %fusion.170 = (f32[512,4]{0,1:T(4,128)S(1)}, bf16[512,4,1024]{0,2,1:T(8,128)(2,1)}) fusion(f32[4,1024,512]{2,1,0:T(8,128)S(1)} %fusion.95, pred[512,1024]{0,1:T(8,128)(4,1)S(1)} %compare_and_fusion), kind=kOutput, calls=%fused_computation.274 | output fusion | flops 16778240 | bytes 13115392 | tf_op jit(solution)/shard_map/sub | solution.py:44
  116.8 2.9 %fusion.58 = bf16[512,4,128]{0,2,1:T(8,128)(2,1)S(1)} fusion(bf16[1024,4,128]{0,2,1:T(8,128)(2,1)S(1)} %bitcast.106, bf16[512,4,1024]{0,2,1:T(8,128)(2,1)} %get-tuple-element.91, f32[512,4]{0,1:T(4,128)S(1)} %get-tuple-element.90), kind=kOutput, calls=%fused_computation.69 | convolution fusion | flops 537395200 | bytes 5775360 | tf_op jit(solution)/shard_map/qhk,khd->qhd/dot_general | solution.py:46
  127.3 3.2 %collective-permute-done.24 = bf16[512,512]{1,0:T(8,128)(2,1)} collective-permute-done((bf16[512,512]{1,0:T(8,128)(2,1)}, bf16[512,512]{1,0:T(8,128)(2,1)}, u32[]{:S(2)}, u32[]{:S(2)}) %collective-permute-start.24) | collective-permute-done | bytes 524320 | tf_op jit(solution)/shard_map/ppermute | solution.py:85
  133.0 3.1 %collective-permute-done.7 = bf16[512,512]{1,0:T(8,128)(2,1)} collective-permute-done((bf16[512,512]{1,0:T(8,128)(2,1)S(1)}, bf16[512,512]{1,0:T(8,128)(2,1)}, u32[]{:S(2)}, u32[]{:S(2)}) %collective-permute-start.7) | collective-permute-done | bytes 524320 | tf_op jit(solution)/shard_map/ppermute | solution.py:85
  141.9 2.4 fusion.26
  144.3 2.4 fusion.32
  156.3 2.4 fusion.34
  158.7 12.1 %fusion.24 = f32[512,768]{1,0:T(8,128)S(1)} fusion(bf16[1,2,5120,768]{3,2,1,0:T(8,128)(2,1)} %param.16, bf16[256,1024]{1,0:T(8,128)(2,1)S(1)} %collective-permute-done.25, bf16[256,1024]{1,0:T(8,128)(2,1)S(1)} %get-tuple-element.60), kind=kOutput, calls=%fused_computation.33 | convolution fusion | flops 807403520 | bytes 4194304 | tf_op jit(solution)/shard_map/dot_general | solution.py:152
  170.9 3.0 %multiply_convert_fusion.5 = bf16[512,768]{1,0:T(8,128)(2,1)S(1)} fusion(f32[512,768]{1,0:T(8,128)S(1)} %fusion.24, f32[512,768]{1,0:T(8,128)S(1)} %fusion.26, f32[512,768]{1,0:T(8,128)S(1)} %fusion.30, f32[512,768]{1,0:T(8,128)S(1)} %fusion.28, f32[512,768]{1,0:T(8,128)S(1)} %fusion.32, f32[512,768]{1,0:T(8,128)S(1)} %fusion.34, ...), kind=kOutput, calls=%fused_computation.51 | convolution fusion | flops 812908544 | bytes 17563648 | tf_op jit(solution)/shard_map/dot_general | solution.py:152
  193.2 6.7 %collective-permute-done.56 = bf16[256,1024]{1,0:T(8,128)(2,1)S(1)} collective-permute-done((bf16[256,1024]{1,0:T(8,128)(2,1)S(1)}, bf16[256,1024]{1,0:T(8,128)(2,1)S(1)}, u32[]{:S(2)}, u32[]{:S(2)}) %collective-permute-start.56) | collective-permute-done | bytes 524320 | tf_op jit(solution)/shard_map/ppermute | solution.py:79
  201.3 5.5 %collective-permute-start.58 = (bf16[64,1024]{1,0:T(8,128)(2,1)S(1)}, bf16[64,1024]{1,0:T(8,128)(2,1)S(1)}, u32[]{:S(2)}, u32[]{:S(2)}) collective-permute-start(bf16[64,1024]{1,0:T(8,128)(2,1)S(1)} %get-tuple-element.74), channel_id=1, source_target_pairs={{0,8},{1,9},{2,10},{3,11},{4,12},{5,13},{6,14},{7,15},{8,0},{9,1},... | collective-permute-start | bytes 393224 | tf_op jit(solution)/shard_map/ppermute | solution.py:76
  207.1 3.6 %collective-permute-done.44 = bf16[256,1024]{1,0:T(8,128)(2,1)S(1)} collective-permute-done((bf16[256,1024]{1,0:T(8,128)(2,1)S(1)}, bf16[256,1024]{1,0:T(8,128)(2,1)S(1)}, u32[]{:S(2)}, u32[]{:S(2)}) %collective-permute-start.44) | collective-permute-done | bytes 524320 | tf_op jit(solution)/shard_map/ppermute | solution.py:79
  210.7 5.1 %collective-permute-start.59 = (bf16[64,1024]{1,0:T(8,128)(2,1)S(1)}, bf16[64,1024]{1,0:T(8,128)(2,1)S(1)}, u32[]{:S(2)}, u32[]{:S(2)}) collective-permute-start(bf16[64,1024]{1,0:T(8,128)(2,1)S(1)} %get-tuple-element.73), channel_id=1, source_target_pairs={{0,4},{1,5},{2,6},{3,7},{4,8},{5,9},{6,10},{7,11},{8,12},{9,13},{1... | collective-permute-start | bytes 393224 | tf_op jit(solution)/shard_map/ppermute | solution.py:76
  217.0 6.0 %collective-permute-done.32 = bf16[512,512]{1,0:T(8,128)(2,1)S(1)} collective-permute-done((bf16[512,512]{1,0:T(8,128)(2,1)S(1)}, bf16[512,512]{1,0:T(8,128)(2,1)S(1)}, u32[]{:S(2)}, u32[]{:S(2)}) %collective-permute-start.32) | collective-permute-done | bytes 524320 | tf_op jit(solution)/shard_map/ppermute | solution.py:85
  224.1 6.1 %collective-permute-start.46 = (bf16[64,1024]{1,0:T(8,128)(2,1)S(1)}, bf16[64,1024]{1,0:T(8,128)(2,1)S(1)}, u32[]{:S(2)}, u32[]{:S(2)}) collective-permute-start(bf16[64,1024]{1,0:T(8,128)(2,1)S(1)} %get-tuple-element.77), channel_id=1, source_target_pairs={{0,8},{1,9},{2,10},{3,11},{4,12},{5,13},{6,14},{7,15},{8,0},{9,1},... | collective-permute-start | bytes 393224 | tf_op jit(solution)/shard_map/ppermute | solution.py:76
  232.9 8.0 %collective-permute-done.46 = bf16[64,1024]{1,0:T(8,128)(2,1)S(1)} collective-permute-done((bf16[64,1024]{1,0:T(8,128)(2,1)S(1)}, bf16[64,1024]{1,0:T(8,128)(2,1)S(1)}, u32[]{:S(2)}, u32[]{:S(2)}) %collective-permute-start.46) | collective-permute-done | bytes 131104 | tf_op jit(solution)/shard_map/ppermute | solution.py:76
  243.2 3.3 %collective-permute-start.34 = (bf16[64,512]{1,0:T(8,128)(2,1)S(1)}, bf16[64,512]{1,0:T(8,128)(2,1)S(1)}, u32[]{:S(2)}, u32[]{:S(2)}) collective-permute-start(bf16[64,512]{1,0:T(8,128)(2,1)S(1)} %get-tuple-element.84), channel_id=1, source_target_pairs={{0,12},{1,13},{2,14},{3,15},{4,0},{5,1},{6,2},{7,3},{8,4},{9,5},{1... | collective-permute-start | bytes 196616 | tf_op jit(solution)/shard_map/ppermute | solution.py:76
  250.1 2.5 collective-permute-start.40
  256.5 2.4 collective-permute-start.52
  261.8 2.7 %collective-permute-done.53 = bf16[64,512]{1,0:T(8,128)(2,1)S(1)} collective-permute-done((bf16[64,512]{1,0:T(8,128)(2,1)S(1)}, bf16[64,512]{1,0:T(8,128)(2,1)S(1)}, u32[]{:S(2)}, u32[]{:S(2)}) %collective-permute-start.53) | collective-permute-done | bytes 65568 | tf_op jit(solution)/shard_map/ppermute | solution.py:76
  264.5 2.6 collective-permute-done.54
  (263 shorter events, 115.0 us)
Async XLA Ops:
  2.4 50.5 %collective-permute-start.10 = (bf16[64,512]{1,0:T(8,128)(2,1)}, bf16[64,512]{1,0:T(8,128)(2,1)}, u32[]{:S(2)}, u32[]{:S(2)}) collective-permute-start(bf16[64,512]{1,0:T(8,128)(2,1)} %get-tuple-element.23), channel_id=1, source_target_pairs={{0,8},{1,9},{2,10},{3,11},{4,12},{5,13},{6,14},{7,15},{8,0},{9,1},... | collective-permute-start | bytes 196616 | tf_op jit(solution)/shard_map/ppermute | solution.py:76
  6.4 47.4 %collective-permute-start.11 = (bf16[64,512]{1,0:T(8,128)(2,1)}, bf16[64,512]{1,0:T(8,128)(2,1)}, u32[]{:S(2)}, u32[]{:S(2)}) collective-permute-start(bf16[64,512]{1,0:T(8,128)(2,1)} %get-tuple-element.23), channel_id=1, source_target_pairs={{0,12},{1,13},{2,14},{3,15},{4,0},{5,1},{6,2},{7,3},{8,4},{9,5},{1... | collective-permute-start | bytes 196616 | tf_op jit(solution)/shard_map/ppermute | solution.py:76
  7.8 42.5 %collective-permute-start.9 = (bf16[64,512]{1,0:T(8,128)(2,1)}, bf16[64,512]{1,0:T(8,128)(2,1)}, u32[]{:S(2)}, u32[]{:S(2)}) collective-permute-start(bf16[64,512]{1,0:T(8,128)(2,1)} %get-tuple-element.23), channel_id=1, source_target_pairs={{0,4},{1,5},{2,6},{3,7},{4,8},{5,9},{6,10},{7,11},{8,12},{9,13},{1... | collective-permute-start | bytes 196616 | tf_op jit(solution)/shard_map/ppermute | solution.py:76
  8.4 52.2 %collective-permute-start.20 = (bf16[64,512]{1,0:T(8,128)(2,1)}, bf16[64,512]{1,0:T(8,128)(2,1)}, u32[]{:S(2)}, u32[]{:S(2)}) collective-permute-start(bf16[64,512]{1,0:T(8,128)(2,1)} %get-tuple-element.71), channel_id=1, source_target_pairs={{0,4},{1,5},{2,6},{3,7},{4,8},{5,9},{6,10},{7,11},{8,12},{9,13},{1... | collective-permute-start | bytes 196616 | tf_op jit(solution)/shard_map/ppermute | solution.py:76
  10.0 37.6 %collective-permute-start.1 = (s32[512]{0:T(512)}, s32[512]{0:T(512)}, u32[]{:S(2)}, u32[]{:S(2)}) collective-permute-start(s32[512]{0:T(512)} %param.12), channel_id=1, source_target_pairs={{0,16},{1,17},{2,18},{3,19},{4,20},{5,21},{6,22},{7,23},{8,24},{9,... | collective-permute-start | bytes 6152 | tf_op jit(solution)/shard_map/ppermute | solution.py:21
  47.7 15.3 %collective-permute-start.21 = (bf16[64,512]{1,0:T(8,128)(2,1)}, bf16[64,512]{1,0:T(8,128)(2,1)S(1)}, u32[]{:S(2)}, u32[]{:S(2)}) collective-permute-start(bf16[64,512]{1,0:T(8,128)(2,1)} %get-tuple-element.71), channel_id=1, source_target_pairs={{0,8},{1,9},{2,10},{3,11},{4,12},{5,13},{6,14},{7,15},{8,0},{9,1},... | collective-permute-start | bytes 196616 | tf_op jit(solution)/shard_map/ppermute | solution.py:76
  53.9 15.3 %collective-permute-start.4 = (bf16[64,512]{1,0:T(8,128)(2,1)}, bf16[64,512]{1,0:T(8,128)(2,1)S(1)}, u32[]{:S(2)}, u32[]{:S(2)}) collective-permute-start(bf16[64,512]{1,0:T(8,128)(2,1)} %get-tuple-element.69), channel_id=1, source_target_pairs={{0,8},{1,9},{2,10},{3,11},{4,12},{5,13},{6,14},{7,15},{8,0},{9,1},... | collective-permute-start | bytes 196616 | tf_op jit(solution)/shard_map/ppermute | solution.py:76
  64.1 15.3 %collective-permute-start.16 = (bf16[64,1024]{1,0:T(8,128)(2,1)}, bf16[64,1024]{1,0:T(8,128)(2,1)S(1)}, u32[]{:S(2)}, u32[]{:S(2)}) collective-permute-start(bf16[64,1024]{1,0:T(8,128)(2,1)} %get-tuple-element.67), channel_id=1, source_target_pairs={{0,8},{1,9},{2,10},{3,11},{4,12},{5,13},{6,14},{7,15},{8,0},{9,1},... | collective-permute-start | bytes 393224 | tf_op jit(solution)/shard_map/ppermute | solution.py:76
  66.3 15.0 %collective-permute-start.17 = (bf16[64,1024]{1,0:T(8,128)(2,1)}, bf16[64,1024]{1,0:T(8,128)(2,1)S(1)}, u32[]{:S(2)}, u32[]{:S(2)}) collective-permute-start(bf16[64,1024]{1,0:T(8,128)(2,1)} %get-tuple-element.67), channel_id=1, source_target_pairs={{0,12},{1,13},{2,14},{3,15},{4,0},{5,1},{6,2},{7,3},{8,4},{9,5},{1... | collective-permute-start | bytes 393224 | tf_op jit(solution)/shard_map/ppermute | solution.py:76
  69.2 15.7 %collective-permute-start.26 = (bf16[64,1024]{1,0:T(8,128)(2,1)S(1)}, bf16[64,1024]{1,0:T(8,128)(2,1)S(1)}, u32[]{:S(2)}, u32[]{:S(2)}) collective-permute-start(bf16[64,1024]{1,0:T(8,128)(2,1)S(1)} %get-tuple-element.64), channel_id=1, source_target_pairs={{0,4},{1,5},{2,6},{3,7},{4,8},{5,9},{6,10},{7,11},{8,12},{9,13},{1... | collective-permute-start | bytes 393224 | tf_op jit(solution)/shard_map/ppermute | solution.py:76
  69.6 17.0 %collective-permute-start.27 = (bf16[64,1024]{1,0:T(8,128)(2,1)S(1)}, bf16[64,1024]{1,0:T(8,128)(2,1)S(1)}, u32[]{:S(2)}, u32[]{:S(2)}) collective-permute-start(bf16[64,1024]{1,0:T(8,128)(2,1)S(1)} %get-tuple-element.64), channel_id=1, source_target_pairs={{0,8},{1,9},{2,10},{3,11},{4,12},{5,13},{6,14},{7,15},{8,0},{9,1},... | collective-permute-start | bytes 393224 | tf_op jit(solution)/shard_map/ppermute | solution.py:76
  79.4 26.0 %collective-permute-start.2 = (bf16[512,512]{0,1:T(8,128)(2,1)S(1)}, bf16[512,512]{0,1:T(8,128)(2,1)S(1)}, u32[]{:S(2)}, u32[]{:S(2)}) collective-permute-start(bf16[512,512]{0,1:T(8,128)(2,1)S(1)} %copy.30), channel_id=1, source_target_pairs={{0,16},{1,17},{2,18},{3,19},{4,20},{5,21},{6,22},{7,23},{8,24},{9,... | collective-permute-start | bytes 1572872 | tf_op jit(solution)/shard_map/ppermute | solution.py:19
  81.4 33.5 %collective-permute-start = (bf16[512,512]{1,0:T(8,128)(2,1)S(1)}, bf16[512,512]{1,0:T(8,128)(2,1)}, u32[]{:S(2)}, u32[]{:S(2)}) collective-permute-start(bf16[512,512]{1,0:T(8,128)(2,1)S(1)} %copy-done.12), channel_id=1, source_target_pairs={{0,16},{1,17},{2,18},{3,19},{4,20},{5,21},{6,22},{7,23},{8,24},{9,... | collective-permute-start | bytes 1572872 | tf_op jit(solution)/shard_map/ppermute | solution.py:20
  87.0 18.4 %collective-permute-start.6 = (bf16[256,512]{1,0:T(8,128)(2,1)S(1)}, bf16[256,512]{1,0:T(8,128)(2,1)S(1)}, u32[]{:S(2)}, u32[]{:S(2)}) collective-permute-start(bf16[256,512]{1,0:T(8,128)(2,1)S(1)} %pad_maximum_fusion.21), channel_id=1, source_target_pairs={{0,2},{1,3},{2,0},{3,1},{4,6},{5,7},{6,4},{7,5},{8,10},{9,11},{10,... | collective-permute-start | bytes 786440 | tf_op jit(solution)/shard_map/ppermute | solution.py:79
  94.1 26.6 %collective-permute-start.18 = (bf16[256,1024]{1,0:T(8,128)(2,1)}, bf16[256,1024]{1,0:T(8,128)(2,1)}, u32[]{:S(2)}, u32[]{:S(2)}) collective-permute-start(bf16[256,1024]{1,0:T(8,128)(2,1)} %pad_maximum_fusion.19), channel_id=1, source_target_pairs={{0,2},{1,3},{2,0},{3,1},{4,6},{5,7},{6,4},{7,5},{8,10},{9,11},{10,... | collective-permute-start | bytes 1572872 | tf_op jit(solution)/shard_map/ppermute | solution.py:79
  99.7 25.2 %collective-permute-start.29 = (bf16[256,1024]{1,0:T(8,128)(2,1)}, bf16[256,1024]{1,0:T(8,128)(2,1)}, u32[]{:S(2)}, u32[]{:S(2)}) collective-permute-start(bf16[256,1024]{1,0:T(8,128)(2,1)} %pad_maximum_fusion.20), channel_id=1, source_target_pairs={{0,2},{1,3},{2,0},{3,1},{4,6},{5,7},{6,4},{7,5},{8,10},{9,11},{10,... | collective-permute-start | bytes 1572872 | tf_op jit(solution)/shard_map/ppermute | solution.py:79
  105.4 21.9 %collective-permute-start.13 = (bf16[512,512]{1,0:T(8,128)(2,1)}, bf16[512,512]{1,0:T(8,128)(2,1)}, u32[]{:S(2)}, u32[]{:S(2)}) collective-permute-start(bf16[512,512]{1,0:T(8,128)(2,1)} %constant_dynamic-update-slice_fusion.7), channel_id=1, source_target_pairs={{0,16},{16,0},{1,17},{17,1},{2,18},{18,2},{3,19},{19,3},{4,20},{20... | collective-permute-start | bytes 1572872 | tf_op jit(solution)/shard_map/ppermute | solution.py:85
  105.4 25.1 %collective-permute-start.24 = (bf16[512,512]{1,0:T(8,128)(2,1)}, bf16[512,512]{1,0:T(8,128)(2,1)}, u32[]{:S(2)}, u32[]{:S(2)}) collective-permute-start(bf16[512,512]{1,0:T(8,128)(2,1)} %constant_dynamic-update-slice_fusion.17), channel_id=1, source_target_pairs={{0,16},{16,0},{1,17},{17,1},{2,18},{18,2},{3,19},{19,3},{4,20},{20... | collective-permute-start | bytes 1572872 | tf_op jit(solution)/shard_map/ppermute | solution.py:85
  114.9 21.2 %collective-permute-start.7 = (bf16[512,512]{1,0:T(8,128)(2,1)S(1)}, bf16[512,512]{1,0:T(8,128)(2,1)}, u32[]{:S(2)}, u32[]{:S(2)}) collective-permute-start(bf16[512,512]{1,0:T(8,128)(2,1)S(1)} %constant_dynamic-update-slice_fusion.2), channel_id=1, source_target_pairs={{0,16},{16,0},{1,17},{17,1},{2,18},{18,2},{3,19},{19,3},{4,20},{20... | collective-permute-start | bytes 1572872 | tf_op jit(solution)/shard_map/ppermute | solution.py:85
  126.8 17.4 %collective-permute-start.30 = (bf16[256,1024]{1,0:T(8,128)(2,1)S(1)}, bf16[256,1024]{1,0:T(8,128)(2,1)S(1)}, u32[]{:S(2)}, u32[]{:S(2)}) collective-permute-start(bf16[256,1024]{1,0:T(8,128)(2,1)S(1)} %get-tuple-element.49), channel_id=1, source_target_pairs={{0,1},{1,0},{2,3},{3,2},{4,5},{5,4},{6,7},{7,6},{8,9},{9,8},{10,11... | collective-permute-start | bytes 1572872 | tf_op jit(solution)/shard_map/ppermute | solution.py:82
  138.9 17.4 %collective-permute-start.25 = (bf16[256,1024]{1,0:T(8,128)(2,1)S(1)}, bf16[256,1024]{1,0:T(8,128)(2,1)S(1)}, u32[]{:S(2)}, u32[]{:S(2)}) collective-permute-start(bf16[256,1024]{1,0:T(8,128)(2,1)S(1)} %get-tuple-element.61), channel_id=1, source_target_pairs={{0,1},{1,0},{2,3},{3,2},{4,5},{5,4},{6,7},{7,6},{8,9},{9,8},{10,11... | collective-permute-start | bytes 1572872 | tf_op jit(solution)/shard_map/ppermute | solution.py:82
  187.7 23.0 %collective-permute-start.44 = (bf16[256,1024]{1,0:T(8,128)(2,1)S(1)}, bf16[256,1024]{1,0:T(8,128)(2,1)S(1)}, u32[]{:S(2)}, u32[]{:S(2)}) collective-permute-start(bf16[256,1024]{1,0:T(8,128)(2,1)S(1)} %slice.599), channel_id=1, source_target_pairs={{0,2},{1,3},{2,0},{3,1},{4,6},{5,7},{6,4},{7,5},{8,10},{9,11},{10,... | collective-permute-start | bytes 1572872 | tf_op jit(solution)/shard_map/ppermute | solution.py:79
  190.2 25.9 %collective-permute-start.38 = (bf16[512,512]{1,0:T(8,128)(2,1)S(1)}, bf16[512,512]{1,0:T(8,128)(2,1)S(1)}, u32[]{:S(2)}, u32[]{:S(2)}) collective-permute-start(bf16[512,512]{1,0:T(8,128)(2,1)S(1)} %fusion.93), channel_id=1, source_target_pairs={{0,16},{16,0},{1,17},{17,1},{2,18},{18,2},{3,19},{19,3},{4,20},{20... | collective-permute-start | bytes 1572872 | tf_op jit(solution)/shard_map/ppermute | solution.py:85
  192.8 30.2 %collective-permute-start.32 = (bf16[512,512]{1,0:T(8,128)(2,1)S(1)}, bf16[512,512]{1,0:T(8,128)(2,1)S(1)}, u32[]{:S(2)}, u32[]{:S(2)}) collective-permute-start(bf16[512,512]{1,0:T(8,128)(2,1)S(1)} %fusion.92), channel_id=1, source_target_pairs={{0,16},{16,0},{1,17},{17,1},{2,18},{18,2},{3,19},{19,3},{4,20},{20... | collective-permute-start | bytes 1572872 | tf_op jit(solution)/shard_map/ppermute | solution.py:85
  200.1 23.9 %collective-permute-start.57 = (bf16[64,1024]{1,0:T(8,128)(2,1)S(1)}, bf16[64,1024]{1,0:T(8,128)(2,1)S(1)}, u32[]{:S(2)}, u32[]{:S(2)}) collective-permute-start(bf16[64,1024]{1,0:T(8,128)(2,1)S(1)} %get-tuple-element.72), channel_id=1, source_target_pairs={{0,12},{1,13},{2,14},{3,15},{4,0},{5,1},{6,2},{7,3},{8,4},{9,5},{1... | collective-permute-start | bytes 393224 | tf_op jit(solution)/shard_map/ppermute | solution.py:76
  201.3 28.9 %collective-permute-start.58 = (bf16[64,1024]{1,0:T(8,128)(2,1)S(1)}, bf16[64,1024]{1,0:T(8,128)(2,1)S(1)}, u32[]{:S(2)}, u32[]{:S(2)}) collective-permute-start(bf16[64,1024]{1,0:T(8,128)(2,1)S(1)} %get-tuple-element.74), channel_id=1, source_target_pairs={{0,8},{1,9},{2,10},{3,11},{4,12},{5,13},{6,14},{7,15},{8,0},{9,1},... | collective-permute-start | bytes 393224 | tf_op jit(solution)/shard_map/ppermute | solution.py:76
  210.7 19.5 %collective-permute-start.59 = (bf16[64,1024]{1,0:T(8,128)(2,1)S(1)}, bf16[64,1024]{1,0:T(8,128)(2,1)S(1)}, u32[]{:S(2)}, u32[]{:S(2)}) collective-permute-start(bf16[64,1024]{1,0:T(8,128)(2,1)S(1)} %get-tuple-element.73), channel_id=1, source_target_pairs={{0,4},{1,5},{2,6},{3,7},{4,8},{5,9},{6,10},{7,11},{8,12},{9,13},{1... | collective-permute-start | bytes 393224 | tf_op jit(solution)/shard_map/ppermute | solution.py:76
  216.1 30.4 %collective-permute-start.51 = (bf16[256,512]{1,0:T(8,128)(2,1)S(1)}, bf16[256,512]{1,0:T(8,128)(2,1)S(1)}, u32[]{:S(2)}, u32[]{:S(2)}) collective-permute-start(bf16[256,512]{1,0:T(8,128)(2,1)S(1)} %slice.600), channel_id=1, source_target_pairs={{0,2},{1,3},{2,0},{3,1},{4,6},{5,7},{6,4},{7,5},{8,10},{9,11},{10,... | collective-permute-start | bytes 786440 | tf_op jit(solution)/shard_map/ppermute | solution.py:79
  224.1 16.8 %collective-permute-start.46 = (bf16[64,1024]{1,0:T(8,128)(2,1)S(1)}, bf16[64,1024]{1,0:T(8,128)(2,1)S(1)}, u32[]{:S(2)}, u32[]{:S(2)}) collective-permute-start(bf16[64,1024]{1,0:T(8,128)(2,1)S(1)} %get-tuple-element.77), channel_id=1, source_target_pairs={{0,8},{1,9},{2,10},{3,11},{4,12},{5,13},{6,14},{7,15},{8,0},{9,1},... | collective-permute-start | bytes 393224 | tf_op jit(solution)/shard_map/ppermute | solution.py:76
  230.2 18.0 %collective-permute-start.39 = (bf16[256,512]{1,0:T(8,128)(2,1)S(1)}, bf16[256,512]{1,0:T(8,128)(2,1)S(1)}, u32[]{:S(2)}, u32[]{:S(2)}) collective-permute-start(bf16[256,512]{1,0:T(8,128)(2,1)S(1)} %slice.601), channel_id=1, source_target_pairs={{0,2},{1,3},{2,0},{3,1},{4,6},{5,7},{6,4},{7,5},{8,10},{9,11},{10,... | collective-permute-start | bytes 786440 | tf_op jit(solution)/shard_map/ppermute | solution.py:79
  240.9 26.3 %collective-permute-start.60 = (bf16[64,512]{1,0:T(8,128)(2,1)S(1)}, bf16[64,512]{1,0:T(8,128)(2,1)S(1)}, u32[]{:S(2)}, u32[]{:S(2)}) collective-permute-start(bf16[64,512]{1,0:T(8,128)(2,1)S(1)} %fusion.114), channel_id=1, source_target_pairs={{0,16},{16,0},{1,17},{17,1},{2,18},{18,2},{3,19},{19,3},{4,20},{20... | collective-permute-start | bytes 196616 | tf_op jit(solution)/shard_map/ppermute | solution.py:85
  241.3 20.5 %collective-permute-start.48 = (bf16[64,512]{1,0:T(8,128)(2,1)S(1)}, bf16[64,512]{1,0:T(8,128)(2,1)S(1)}, u32[]{:S(2)}, u32[]{:S(2)}) collective-permute-start(bf16[64,512]{1,0:T(8,128)(2,1)S(1)} %fusion.113), channel_id=1, source_target_pairs={{0,16},{16,0},{1,17},{17,1},{2,18},{18,2},{3,19},{19,3},{4,20},{20... | collective-permute-start | bytes 196616 | tf_op jit(solution)/shard_map/ppermute | solution.py:85
  (48 other events, 512.4 us)

commit v2 on v1

--- a/solution.py
+++ b/solution.py
@@ -1,6 +1,8 @@
 import jax
 import jax.numpy as jnp
 from jax import lax
+from jax.experimental import pallas as pl
+from jax.experimental.pallas import tpu as pltpu
 from jax.sharding import PartitionSpec as P
 
 HD = 128
@@ -51,6 +53,230 @@
     )
     return (summed / total[:, :, None]).reshape(rows, heads * HD).astype(BF16)
 
+SHARED = 2048
+OVER_X = 1536
+Z_ORDER = [1, 3, 2]
+GROUPS = [[0, 1, 3, 2]]
+BACK = [2, 1, 3, 0]
+
+VMEM = pl.BlockSpec(memory_space=pltpu.VMEM)
+ROOM = 48 * 1024 * 1024
+LANES = 128
+
+
+def call(body, out_shape, flops, moved, **kw):
+    return pl.pallas_call(
+        body,
+        out_shape=out_shape,
+        compiler_params=pltpu.CompilerParams(vmem_limit_bytes=ROOM),
+        cost_estimate=pl.CostEstimate(flops=flops, bytes_accessed=moved, transcendentals=0),
+        **kw,
+    )
+
+
+def pick(blocks, me, cap, experts):
+    count = len(blocks)
+    rows, width = blocks[0].shape
+
+    def body(me_ref, *refs):
+        ins, (near, other, placing) = refs[:count], refs[count:]
+        mine = me_ref[0]
+        lane = lax.broadcasted_iota(jnp.int32, (rows, LANES), 1)
+        earlier = lax.broadcasted_iota(jnp.int32, (rows, rows), 0) > lax.broadcasted_iota(
+            jnp.int32, (rows, rows), 1
+        )
+        slot = lax.broadcasted_iota(jnp.int32, (rows, cap), 1).astype(F32)
+        for i, ref in enumerate(ins):
+            member = ref[:, width - LANES :]
+            rank = jnp.dot(earlier.astype(BF16), member, preferred_element_type=F32)
+            member = member.astype(F32)
+            for j, out in enumerate((near, other)):
+                at = lane == (mine if j == 0 else mine + 1 - 2 * (mine % 2))
+                hit = jnp.sum(jnp.where(at, member, 0.0), axis=1, keepdims=True)
+                place = jnp.sum(jnp.where(at, rank, 0.0), axis=1, keepdims=True)
+                onehot = jnp.where((place == slot) & (hit > 0.5), 1.0, 0.0).astype(BF16)
+                placing[i, :, j * cap : (j + 1) * cap] = onehot
+                out[i * cap : (i + 1) * cap, :] = lax.dot_general(
+                    onehot, ref[...], (((0,), (0,)), ((), ())), preferred_element_type=F32
+                ).astype(BF16)
+
+    slots = jax.ShapeDtypeStruct((count * cap, width), BF16)
+    return call(
+        body,
+        (slots, slots, jax.ShapeDtypeStruct((count, rows, 2 * cap), BF16)),
+        4 * count * cap * rows * width,
+        2 * count * (rows + 2 * cap) * width,
+        in_specs=[pl.BlockSpec(memory_space=pltpu.SMEM)] + [VMEM] * count,
+        out_specs=(VMEM,) * 3,
+    )(me.reshape(1), *blocks)
+
+
+def pick_more(arrays, placing, cap):
+    total, rows, _ = placing.shape
+    width = arrays[0].shape[1]
+
+    def body(placing, *refs):
+        ins, (near, other) = refs[:-2], refs[-2:]
+        i = 0
+        for ref in ins:
+            for b in range(ref.shape[0] // rows):
+                for j, out in enumerate((near, other)):
+                    out[i * cap : (i + 1) * cap, :] = lax.dot_general(
+                        placing[i, :, j * cap : (j + 1) * cap],
+                        ref[b * rows : (b + 1) * rows, :],
+                        (((0,), (0,)), ((), ())),
+                        preferred_element_type=F32,
+                    ).astype(BF16)
+                i += 1
+
+    slots = jax.ShapeDtypeStruct((total * cap, width), BF16)
+    return call(
+        body,
+        (slots, slots),
+        4 * total * cap * rows * width,
+        2 * total * (rows + 2 * cap) * width,
+        in_specs=[VMEM] * (1 + len(arrays)),
+        out_specs=(VMEM,) * 2,
+    )(placing, *arrays)
+
+
+def widen(near, near_x, far, far_x, w_in, me, at_x, shared, split, experts, tile=512):
+    slots = near.shape[0]
+    width = near.shape[1]
+    units = w_in.shape[3]
+    main, more = (shared + split) // tile, split // tile
+    steps = main + more
+
+    def place(k, s):
+        first, own, other = shared // tile, s[1] * more, (1 - s[1]) * more
+        return jnp.where(
+            k < first, k, jnp.where(k < main, own + k, other + k - more)
+        )
+
+    def body(s, near, near_x, far, far_x, w, hidden, weight, gate, up):
+        k = pl.program_id(0)
+
+        @pl.when(k == 0)
+        def _():
+            gate[...] = jnp.zeros_like(gate)
+            up[...] = jnp.zeros_like(up)
+            lane = lax.broadcasted_iota(jnp.int32, (slots, LANES), 1)
+            at = (lane % experts == s[0]) & (lane >= experts) & (lane < 4 * experts)
+            for i, ref in enumerate((near, far)):
+                meta = ref[:, width - LANES :].astype(F32)
+                weight[i * slots : (i + 1) * slots, :] = jnp.sum(
+                    jnp.where(at, meta, 0.0), axis=1, keepdims=True
+                )
+
+        def add(a, b, column):
+            columns = pl.ds(pl.multiple_of(column, tile), tile)
+            block = jnp.concatenate([a[:, columns], b[:, columns]], axis=0)
+            gate[...] += jnp.dot(block, w[0, 0], preferred_element_type=F32)
+            up[...] += jnp.dot(block, w[0, 1], preferred_element_type=F32)
+
+        @pl.when(k < main)
+        def _():
+            add(near, far, k * tile)
+
+        @pl.when(k >= main)
+        def _():
+            add(near_x, far_x, (k - main) * tile)
+
+        @pl.when(k == steps - 1)
+        def _():
+            hidden[...] = (jax.nn.silu(gate[...]) * up[...]).astype(BF16)
+
+    whole = lambda shape: pl.BlockSpec(shape, lambda k, s: (0,) * len(shape))
+    return call(
+        body,
+        (
+            jax.ShapeDtypeStruct((2 * slots, units), BF16),
+            jax.ShapeDtypeStruct((2 * slots, 1), F32),
+        ),
+        8 * slots * units * steps * tile,
+        4 * units * steps * tile,
+        grid_spec=pltpu.PrefetchScalarGridSpec(
+            num_scalar_prefetch=1,
+            grid=(steps,),
+            in_specs=[whole(a.shape) for a in (near, near_x, far, far_x)]
+            + [pl.BlockSpec((1, 2, tile, units), lambda k, s: (0, 0, place(k, s), 0))],
+            out_specs=(whole((2 * slots, units)), whole((2 * slots, 1))),
+            scratch_shapes=[pltpu.VMEM((2 * slots, units), F32)] * 2,
+        ),
+    )(jnp.stack([me, at_x]), near, near_x, far, far_x, w_in)
+
+
+def narrow(hidden, weight, w_down, at_x, columns, tile):
+    slots, units = hidden.shape
+    slots = slots // 2
+    steps = len(columns[0])
+    table = jnp.where(at_x == 0, jnp.array(columns[0], jnp.int32), jnp.array(columns[1], jnp.int32))
+
+    def body(s, hidden, weight, w, near, far):
+        out = jnp.dot(hidden[...], w[0], preferred_element_type=F32) * weight[...]
+        near[...] = out[:slots].astype(BF16)
+        far[...] = out[slots:].astype(BF16)
+
+    out = jax.ShapeDtypeStruct((slots, steps * tile), BF16)
+    return call(
+        body,
+        (out, out),
+        4 * slots * units * steps * tile,
+        2 * units * steps * tile + 4 * slots * steps * tile,
+        grid_spec=pltpu.PrefetchScalarGridSpec(
+            num_scalar_prefetch=1,
+            grid=(steps,),
+            in_specs=[
+                pl.BlockSpec(hidden.shape, lambda n, s: (0, 0)),
+                pl.BlockSpec(weight.shape, lambda n, s: (0, 0)),
+                pl.BlockSpec((1, units, tile), lambda n, s: (0, 0, s[n])),
+            ],
+            out_specs=(pl.BlockSpec((slots, tile), lambda n, s: (0, n)),) * 2,
+        ),
+    )(table, hidden, weight, w_down)
+
+
+def mix(placing, near, far, first, count, adds=(), dtype=BF16):
+    _, rows, both = placing.shape
+    cap = both // 2
+    width = near.shape[1]
+
+    def body(placing, near, far, *refs):
+        slots = jnp.concatenate([near[...], far[...]], axis=0)
+        total = jnp.dot(placing[0], slots, preferred_element_type=F32)
+        narrow = [r for r in refs[:-1] if r.shape[1] < width]
+        full = [r for r in refs[:-1] if r.shape[1] == width]
+        out = refs[-1]
+        for ref in full:
+            total = total + ref[...].astype(F32)
+        if narrow:
+            edge = narrow[0].shape[1]
+            left = total[:, :edge]
+            for ref in narrow:
+                left = left + ref[...].astype(F32)
+            out[:, :edge] = left.astype(dtype)
+            out[:, edge:] = total[:, edge:].astype(dtype)
+        else:
+            out[...] = total.astype(dtype)
+
+    def at(base):
+        return lambda g: (g + base, 0)
+
+    return call(
+        body,
+        jax.ShapeDtypeStruct((count * rows, width), dtype),
+        4 * count * rows * cap * width,
+        2 * count * (rows + 2 * cap) * width,
+        grid=(count,),
+        in_specs=[
+            pl.BlockSpec((1, rows, both), lambda g: (g + first, 0, 0)),
+            pl.BlockSpec((cap, width), at(first)),
+            pl.BlockSpec((cap, width), at(first)),
+        ]
+        + [pl.BlockSpec((rows, a.shape[1]), at(base)) for a, base in adds],
+        out_specs=pl.BlockSpec((rows, width), at(0)),
+    )(placing, near, far, *[a for a, _ in adds])
+
 
 def spread(onehot):
     blocks, cap, rows = onehot.shape
@@ -203,6 +429,85 @@
         attn_out = attend(q_input, k_input, v_input, segment_ids, n_ctx)
         return attn_out, moe_out
 
+    def pair_device(
+        q_input, k_input, v_input, segment_ids, tokens, expert_ids, route_weight, w_in, w_down
+    ):
+        me = lax.axis_index("exp")
+        at_x = lax.axis_index("ctx")
+        rows, width = tokens.shape
+        cap = rows * 8 // n_exp
+        half = width // 2
+
+        named = expert_ids[:, :, None] == jnp.arange(n_exp, dtype=jnp.int32)
+        member = jnp.any(named, axis=1).astype(F32)
+        weight = jnp.sum(jnp.where(named, route_weight[:, :, None], 0.0), axis=1)
+        high = lax.reduce_precision(weight, 8, 7)
+        middle = lax.reduce_precision(weight - high, 8, 7)
+        low = weight - high - middle
+        meta = jnp.concatenate([member, high, middle, low], axis=1).astype(BF16)
+        meta = jnp.pad(meta, ((0, 0), (0, LANES - meta.shape[1])))
+
+        split = (width - SHARED) // 2
+        mine = lax.dynamic_slice_in_dim(tokens, SHARED + at_x * split, split, 1)
+        theirs = lax.dynamic_slice_in_dim(tokens, SHARED + (1 - at_x) * split, split, 1)
+        block = jnp.concatenate([tokens[:, :SHARED], mine, meta], axis=1)
+        line = {0: block}
+        for d in Z_ORDER:
+            line[d] = z_shift(block, d)
+        across = {d: y_swap(line[d]) for d in [0] + Z_ORDER}
+        cut = lambda a: a[:, SHARED : SHARED + split]
+        more = {0: [theirs, x_swap(cut(across[0]))]}
+        for d in Z_ORDER:
+            more[d] = [x_swap(jnp.concatenate([cut(line[d]), cut(across[d])], axis=0))]
+
+        tile = 512
+        per = half // tile
+        first = OVER_X // tile
+        lists = []
+        for x in range(2):
+            own, other = x * per, (1 - x) * per
+            late = [other + n for n in range(first)]
+            main = [own + n for n in range(per)] + [other + n for n in range(first, per)]
+            lists.append((late, main))
+
+        done = {}
+        for group in GROUPS:
+            near, out, placing = pick(
+                [b for d in group for b in (line[d], across[d])], me, cap, n_exp
+            )
+            near_x, out_x = pick_more([a for d in group for a in more[d]], placing, cap)
+            far, far_x = core_swap(out), core_swap(out_x)
+            hidden, scale = widen(
+                near, near_x, far, far_x, w_in, me, at_x, SHARED, split, n_exp
+            )
+            near_l, out_l = narrow(hidden, scale, w_down, at_x, [l[0] for l in lists], tile)
+            far_l = core_swap(out_l)
+            near_m, out_m = narrow(hidden, scale, w_down, at_x, [l[1] for l in lists], tile)
+            far_m = core_swap(out_m)
+            for i, d in sorted(enumerate(group), key=lambda p: BACK.index(p[1])):
+                b = 2 * i
+                got_x = x_swap(mix(placing, near_l, far_l, b, 2))
+                got_y = y_swap(mix(placing, near_m, far_m, b + 1, 1, [(got_x, 1)]))
+                sums = mix(
+                    placing,
+                    near_m,
+                    far_m,
+                    b,
+                    1,
+                    [(got_x, 0), (got_y, 0)],
+                    F32 if d == 0 else BF16,
+                )
+                done[d] = sums if d == 0 else z_shift(sums, -d)
+        total = done[0]
+        for d in Z_ORDER:
+            total = total + done[d].astype(F32)
+        got = x_swap(total[:, half:].astype(BF16))
+        moe_out = jnp.concatenate(
+            [total[:, :OVER_X], total[:, OVER_X:half] + got.astype(F32)], axis=1
+        ).astype(BF16)
+        attn_out = attend(q_input, k_input, v_input, segment_ids, n_ctx)
+        return attn_out, moe_out
+
     in_specs = (
         P("ctx", "exp"),
         P("ctx", "exp"),
@@ -216,5 +521,9 @@
     )
     out_specs = (P("ctx", "exp"), P("exp", "ctx"))
     return jax.shard_map(
-        on_device, mesh=mesh, in_specs=in_specs, out_specs=out_specs, check_vma=False
+        pair_device if n_ctx == 2 else on_device,
+        mesh=mesh,
+        in_specs=in_specs,
+        out_specs=out_specs,
+        check_vma=False,
     )

time: 272 us -> 260 us (0.956)
  waiting for transfers between devices: 60.8 us -> 120 us
  Pallas kernels: 0 us -> 53.2 us
  matrix products: 52 us -> 5.3 us
  starting transfers between devices: 75.5 us -> 45.8 us
  local copies, waits for them, and re-layouts: 35.1 us -> 13.9 us
  blocking collectives: 20.6 us -> 0 us
  other arithmetic: 22.2 us -> 19.4 us
    pallas_call x0 -> x17, Pallas kernels: none -> 53.2 us  [the longest x12 16.7 us: mix(): call(body, jax.ShapeDtypeStruct((count * rows, width), dtype), 4 * count...]
    dot_general x25 -> x0, matrix products: 47.8 us -> none  [the longest x5 22.3 us: on_device(): jnp.dot(block, w_in[0, 1, start:start + size], preferred_element_type=F32)]
    ppermute x30 -> x6, starting transfers between devices: 52.4 us -> 11.2 us  [z_shift(): return lax.ppermute(x, 'exp', pairs(lambda z, y, c: (z + d, y, c)))]
    ppermute x8 -> x9, waiting for transfers between devices: 12.8 us -> 50 us  [x_swap(): return lax.ppermute(x, 'ctx', [(0, 1), (1, 0)])]
    ppermute x30 -> x6, waiting for transfers between devices: 25.1 us -> 51.8 us  [z_shift(): return lax.ppermute(x, 'exp', pairs(lambda z, y, c: (z + d, y, c)))]
    all_gather x1 -> x0, blocking collectives: 20.6 us -> none  [on_device(): meta = lax.all_gather(meta, 'exp', axis=0, tiled=False)]
    unnamed x57 -> x32, local copies, waits for them, and re-layouts: 19.5 us -> 6.43 us
    ppermute x10 -> x8, waiting for transfers between devices: 22.8 us -> 11.2 us  [y_swap(): return lax.ppermute(x, 'exp', pairs(lambda z, y, c: (z, 1 - y, c)))]
  transfers between devices with their start and end apart: 61 -> 30, of which waited for: 21 -> 13; matrix products, arithmetic and copies ran while one was open for 31% -> 11% of each run, Pallas kernels for 0% -> 9%
where the time goes in v2:
time: 260 us; the launch traced here: 259 us
  waiting for transfers between devices  120 us (46%)
  Pallas kernels  53.2 us (20%)
  starting transfers between devices  45.8 us (18%)
  other arithmetic  19.4 us (7%)
  local copies, waits for them, and re-layouts  13.9 us (5%)
  matrix products  5.3 us (2%)
    ppermute x6, waiting for transfers between devices, z_shift(): return lax.ppermute(x, 'exp', pairs(lambda z, y, c: (z + d, y, c)))  51.8 us
    ppermute x9, waiting for transfers between devices, x_swap(): return lax.ppermute(x, 'ctx', [(0, 1), (1, 0)])  50 us
    pallas_call x12, Pallas kernels, mix(): call(body, jax.ShapeDtypeStruct((count * rows, width), dtype), 4 * count...  16.7 us
    pallas_call x1, Pallas kernels, widen(): call(body, (jax.ShapeDtypeStruct((2 * slots, units), BF16), jax.ShapeDtyp...  15.2 us
    pallas_call x2, Pallas kernels, narrow(): call(body, (out, out), 4 * slots * units * steps * tile, 2 * units * step...  13.4 us
    ppermute x8, starting transfers between devices, y_swap(): return lax.ppermute(x, 'exp', pairs(lambda z, y, c: (z, 1 - y, c)))  12.7 us
    sub x1, other arithmetic, attend(): scores - newest[:, :, None]  12.2 us
    ppermute x9, starting transfers between devices, x_swap(): return lax.ppermute(x, 'ctx', [(0, 1), (1, 0)])  11.6 us
  transfers between devices with their start and end apart: 30, of which 13 were waited for; matrix products, arithmetic and copies ran while one was open for 11% of the time, Pallas kernels for 9%

profile of v2, /device:TPU:0, one launch (start us, length us, event | category | flops | bytes accessed | tf_op | source)
XLA Modules:
  0.0 258.6 jit_solution(10857337770575989714)
XLA Ops:
  5.3 3.1 %collective-permute-start.4 = (bf16[64,3712]{1,0:T(8,128)(2,1)S(1)}, bf16[64,3712]{1,0:T(8,128)(2,1)S(1)}, u32[]{:S(2)}, u32[]{:S(2)}) collective-permute-start(bf16[64,3712]{1,0:T(8,128)(2,1)S(1)} %pad_maximum_fusion.2.refs_0_), channel_id=1, source_target_pairs={{0,4},{1,5},{2,6},{3,7},{4,8},{5,9},{6,10},{7,11},{8,12},{9,13},{1... | collective-permute-start | bytes 1425416 | tf_op jit(solution)/shard_map/ppermute | solution.py:302
  8.4 2.1 collective-permute-start.6
  12.9 9.2 %collective-permute-done.4.refs_2_ = bf16[64,3712]{1,0:T(8,128)(2,1)S(1)} collective-permute-done((bf16[64,3712]{1,0:T(8,128)(2,1)S(1)}, bf16[64,3712]{1,0:T(8,128)(2,1)S(1)}, u32[]{:S(2)}, u32[]{:S(2)}) %collective-permute-start.4) | collective-permute-done | bytes 475168 | tf_op jit(solution)/shard_map/ppermute | solution.py:302
  22.1 1.8 collective-permute-start.5
  23.9 7.0 %collective-permute-done.6.refs_4_ = bf16[64,3712]{1,0:T(8,128)(2,1)S(1)} collective-permute-done((bf16[64,3712]{1,0:T(8,128)(2,1)S(1)}, bf16[64,3712]{1,0:T(8,128)(2,1)S(1)}, u32[]{:S(2)}, u32[]{:S(2)}) %collective-permute-start.6) | collective-permute-done | bytes 475168 | tf_op jit(solution)/shard_map/ppermute | solution.py:302
  32.4 19.4 %collective-permute-done.8.refs_6_ = bf16[64,3712]{1,0:T(8,128)(2,1)S(1)} collective-permute-done((bf16[64,3712]{1,0:T(8,128)(2,1)S(1)}, bf16[64,3712]{1,0:T(8,128)(2,1)S(1)}, u32[]{:S(2)}, u32[]{:S(2)}) %collective-permute-start.8) | collective-permute-done | bytes 475168 | tf_op jit(solution)/shard_map/ppermute | solution.py:302
  53.4 11.2 %collective-permute-done.9.refs_7_ = bf16[64,3712]{1,0:T(8,128)(2,1)S(1)} collective-permute-done((bf16[64,3712]{1,0:T(8,128)(2,1)S(1)}, bf16[64,3712]{1,0:T(8,128)(2,1)S(1)}, u32[]{:S(2)}, u32[]{:S(2)}) %collective-permute-start.9) | collective-permute-done | bytes 475168 | tf_op jit(solution)/shard_map/ppermute | solution.py:305
  66.4 6.1 %shard_map.140 = (bf16[256,3712]{1,0:T(8,128)(2,1)S(1)}, bf16[256,3712]{1,0:T(8,128)(2,1)}, bf16[8,64,64]{2,1,0:T(8,128)(2,1)S(1)}) custom-call(s32[1]{0:T(128)} %bitcast.5.me_ref, bf16[64,3712]{1,0:T(8,128)(2,1)S(1)} %pad_maximum_fusion.2.refs_0_, bf16[64,3712]{1,0:T(8,128)(2,1)S(1)} %collective-permute-done.3.refs_1_, ...), custom_call_target="tpu_custom_call" | custom-call | flops 243269632 | bytes 7602176 | tf_op jit(solution)/shard_map/pallas_call | solution.py:104
  79.0 27.1 %collective-permute-done.10.refs_1_ = bf16[64,1536]{1,0:T(8,128)(2,1)S(1)} collective-permute-done((bf16[64,1536]{1,0:T(8,128)(2,1)S(1)}, bf16[64,1536]{1,0:T(8,128)(2,1)S(1)}, u32[]{:S(2)}, u32[]{:S(2)}) %collective-permute-start.10) | collective-permute-done | bytes 196640 | tf_op jit(solution)/shard_map/ppermute | solution.py:311
  106.2 1.8 shard_map.141
  108.0 2.4 collective-permute-done.15.far_x
  112.0 15.2 %shard_map.142 = (bf16[512,768]{1,0:T(8,128)(2,1)S(1)}, f32[512,1]{1,0:T(8,128)S(1)}) custom-call(s32[2]{0:T(128)S(1)} %pad_add_fusion.1.s, bf16[256,3712]{1,0:T(8,128)(2,1)S(1)} %copy-done.6, bf16[256,1536]{1,0:T(8,128)(2,1)S(1)} %get-tuple-element.15.near_x, bf16[256,3712]{1,0:T(8,128)(2,1)} %collective-permute-done.14.far, ...), custom_call_target="tpu_custom_call" | custom-call | flops 8053063680 | bytes 15728640 | tf_op jit(solution)/shard_map/pallas_call | solution.py:190
  127.2 8.5 %shard_map.143 = (bf16[256,3584]{1,0:T(8,128)(2,1)S(1)}, bf16[256,3584]{1,0:T(8,128)(2,1)}) custom-call(s32[7]{0:T(128)S(1)} %broadcast_select_fusion.1.s, bf16[512,768]{1,0:T(8,128)(2,1)S(1)} %get-tuple-element.18.hidden, f32[512,1]{1,0:T(8,128)S(1)} %get-tuple-element.19.weight, bf16[1,768,5120]{2,1,0:T(8,128)(2,1)} %w.5), custom_call_target="tpu_custom_call" | custom-call | flops 2818572288 | bytes 9175040 | tf_op jit(solution)/shard_map/pallas_call | solution.py:221
  135.9 4.8 %shard_map.144 = (bf16[256,1536]{1,0:T(8,128)(2,1)S(1)}, bf16[256,1536]{1,0:T(8,128)(2,1)}) custom-call(s32[3]{0:T(128)S(1)} %broadcast_select_fusion.s, bf16[512,768]{1,0:T(8,128)(2,1)S(1)} %get-tuple-element.18.hidden, f32[512,1]{1,0:T(8,128)S(1)} %get-tuple-element.19.weight, bf16[1,768,5120]{2,1,0:T(8,128)(2,1)} %w.5), custom_call_target="tpu_custom_call" | custom-call | flops 1207959552 | bytes 3932160 | tf_op jit(solution)/shard_map/pallas_call | solution.py:221
  141.1 3.4 %collective-permute-start.1 = (s32[512]{0:T(512)S(1)}, s32[512]{0:T(512)S(1)}, u32[]{:S(2)}, u32[]{:S(2)}) collective-permute-start(s32[512]{0:T(512)S(1)} %copy-done.10), channel_id=1, source_target_pairs={{0,16},{1,17},{2,18},{3,19},{4,20},{5,21},{6,22},{7,23},{8,24},{9,... | collective-permute-start | bytes 6152 | tf_op jit(solution)/shard_map/ppermute | solution.py:23
  144.5 2.0 copy.41
  146.5 2.1 collective-permute-start.2
  151.4 2.1 collective-permute-start.23
  155.8 4.6 %collective-permute-done.2 = bf16[512,512]{0,1:T(8,128)(2,1)} collective-permute-done((bf16[512,512]{0,1:T(8,128)(2,1)}, bf16[512,512]{0,1:T(8,128)(2,1)}, u32[]{:S(2)}, u32[]{:S(2)}) %collective-permute-start.2) | collective-permute-done | bytes 524320 | tf_op jit(solution)/shard_map/ppermute | solution.py:21
  160.4 4.4 %collective-permute-start = (bf16[512,512]{1,0:T(8,128)(2,1)S(1)}, bf16[512,512]{1,0:T(8,128)(2,1)S(1)}, u32[]{:S(2)}, u32[]{:S(2)}) collective-permute-start(bf16[512,512]{1,0:T(8,128)(2,1)S(1)} %copy-done.9), channel_id=1, source_target_pairs={{0,16},{1,17},{2,18},{3,19},{4,20},{5,21},{6,22},{7,23},{8,24},{9,... | collective-permute-start | bytes 1572872 | tf_op jit(solution)/shard_map/ppermute | solution.py:22
  168.7 2.5 collective-permute-start.18
  174.0 3.2 %collective-permute-done.23.refs_0_ = bf16[128,1536]{1,0:T(8,128)(2,1)S(1)} collective-permute-done((bf16[128,1536]{1,0:T(8,128)(2,1)S(1)}, bf16[128,1536]{1,0:T(8,128)(2,1)S(1)}, u32[]{:S(2)}, u32[]{:S(2)}) %collective-permute-start.23) | collective-permute-done | bytes 393248 | tf_op jit(solution)/shard_map/ppermute | solution.py:311
  179.9 5.6 %collective-permute-done.26.refs_0_ = bf16[128,1536]{1,0:T(8,128)(2,1)S(1)} collective-permute-done((bf16[128,1536]{1,0:T(8,128)(2,1)S(1)}, bf16[128,1536]{1,0:T(8,128)(2,1)S(1)}, u32[]{:S(2)}, u32[]{:S(2)}) %collective-permute-start.26) | collective-permute-done | bytes 393248 | tf_op jit(solution)/shard_map/ppermute | solution.py:311
  188.4 4.6 %fusion.16 = f32[4,1024,512]{2,1,0:T(8,128)} fusion(bf16[1024,4,128]{0,2,1:T(8,128)(2,1)S(1)} %bitcast.32, bf16[512,512]{1,0:T(8,128)(2,1)S(1)} %copy-done), kind=kOutput, calls=%fused_computation.16 | convolution fusion | flops 536870912 | bytes 9961472 | tf_op jit(solution)/shard_map/qhd,khd->qhk/dot_general | solution.py:39
  192.9 11.5 %collective-permute-done.18.refs_0_ = bf16[128,1536]{1,0:T(8,128)(2,1)S(1)} collective-permute-done((bf16[128,1536]{1,0:T(8,128)(2,1)S(1)}, bf16[128,1536]{1,0:T(8,128)(2,1)S(1)}, u32[]{:S(2)}, u32[]{:S(2)}) %collective-permute-start.18) | collective-permute-done | bytes 393248 | tf_op jit(solution)/shard_map/ppermute | solution.py:311
  209.2 2.0 shard_map.153
  212.7 2.0 shard_map.156
  214.7 2.8 %collective-permute-start.28 = (bf16[64,3584]{1,0:T(8,128)(2,1)}, bf16[64,3584]{1,0:T(8,128)(2,1)}, u32[]{:S(2)}, u32[]{:S(2)}) collective-permute-start(bf16[64,3584]{1,0:T(8,128)(2,1)} %shard_map.156), channel_id=1, source_target_pairs={{0,8},{1,9},{2,10},{3,11},{4,12},{5,13},{6,14},{7,15},{8,0},{9,1},... | collective-permute-start | bytes 1376264 | tf_op jit(solution)/shard_map/ppermute | solution.py:302
  217.5 12.2 %fusion.32 = (f32[512,4]{0,1:T(4,128)S(1)}, bf16[512,4,1024]{0,2,1:T(8,128)(2,1)}) fusion(f32[4,1024,512]{2,1,0:T(8,128)} %fusion.16, pred[512,1024]{0,1:T(8,128)(4,1)S(1)} %compare_and_fusion), kind=kOutput, calls=%fused_computation.52 | output fusion | flops 16778240 | bytes 13115392 | tf_op jit(solution)/shard_map/sub | solution.py:46
  230.8 2.3 copy.40
  234.6 16.2 %collective-permute-done.28 = bf16[64,3584]{1,0:T(8,128)(2,1)} collective-permute-done((bf16[64,3584]{1,0:T(8,128)(2,1)}, bf16[64,3584]{1,0:T(8,128)(2,1)}, u32[]{:S(2)}, u32[]{:S(2)}) %collective-permute-start.28) | collective-permute-done | bytes 458784 | tf_op jit(solution)/shard_map/ppermute | solution.py:302
  252.3 2.6 collective-permute-start.29
  (119 shorter events, 52.0 us)
Async XLA Ops:
  0.6 187.7 %copy-start = (bf16[512,512]{1,0:T(8,128)(2,1)S(1)}, bf16[512,512]{1,0:T(8,128)(2,1)}, u32[]{:S(2)}) copy-start(bf16[512,512]{1,0:T(8,128)(2,1)} %param.13) | copy-start | bytes 1572868
  5.3 16.8 %collective-permute-start.4 = (bf16[64,3712]{1,0:T(8,128)(2,1)S(1)}, bf16[64,3712]{1,0:T(8,128)(2,1)S(1)}, u32[]{:S(2)}, u32[]{:S(2)}) collective-permute-start(bf16[64,3712]{1,0:T(8,128)(2,1)S(1)} %pad_maximum_fusion.2.refs_0_), channel_id=1, source_target_pairs={{0,4},{1,5},{2,6},{3,7},{4,8},{5,9},{6,10},{7,11},{8,12},{9,13},{1... | collective-permute-start | bytes 1425416 | tf_op jit(solution)/shard_map/ppermute | solution.py:302
  8.4 22.5 %collective-permute-start.6 = (bf16[64,3712]{1,0:T(8,128)(2,1)S(1)}, bf16[64,3712]{1,0:T(8,128)(2,1)S(1)}, u32[]{:S(2)}, u32[]{:S(2)}) collective-permute-start(bf16[64,3712]{1,0:T(8,128)(2,1)S(1)} %pad_maximum_fusion.2.refs_0_), channel_id=1, source_target_pairs={{0,12},{1,13},{2,14},{3,15},{4,0},{5,1},{6,2},{7,3},{8,4},{9,5},{1... | collective-permute-start | bytes 1425416 | tf_op jit(solution)/shard_map/ppermute | solution.py:302
  10.5 41.3 %collective-permute-start.8 = (bf16[64,3712]{1,0:T(8,128)(2,1)S(1)}, bf16[64,3712]{1,0:T(8,128)(2,1)S(1)}, u32[]{:S(2)}, u32[]{:S(2)}) collective-permute-start(bf16[64,3712]{1,0:T(8,128)(2,1)S(1)} %pad_maximum_fusion.2.refs_0_), channel_id=1, source_target_pairs={{0,8},{1,9},{2,10},{3,11},{4,12},{5,13},{6,14},{7,15},{8,0},{9,1},... | collective-permute-start | bytes 1425416 | tf_op jit(solution)/shard_map/ppermute | solution.py:302
  11.4 42.0 %collective-permute-start.3 = (bf16[64,3712]{1,0:T(8,128)(2,1)S(1)}, bf16[64,3712]{1,0:T(8,128)(2,1)S(1)}, u32[]{:S(2)}, u32[]{:S(2)}) collective-permute-start(bf16[64,3712]{1,0:T(8,128)(2,1)S(1)} %pad_maximum_fusion.2.refs_0_), channel_id=1, source_target_pairs={{0,2},{1,3},{2,0},{3,1},{4,6},{5,7},{6,4},{7,5},{8,10},{9,11},{10,... | collective-permute-start | bytes 1425416 | tf_op jit(solution)/shard_map/ppermute | solution.py:305
  22.1 31.3 %collective-permute-start.5 = (bf16[64,3712]{1,0:T(8,128)(2,1)S(1)}, bf16[64,3712]{1,0:T(8,128)(2,1)}, u32[]{:S(2)}, u32[]{:S(2)}) collective-permute-start(bf16[64,3712]{1,0:T(8,128)(2,1)S(1)} %collective-permute-done.4.refs_2_), channel_id=1, source_target_pairs={{0,2},{1,3},{2,0},{3,1},{4,6},{5,7},{6,4},{7,5},{8,10},{9,11},{10,... | collective-permute-start | bytes 1425416 | tf_op jit(solution)/shard_map/ppermute | solution.py:305
  30.9 22.5 %collective-permute-start.7 = (bf16[64,3712]{1,0:T(8,128)(2,1)S(1)}, bf16[64,3712]{1,0:T(8,128)(2,1)}, u32[]{:S(2)}, u32[]{:S(2)}) collective-permute-start(bf16[64,3712]{1,0:T(8,128)(2,1)S(1)} %collective-permute-done.6.refs_4_), channel_id=1, source_target_pairs={{0,2},{1,3},{2,0},{3,1},{4,6},{5,7},{6,4},{7,5},{8,10},{9,11},{10,... | collective-permute-start | bytes 1425416 | tf_op jit(solution)/shard_map/ppermute | solution.py:305
  51.8 12.8 %collective-permute-start.9 = (bf16[64,3712]{1,0:T(8,128)(2,1)S(1)}, bf16[64,3712]{1,0:T(8,128)(2,1)S(1)}, u32[]{:S(2)}, u32[]{:S(2)}) collective-permute-start(bf16[64,3712]{1,0:T(8,128)(2,1)S(1)} %collective-permute-done.8.refs_6_), channel_id=1, source_target_pairs={{0,2},{1,3},{2,0},{3,1},{4,6},{5,7},{6,4},{7,5},{8,10},{9,11},{10,... | collective-permute-start | bytes 1425416 | tf_op jit(solution)/shard_map/ppermute | solution.py:305
  53.3 52.8 %copy-start.4 = (bf16[64,1536]{1,0:T(8,128)(2,1)S(1)}, bf16[64,1536]{1,0:T(8,128)(2,1)}, u32[]{:S(2)}) copy-start(bf16[64,1536]{1,0:T(8,128)(2,1)} %get-tuple-element.34.refs_0_) | copy-start | bytes 589828
  72.5 38.0 %collective-permute-start.14 = (bf16[256,3712]{1,0:T(8,128)(2,1)}, bf16[256,3712]{1,0:T(8,128)(2,1)}, u32[]{:S(2)}, u32[]{:S(2)}) collective-permute-start(bf16[256,3712]{1,0:T(8,128)(2,1)} %get-tuple-element.16), channel_id=1, source_target_pairs={{0,1},{1,0},{2,3},{3,2},{4,5},{5,4},{6,7},{7,6},{8,9},{9,8},{10,11... | collective-permute-start | bytes 5701640 | tf_op jit(solution)/shard_map/ppermute | solution.py:308
  73.7 32.4 %collective-permute-start.11 = (bf16[128,1536]{1,0:T(8,128)(2,1)S(1)}, bf16[128,1536]{1,0:T(8,128)(2,1)S(1)}, u32[]{:S(2)}, u32[]{:S(2)}) collective-permute-start(bf16[128,1536]{1,0:T(8,128)(2,1)S(1)} %pad_maximum_fusion.3), channel_id=1, source_target_pairs={{0,16},{16,0},{1,17},{17,1},{2,18},{18,2},{3,19},{19,3},{4,20},{20... | collective-permute-start | bytes 1179656 | tf_op jit(solution)/shard_map/ppermute | solution.py:311
  76.2 29.9 %collective-permute-start.12 = (bf16[128,1536]{1,0:T(8,128)(2,1)S(1)}, bf16[128,1536]{1,0:T(8,128)(2,1)S(1)}, u32[]{:S(2)}, u32[]{:S(2)}) collective-permute-start(bf16[128,1536]{1,0:T(8,128)(2,1)S(1)} %pad_maximum_fusion.4), channel_id=1, source_target_pairs={{0,16},{16,0},{1,17},{17,1},{2,18},{18,2},{3,19},{19,3},{4,20},{20... | collective-permute-start | bytes 1179656 | tf_op jit(solution)/shard_map/ppermute | solution.py:311
  76.8 29.3 %collective-permute-start.13 = (bf16[128,1536]{1,0:T(8,128)(2,1)S(1)}, bf16[128,1536]{1,0:T(8,128)(2,1)S(1)}, u32[]{:S(2)}, u32[]{:S(2)}) collective-permute-start(bf16[128,1536]{1,0:T(8,128)(2,1)S(1)} %pad_maximum_fusion.5), channel_id=1, source_target_pairs={{0,16},{16,0},{1,17},{17,1},{2,18},{18,2},{3,19},{19,3},{4,20},{20... | collective-permute-start | bytes 1179656 | tf_op jit(solution)/shard_map/ppermute | solution.py:311
  78.4 27.7 %collective-permute-start.10 = (bf16[64,1536]{1,0:T(8,128)(2,1)S(1)}, bf16[64,1536]{1,0:T(8,128)(2,1)S(1)}, u32[]{:S(2)}, u32[]{:S(2)}) collective-permute-start(bf16[64,1536]{1,0:T(8,128)(2,1)S(1)} %slice.46), channel_id=1, source_target_pairs={{0,16},{16,0},{1,17},{17,1},{2,18},{18,2},{3,19},{19,3},{4,20},{20... | collective-permute-start | bytes 589832 | tf_op jit(solution)/shard_map/ppermute | solution.py:311
  108.0 2.5 collective-permute-start.15
  135.7 35.5 %collective-permute-start.16 = (bf16[256,3584]{1,0:T(8,128)(2,1)}, bf16[256,3584]{1,0:T(8,128)(2,1)}, u32[]{:S(2)}, u32[]{:S(2)}) collective-permute-start(bf16[256,3584]{1,0:T(8,128)(2,1)} %get-tuple-element.21), channel_id=1, source_target_pairs={{0,1},{1,0},{2,3},{3,2},{4,5},{5,4},{6,7},{7,6},{8,9},{9,8},{10,11... | collective-permute-start | bytes 5505032 | tf_op jit(solution)/shard_map/ppermute | solution.py:308
  140.7 7.9 %collective-permute-start.17 = (bf16[256,1536]{1,0:T(8,128)(2,1)}, bf16[256,1536]{1,0:T(8,128)(2,1)}, u32[]{:S(2)}, u32[]{:S(2)}) collective-permute-start(bf16[256,1536]{1,0:T(8,128)(2,1)} %get-tuple-element.23), channel_id=1, source_target_pairs={{0,1},{1,0},{2,3},{3,2},{4,5},{5,4},{6,7},{7,6},{8,9},{9,8},{10,11... | collective-permute-start | bytes 2359304 | tf_op jit(solution)/shard_map/ppermute | solution.py:308
  141.1 13.7 %collective-permute-start.1 = (s32[512]{0:T(512)S(1)}, s32[512]{0:T(512)S(1)}, u32[]{:S(2)}, u32[]{:S(2)}) collective-permute-start(s32[512]{0:T(512)S(1)} %copy-done.10), channel_id=1, source_target_pairs={{0,16},{1,17},{2,18},{3,19},{4,20},{5,21},{6,22},{7,23},{8,24},{9,... | collective-permute-start | bytes 6152 | tf_op jit(solution)/shard_map/ppermute | solution.py:23
  146.5 13.9 %collective-permute-start.2 = (bf16[512,512]{0,1:T(8,128)(2,1)}, bf16[512,512]{0,1:T(8,128)(2,1)}, u32[]{:S(2)}, u32[]{:S(2)}) collective-permute-start(bf16[512,512]{0,1:T(8,128)(2,1)} %copy.41), channel_id=1, source_target_pairs={{0,16},{1,17},{2,18},{3,19},{4,20},{5,21},{6,22},{7,23},{8,24},{9,... | collective-permute-start | bytes 1572872 | tf_op jit(solution)/shard_map/ppermute | solution.py:21
  150.0 18.7 %collective-permute-start.20 = (bf16[128,1536]{1,0:T(8,128)(2,1)S(1)}, bf16[128,1536]{1,0:T(8,128)(2,1)S(1)}, u32[]{:S(2)}, u32[]{:S(2)}) collective-permute-start(bf16[128,1536]{1,0:T(8,128)(2,1)S(1)} %shard_map.148), channel_id=1, source_target_pairs={{0,16},{16,0},{1,17},{17,1},{2,18},{18,2},{3,19},{19,3},{4,20},{20... | collective-permute-start | bytes 1179656 | tf_op jit(solution)/shard_map/ppermute | solution.py:311
  151.4 25.7 %collective-permute-start.23 = (bf16[128,1536]{1,0:T(8,128)(2,1)S(1)}, bf16[128,1536]{1,0:T(8,128)(2,1)S(1)}, u32[]{:S(2)}, u32[]{:S(2)}) collective-permute-start(bf16[128,1536]{1,0:T(8,128)(2,1)S(1)} %shard_map.151), channel_id=1, source_target_pairs={{0,16},{16,0},{1,17},{17,1},{2,18},{18,2},{3,19},{19,3},{4,20},{20... | collective-permute-start | bytes 1179656 | tf_op jit(solution)/shard_map/ppermute | solution.py:311
  154.8 30.8 %collective-permute-start.26 = (bf16[128,1536]{1,0:T(8,128)(2,1)S(1)}, bf16[128,1536]{1,0:T(8,128)(2,1)S(1)}, u32[]{:S(2)}, u32[]{:S(2)}) collective-permute-start(bf16[128,1536]{1,0:T(8,128)(2,1)S(1)} %shard_map.154), channel_id=1, source_target_pairs={{0,16},{16,0},{1,17},{17,1},{2,18},{18,2},{3,19},{19,3},{4,20},{20... | collective-permute-start | bytes 1179656 | tf_op jit(solution)/shard_map/ppermute | solution.py:311
  160.4 69.3 %collective-permute-start = (bf16[512,512]{1,0:T(8,128)(2,1)S(1)}, bf16[512,512]{1,0:T(8,128)(2,1)S(1)}, u32[]{:S(2)}, u32[]{:S(2)}) collective-permute-start(bf16[512,512]{1,0:T(8,128)(2,1)S(1)} %copy-done.9), channel_id=1, source_target_pairs={{0,16},{1,17},{2,18},{3,19},{4,20},{5,21},{6,22},{7,23},{8,24},{9,... | collective-permute-start | bytes 1572872 | tf_op jit(solution)/shard_map/ppermute | solution.py:22
  168.7 35.7 %collective-permute-start.18 = (bf16[128,1536]{1,0:T(8,128)(2,1)S(1)}, bf16[128,1536]{1,0:T(8,128)(2,1)S(1)}, u32[]{:S(2)}, u32[]{:S(2)}) collective-permute-start(bf16[128,1536]{1,0:T(8,128)(2,1)S(1)} %shard_map.145), channel_id=1, source_target_pairs={{0,16},{16,0},{1,17},{17,1},{2,18},{18,2},{3,19},{19,3},{4,20},{20... | collective-permute-start | bytes 1179656 | tf_op jit(solution)/shard_map/ppermute | solution.py:311
  172.4 34.8 %collective-permute-start.21 = (bf16[64,3584]{1,0:T(8,128)(2,1)S(1)}, bf16[64,3584]{1,0:T(8,128)(2,1)S(1)}, u32[]{:S(2)}, u32[]{:S(2)}) collective-permute-start(bf16[64,3584]{1,0:T(8,128)(2,1)S(1)} %shard_map.149), channel_id=1, source_target_pairs={{0,2},{1,3},{2,0},{3,1},{4,6},{5,7},{6,4},{7,5},{8,10},{9,11},{10,... | collective-permute-start | bytes 1376264 | tf_op jit(solution)/shard_map/ppermute | solution.py:305
  178.3 30.9 %collective-permute-start.24 = (bf16[64,3584]{1,0:T(8,128)(2,1)S(1)}, bf16[64,3584]{1,0:T(8,128)(2,1)S(1)}, u32[]{:S(2)}, u32[]{:S(2)}) collective-permute-start(bf16[64,3584]{1,0:T(8,128)(2,1)S(1)} %shard_map.152), channel_id=1, source_target_pairs={{0,2},{1,3},{2,0},{3,1},{4,6},{5,7},{6,4},{7,5},{8,10},{9,11},{10,... | collective-permute-start | bytes 1376264 | tf_op jit(solution)/shard_map/ppermute | solution.py:305
  186.8 25.9 %collective-permute-start.27 = (bf16[64,3584]{1,0:T(8,128)(2,1)S(1)}, bf16[64,3584]{1,0:T(8,128)(2,1)S(1)}, u32[]{:S(2)}, u32[]{:S(2)}) collective-permute-start(bf16[64,3584]{1,0:T(8,128)(2,1)S(1)} %shard_map.155), channel_id=1, source_target_pairs={{0,2},{1,3},{2,0},{3,1},{4,6},{5,7},{6,4},{7,5},{8,10},{9,11},{10,... | collective-permute-start | bytes 1376264 | tf_op jit(solution)/shard_map/ppermute | solution.py:305
  205.6 27.4 %collective-permute-start.19 = (bf16[64,3584]{1,0:T(8,128)(2,1)S(1)}, bf16[64,3584]{1,0:T(8,128)(2,1)}, u32[]{:S(2)}, u32[]{:S(2)}) collective-permute-start(bf16[64,3584]{1,0:T(8,128)(2,1)S(1)} %shard_map.146), channel_id=1, source_target_pairs={{0,2},{1,3},{2,0},{3,1},{4,6},{5,7},{6,4},{7,5},{8,10},{9,11},{10,... | collective-permute-start | bytes 1376264 | tf_op jit(solution)/shard_map/ppermute | solution.py:305
  208.4 26.2 %collective-permute-start.22 = (bf16[64,3584]{1,0:T(8,128)(2,1)S(1)}, bf16[64,3584]{1,0:T(8,128)(2,1)}, u32[]{:S(2)}, u32[]{:S(2)}) collective-permute-start(bf16[64,3584]{1,0:T(8,128)(2,1)S(1)} %shard_map.150), channel_id=1, source_target_pairs={{0,12},{1,13},{2,14},{3,15},{4,0},{5,1},{6,2},{7,3},{8,4},{9,5},{1... | collective-permute-start | bytes 1376264 | tf_op jit(solution)/shard_map/ppermute | solution.py:302
  211.2 23.4 %collective-permute-start.25 = (bf16[64,3584]{1,0:T(8,128)(2,1)}, bf16[64,3584]{1,0:T(8,128)(2,1)}, u32[]{:S(2)}, u32[]{:S(2)}) collective-permute-start(bf16[64,3584]{1,0:T(8,128)(2,1)} %shard_map.153), channel_id=1, source_target_pairs={{0,4},{1,5},{2,6},{3,7},{4,8},{5,9},{6,10},{7,11},{8,12},{9,13},{1... | collective-permute-start | bytes 1376264 | tf_op jit(solution)/shard_map/ppermute | solution.py:302
  214.7 36.1 %collective-permute-start.28 = (bf16[64,3584]{1,0:T(8,128)(2,1)}, bf16[64,3584]{1,0:T(8,128)(2,1)}, u32[]{:S(2)}, u32[]{:S(2)}) collective-permute-start(bf16[64,3584]{1,0:T(8,128)(2,1)} %shard_map.156), channel_id=1, source_target_pairs={{0,8},{1,9},{2,10},{3,11},{4,12},{5,13},{6,14},{7,15},{8,0},{9,1},... | collective-permute-start | bytes 1376264 | tf_op jit(solution)/shard_map/ppermute | solution.py:302
  252.3 5.5 %collective-permute-start.29 = (bf16[64,1024]{1,0:T(8,128)(2,1)S(1)}, bf16[64,1024]{1,0:T(8,128)(2,1)S(1)}, u32[]{:S(2)}, u32[]{:S(2)}) collective-permute-start(bf16[64,1024]{1,0:T(8,128)(2,1)S(1)} %slice.55), channel_id=1, source_target_pairs={{0,16},{16,0},{1,17},{17,1},{2,18},{18,2},{3,19},{19,3},{4,20},{20... | collective-permute-start | bytes 393224 | tf_op jit(solution)/shard_map/ppermute | solution.py:311
  (14 other events, 220.0 us)

commit v3 on v1

--- a/solution.py
+++ b/solution.py
@@ -1,6 +1,8 @@
 import jax
 import jax.numpy as jnp
 from jax import lax
+from jax.experimental import pallas as pl
+from jax.experimental.pallas import tpu as pltpu
 from jax.sharding import PartitionSpec as P
 
 HD = 128
@@ -51,6 +53,258 @@
     )
     return (summed / total[:, :, None]).reshape(rows, heads * HD).astype(BF16)
 
+SHARED = 1280
+OVER_X = 1536
+ORDER = [2, 1, 3, 0]
+
+VMEM = pl.BlockSpec(memory_space=pltpu.VMEM)
+SMEM = pl.BlockSpec(memory_space=pltpu.SMEM)
+MIB = 1024 * 1024
+LANES = 128
+
+
+def call(body, out_shape, flops, moved, room, **kw):
+    return pl.pallas_call(
+        body,
+        out_shape=out_shape,
+        compiler_params=pltpu.CompilerParams(vmem_limit_bytes=room * MIB),
+        cost_estimate=pl.CostEstimate(flops=flops, bytes_accessed=moved, transcendentals=0),
+        **kw,
+    )
+
+
+def prepare(tokens, expert_ids, route_weight, at_x, experts):
+    rows, width = tokens.shape
+    split = (width - SHARED) // 2
+
+    def body(x_ref, tokens, ids, weights, out, theirs):
+        own = pl.ds(pl.multiple_of(SHARED + x_ref[0] * split, LANES), split)
+        other = pl.ds(pl.multiple_of(SHARED + (1 - x_ref[0]) * split, LANES), split)
+        out[:, :SHARED] = tokens[:, :SHARED]
+        out[:, SHARED : SHARED + split] = tokens[:, own]
+        theirs[...] = tokens[:, other]
+        column = lax.broadcasted_iota(jnp.int32, (LANES, rows), 0)
+        expert, term = column % experts, column // experts
+        meta = jnp.zeros((LANES, rows), F32)
+        for k in range(TOP):
+            weight = jnp.broadcast_to(weights[k : k + 1, :], (LANES, rows))
+            high = weight.astype(BF16).astype(F32)
+            middle = (weight - high).astype(BF16).astype(F32)
+            low = weight - high - middle
+            value = jnp.where(term == 1, high, jnp.where(term == 2, middle, low))
+            value = jnp.where(term == 0, 1.0, value)
+            meta = jnp.where((ids[k : k + 1, :] == expert) & (term < 4), value, meta)
+        eye = lax.broadcasted_iota(jnp.int32, (LANES, LANES), 0) == lax.broadcasted_iota(
+            jnp.int32, (LANES, LANES), 1
+        )
+        meta = lax.dot_general(
+            meta.astype(BF16),
+            jnp.where(eye, 1.0, 0.0).astype(BF16),
+            (((0,), (0,)), ((), ())),
+            preferred_element_type=F32,
+        )
+        out[:, SHARED + split :] = meta.astype(BF16)
+
+    return call(
+        body,
+        (
+            jax.ShapeDtypeStruct((rows, SHARED + split + LANES), BF16),
+            jax.ShapeDtypeStruct((rows, split), BF16),
+        ),
+        0,
+        4 * rows * width,
+        8,
+        in_specs=[SMEM] + [VMEM] * 3,
+        out_specs=(VMEM,) * 2,
+    )(at_x.reshape(1), tokens, expert_ids.T, route_weight.T)
+
+
+def pick(blocks, more, me, at_x, cap):
+    count = len(blocks)
+    rows, width = blocks[0].shape
+    split = more[0].shape[1]
+    edge = width - LANES
+    features = edge + split
+    step = 4
+    total = count + len(more)
+
+    def body(s_ref, *refs):
+        sources, (near, meta, other, placing, wide, *held, done) = refs[:total], refs[total:]
+        copies = [
+            pltpu.make_async_copy(source, to, done.at[i])
+            for i, (source, to) in enumerate(zip(sources, held))
+        ]
+        for copy in copies:
+            copy.start()
+        for copy in copies:
+            copy.wait()
+        ins, extra = held[:count], held[count:]
+        mine, x = s_ref[0], s_ref[1]
+        lane = lax.broadcasted_iota(jnp.int32, (rows, LANES), 1)
+        earlier = lax.broadcasted_iota(jnp.int32, (rows, rows), 0) > lax.broadcasted_iota(
+            jnp.int32, (rows, rows), 1
+        )
+        slot = lax.broadcasted_iota(jnp.int32, (rows, cap), 1).astype(F32)
+        own = pl.ds(pl.multiple_of(SHARED + x * split, LANES), split)
+        theirs = pl.ds(pl.multiple_of(SHARED + (1 - x) * split, LANES), split)
+        pieces = [
+            ref[b * rows : (b + 1) * rows, :] for ref in extra for b in range(ref.shape[0] // rows)
+        ]
+        for begin in range(0, count, step):
+            wide[...] = jnp.zeros_like(wide)
+            for i in range(begin, begin + step):
+                member = ins[i][:, edge:]
+                rank = jnp.dot(earlier.astype(BF16), member, preferred_element_type=F32)
+                member = member.astype(F32)
+                local = i - begin
+                for j in range(2):
+                    at = lane == (mine if j == 0 else mine + 1 - 2 * (mine % 2))
+                    hit = jnp.sum(jnp.where(at, member, 0.0), axis=1, keepdims=True)
+                    place = jnp.sum(jnp.where(at, rank, 0.0), axis=1, keepdims=True)
+                    onehot = jnp.where((place == slot) & (hit > 0.5), 1.0, 0.0).astype(BF16)
+                    placing[i, :, j * cap : (j + 1) * cap] = onehot
+                    column = (j * step + local) * cap
+                    wide[local * rows : (local + 1) * rows, column : column + cap] = onehot
+            onehot = wide[...]
+            to = slice(begin * cap, (begin + step) * cap)
+
+            def rows_of(parts):
+                got = lax.dot_general(
+                    onehot,
+                    jnp.concatenate(parts, axis=0),
+                    (((0,), (0,)), ((), ())),
+                    preferred_element_type=F32,
+                ).astype(BF16)
+                return got[: step * cap], got[step * cap :]
+
+            these = ins[begin : begin + step]
+            near[to, :SHARED], other[to, :SHARED] = rows_of([r[:, :SHARED] for r in these])
+            near[to, own], other[to, own] = rows_of([r[:, SHARED:edge] for r in these])
+            near[to, theirs], other[to, theirs] = rows_of(pieces[begin : begin + step])
+            meta[to, :], other[to, features:] = rows_of([r[:, edge:] for r in these])
+
+    shape = lambda *s: jax.ShapeDtypeStruct(s, BF16)
+    return call(
+        body,
+        (
+            shape(count * cap, features),
+            shape(count * cap, LANES),
+            shape(count * cap, features + LANES),
+            shape(count, rows, 2 * cap),
+        ),
+        4 * count * cap * rows * features,
+        2 * count * (rows + 2 * cap) * features,
+        20,
+        in_specs=[SMEM] + [pl.BlockSpec(memory_space=pltpu.HBM)] * total,
+        out_specs=(VMEM,) * 4,
+        scratch_shapes=[pltpu.VMEM((step * rows, 2 * step * cap), BF16)]
+        + [pltpu.VMEM(a.shape, BF16) for a in (*blocks, *more)]
+        + [pltpu.SemaphoreType.DMA((total,))],
+    )(jnp.stack([me, at_x]), *blocks, *more)
+
+
+def mix(placing, near, far, far_first, first, count, at_x, late, adds=(), dtype=BF16):
+    _, rows, both = placing.shape
+    cap = both // 2
+    half = near.shape[1] // 2
+    rest = half - OVER_X
+    width = OVER_X if late else half + rest
+
+    def body(x_ref, placing, near, far, *refs):
+        out = refs[-1]
+        own = pl.multiple_of(x_ref[0] * half, LANES)
+        other = pl.multiple_of((1 - x_ref[0]) * half, LANES)
+        if late:
+            parts = [(other, OVER_X, 0)]
+        else:
+            parts = [
+                (own, OVER_X, 0),
+                (pl.multiple_of(own + OVER_X, LANES), rest, OVER_X),
+                (pl.multiple_of(other + OVER_X, LANES), rest, half),
+            ]
+        for start, size, to in parts:
+            columns = pl.ds(start, size)
+            slots = jnp.concatenate([near[:, columns], far[:, columns]], axis=0)
+            total = jnp.dot(placing[0], slots, preferred_element_type=F32)
+            for ref in refs[:-1]:
+                if to + size <= ref.shape[1]:
+                    total = total + ref[:, to : to + size].astype(F32)
+            out[:, to : to + size] = total.astype(dtype)
+
+    def at(base):
+        return lambda g: (g + base, 0)
+
+    return call(
+        body,
+        jax.ShapeDtypeStruct((count * rows, width), dtype),
+        4 * count * rows * cap * width,
+        2 * count * (rows + 2 * cap) * width,
+        12,
+        grid=(count,),
+        in_specs=[
+            SMEM,
+            pl.BlockSpec((1, rows, both), lambda g: (g + first, 0, 0)),
+            pl.BlockSpec((cap, 2 * half), at(first)),
+            pl.BlockSpec((cap, 2 * half), at(first - far_first)),
+        ]
+        + [pl.BlockSpec((rows, a.shape[1]), at(base)) for a, base in adds],
+        out_specs=pl.BlockSpec((rows, width), at(0)),
+    )(at_x.reshape(1), placing, near, far, *[a for a, _ in adds])
+
+
+def attend_pair(q_input, k_input, v_input, docs, past, at_x):
+    rows, width = q_input.shape
+    scale = HD ** (-0.5)
+    turn = (((1,), (1,)), ((), ()))
+
+    def body(x_ref, q, k, v, docs, past_k, past_v, past_docs, out, bias):
+        @pl.when(pl.program_id(0) == 0)
+        def _():
+            i = lax.broadcasted_iota(jnp.int32, (rows, rows), 0)
+            j = lax.broadcasted_iota(jnp.int32, (rows, rows), 1)
+            same = lax.dot_general(docs[...], past_docs[...], turn, preferred_element_type=F32)
+            bias[:, :rows] = jnp.where((same > 0.5) & (x_ref[0] > 0), 0.0, -1e30)
+            same = lax.dot_general(docs[...], docs[...], turn, preferred_element_type=F32)
+            bias[:, rows:] = jnp.where((same > 0.5) & (j <= i), 0.0, -1e30)
+
+        query = q[...]
+        early = lax.dot_general(query, past_k[...], turn, preferred_element_type=F32)
+        late = lax.dot_general(query, k[...], turn, preferred_element_type=F32)
+        early = early * scale + bias[:, :rows]
+        late = late * scale + bias[:, rows:]
+        top = jnp.maximum(
+            jnp.max(early, axis=1, keepdims=True), jnp.max(late, axis=1, keepdims=True)
+        )
+        early, late = jnp.exp(early - top), jnp.exp(late - top)
+        total = jnp.sum(early, axis=1, keepdims=True) + jnp.sum(late, axis=1, keepdims=True)
+        mixed = jnp.dot(early.astype(BF16), past_v[...], preferred_element_type=F32) + jnp.dot(
+            late.astype(BF16), v[...], preferred_element_type=F32
+        )
+        out[...] = (mixed / total).astype(BF16)
+
+    heads = width // HD
+    head = pl.BlockSpec((rows, HD), lambda h: (0, h))
+    return call(
+        body,
+        jax.ShapeDtypeStruct((rows, width), BF16),
+        8 * rows * rows * width,
+        14 * rows * width,
+        14,
+        grid=(heads,),
+        in_specs=[
+            SMEM,
+            head,
+            head,
+            head,
+            pl.BlockSpec((rows, LANES), lambda h: (0, 0)),
+            head,
+            pl.BlockSpec((rows, HD), lambda h: (0, heads + h)),
+            pl.BlockSpec((rows, LANES), lambda h: (0, 2 * heads)),
+        ],
+        out_specs=head,
+        scratch_shapes=[pltpu.VMEM((rows, 2 * rows), F32)],
+    )(at_x.reshape(1), q_input, k_input, v_input, docs, past, past, past)
+
 
 def spread(onehot):
     blocks, cap, rows = onehot.shape
@@ -203,6 +457,104 @@
         attn_out = attend(q_input, k_input, v_input, segment_ids, n_ctx)
         return attn_out, moe_out
 
+    def pair_device(
+        q_input, k_input, v_input, segment_ids, tokens, expert_ids, route_weight, w_in, w_down
+    ):
+        me = lax.axis_index("exp")
+        at_x = lax.axis_index("ctx")
+        rows, width = tokens.shape
+        cap = rows * 8 // n_exp
+        half = width // 2
+        split = (width - SHARED) // 2
+        after = lax.optimization_barrier
+
+        block, theirs = prepare(tokens, expert_ids, route_weight, at_x, n_exp)
+        cut = lambda a: a[:, SHARED : SHARED + split]
+        both = lambda d: jnp.concatenate([cut(line[d]), cut(across[d])], axis=0)
+        line = {0: block, 1: z_shift(block, 1), 3: z_shift(block, -1)}
+        line[2] = z_shift(line[1], 1)
+        across = {0: y_swap(block)}
+        block, segment_ids, k_input = after((block, segment_ids, k_input))
+        docs = segment_ids[:, None] == jnp.arange(LANES, dtype=jnp.int32)
+        docs = docs.astype(BF16)
+        past = lax.ppermute(jnp.concatenate([k_input, v_input, docs], axis=1), "ctx", [(0, 1)])
+        line[1], across[0] = after((line[1], across[0]))
+        across[1] = y_swap(line[1])
+        line[3], across[1] = after((line[3], across[1]))
+        across[3] = y_swap(line[3])
+        across[0], past = after((across[0], past))
+        more = {0: [theirs, x_swap(cut(across[0]))], 1: [x_swap(both(1))]}
+        line[2], across[3], before = after((line[2], across[3], more[0][1]))
+        more[0][1] = before
+        across[2] = y_swap(line[2])
+        more[3] = [x_swap(both(3))]
+        line[2], before = after((line[2], more[1][0]))
+        more[1] = [before]
+        more[2] = [x_swap(cut(line[2]))]
+        attn_out = attend_pair(q_input, k_input, v_input, docs, past, at_x)
+        across[2], before, attn_out = after((across[2], more[3][0], attn_out))
+        more[3] = [before]
+        more[2].append(x_swap(cut(across[2])))
+
+        near, meta, sent, placing = pick(
+            [b for d in ORDER for b in (line[d], across[d])],
+            [a for d in ORDER for a in more[d]],
+            me,
+            at_x,
+            cap,
+        )
+        far = core_swap(sent)
+        def expert(block, meta):
+            gate = jnp.dot(block, w_in[0, 0], preferred_element_type=F32)
+            up = jnp.dot(block, w_in[0, 1], preferred_element_type=F32)
+            gate, up = after((gate, up))
+            hidden = (jax.nn.silu(gate) * up).astype(BF16)
+            lane = jnp.arange(LANES, dtype=jnp.int32)
+            at = (lane % n_exp == me) & (lane >= n_exp) & (lane < 4 * n_exp)
+            scale = jnp.sum(jnp.where(at, meta.astype(F32), 0.0), axis=1, keepdims=True)
+            hidden, scale = after((hidden, scale))
+            out = jnp.dot(hidden, w_down[0], preferred_element_type=F32)
+            return (out * scale).astype(BF16)
+
+        near = expert(near, meta)
+        near, far = after((near, far))
+        sent = expert(far[:, :width], far[:, width:])
+        edge = sent.shape[0] // 2
+        far_a = core_swap(sent[:edge])
+        far_a, rest = after((far_a, sent[edge:]))
+        far_b = core_swap(rest)
+
+        def sums(i, count, late, adds=(), dtype=BF16):
+            far, begin = (far_a, 0) if i < 4 else (far_b, 4)
+            return mix(placing, near, far, begin, i, count, at_x, late, adds, dtype)
+
+        got_x = []
+        for i in range(4):
+            late = sums(2 * i, 2, True)
+            near, late = after((near, late))
+            got_x.append(x_swap(late))
+
+        def over_y(i):
+            return y_swap(sums(2 * i + 1, 1, False, [(got_x[i], 1)]))
+
+        got_y = [over_y(0), over_y(1)]
+        part = sums(0, 1, False, [(got_x[0], 0), (got_y[0], 0)])
+        part = z_shift(part, -1)
+        got_x[2], part = after((got_x[2], part))
+        got_y.append(over_y(2))
+        part = sums(2, 1, False, [(got_x[1], 0), (got_y[1], 0), (part, 0)])
+        right = z_shift(part, -1)
+        got_x[3], right = after((got_x[3], right))
+        got_y.append(over_y(3))
+        left = z_shift(sums(4, 1, False, [(got_x[2], 0), (got_y[2], 0)]), 1)
+        total = sums(6, 1, False, [(got_x[3], 0), (got_y[3], 0)], F32)
+        total = total + right.astype(F32) + left.astype(F32)
+        got = x_swap(total[:, half:].astype(BF16))
+        moe_out = jnp.concatenate(
+            [total[:, :OVER_X], total[:, OVER_X:half] + got.astype(F32)], axis=1
+        ).astype(BF16)
+        return attn_out, moe_out
+
     in_specs = (
         P("ctx", "exp"),
         P("ctx", "exp"),
@@ -216,5 +568,9 @@
     )
     out_specs = (P("ctx", "exp"), P("exp", "ctx"))
     return jax.shard_map(
-        on_device, mesh=mesh, in_specs=in_specs, out_specs=out_specs, check_vma=False
+        pair_device if n_ctx == 2 and nz == 4 else on_device,
+        mesh=mesh,
+        in_specs=in_specs,
+        out_specs=out_specs,
+        check_vma=False,
     )

time: 272 us -> 181 us (0.67); the launches traced: 268 us -> 181 us
  matrix products: 52 us -> 16.9 us
  starting transfers between devices: 75.5 us -> 44.2 us
  waiting for transfers between devices: 60.8 us -> 85.1 us
  local copies, waits for them, and re-layouts: 35.1 us -> 11.7 us
  blocking collectives: 20.6 us -> 0 us
  other arithmetic: 22.2 us -> 3.84 us
  Pallas kernels: 0 us -> 18.2 us
    ppermute x30 -> x6, starting transfers between devices: 52.4 us -> 12.1 us  [z_shift(): return lax.ppermute(x, 'exp', pairs(lambda z, y, c: (z + d, y, c)))]
    dot_general x27 -> x6, matrix products: 52 us -> 16.9 us  [the longest x2 7.79 us: expert(): up = jnp.dot(block, w_in[0, 1], preferred_element_type=F32)]
    ppermute x8 -> x10, waiting for transfers between devices: 12.8 us -> 38 us  [x_swap(): return lax.ppermute(x, 'ctx', [(0, 1), (1, 0)])]
    all_gather x1 -> x0, blocking collectives: 20.6 us -> none  [on_device(): meta = lax.all_gather(meta, 'exp', axis=0, tiled=False)]
    pallas_call x0 -> x15, Pallas kernels: none -> 18.2 us  [the longest x1 7.68 us: attend_pair(): call(body, jax.ShapeDtypeStruct((rows, width), BF16), 8 * rows * rows * w...]
    ppermute x8 -> x10, starting transfers between devices: 6.7 us -> 16.6 us  [x_swap(): return lax.ppermute(x, 'ctx', [(0, 1), (1, 0)])]
    unnamed x57 -> x34, local copies, waits for them, and re-layouts: 19.5 us -> 9.97 us
    slice x23 -> x10, local copies, waits for them, and re-layouts: 8.58 us -> 1.73 us  [the longest x7 1.53 us: pair_device(): cut = lambda a: a[:, SHARED:SHARED + split]]
  transfers between devices with their start and end apart: 61 -> 28, of which waited for: 21 -> 21; matrix products, arithmetic and copies ran while one was open for 31% -> 7% of each run, Pallas kernels for 0% -> 6%
where the time goes in v3:
time: 181 us
  waiting for transfers between devices  85.1 us (47%)
  starting transfers between devices  44.2 us (24%)
  Pallas kernels  18.2 us (10%)
  matrix products  16.9 us (9%)
  local copies, waits for them, and re-layouts  11.7 us (6%)
  other arithmetic  3.84 us (2%)
    ppermute x10, waiting for transfers between devices, x_swap(): return lax.ppermute(x, 'ctx', [(0, 1), (1, 0)])  38 us
    ppermute x8, waiting for transfers between devices, y_swap(): return lax.ppermute(x, 'exp', pairs(lambda z, y, c: (z, 1 - y, c)))  25.5 us
    ppermute x6, waiting for transfers between devices, z_shift(): return lax.ppermute(x, 'exp', pairs(lambda z, y, c: (z + d, y, c)))  18.8 us
    ppermute x10, starting transfers between devices, x_swap(): return lax.ppermute(x, 'ctx', [(0, 1), (1, 0)])  16.6 us
    ppermute x6, starting transfers between devices, z_shift(): return lax.ppermute(x, 'exp', pairs(lambda z, y, c: (z + d, y, c)))  12.1 us
    unnamed x34, local copies, waits for them, and re-layouts  9.97 us
    ppermute x8, starting transfers between devices, y_swap(): return lax.ppermute(x, 'exp', pairs(lambda z, y, c: (z, 1 - y, c)))  9.47 us
    dot_general x2, matrix products, expert(): up = jnp.dot(block, w_in[0, 1], preferred_element_type=F32)  7.79 us
  transfers between devices with their start and end apart: 28, of which 21 were waited for; matrix products, arithmetic and copies ran while one was open for 7% of the time, Pallas kernels for 6%

profile of v3, /device:TPU:0, one launch (start us, length us, event | category | flops | bytes accessed | tf_op | source)
XLA Modules:
  0.0 180.9 jit_solution(8142940027468607862)
XLA Ops:
  6.2 5.0 %collective-permute-start.6 = (bf16[512,1152]{1,0:T(8,128)(2,1)S(1)}, bf16[512,1152]{1,0:T(8,128)(2,1)S(1)}, u32[]{:S(2)}, u32[]{:S(2)}) collective-permute-start(bf16[512,1152]{1,0:T(8,128)(2,1)S(1)} %pad_maximum_fusion), channel_id=1, source_target_pairs={{0,16},{1,17},{2,18},{3,19},{4,20},{5,21},{6,22},{7,23},{8,24},{9,... | collective-permute-start | bytes 3538952 | tf_op jit(solution)/shard_map/ppermute | solution.py:480
  14.4 2.2 %collective-permute-start.2 = (bf16[64,3328]{1,0:T(8,128)(2,1)S(1)}, bf16[64,3328]{1,0:T(8,128)(2,1)S(1)}, u32[]{:S(2)}, u32[]{:S(2)}) collective-permute-start(bf16[64,3328]{1,0:T(8,128)(2,1)S(1)} %get-tuple-element.48.refs_6_), channel_id=1, source_target_pairs={{0,12},{1,13},{2,14},{3,15},{4,0},{5,1},{6,2},{7,3},{8,4},{9,5},{1... | collective-permute-start | bytes 1277960 | tf_op jit(solution)/shard_map/ppermute | solution.py:330
  16.6 5.9 %collective-permute-done.3.refs_7_ = bf16[64,3328]{1,0:T(8,128)(2,1)S(1)} collective-permute-done((bf16[64,3328]{1,0:T(8,128)(2,1)S(1)}, bf16[64,3328]{1,0:T(8,128)(2,1)S(1)}, u32[]{:S(2)}, u32[]{:S(2)}) %collective-permute-start.3) | collective-permute-done | bytes 426016 | tf_op jit(solution)/shard_map/ppermute | solution.py:333
  22.6 4.8 %collective-permute-done.refs_2_ = bf16[64,3328]{1,0:T(8,128)(2,1)S(1)} collective-permute-done((bf16[64,3328]{1,0:T(8,128)(2,1)S(1)}, bf16[64,3328]{1,0:T(8,128)(2,1)S(1)}, u32[]{:S(2)}, u32[]{:S(2)}) %collective-permute-start) | collective-permute-done | bytes 426016 | tf_op jit(solution)/shard_map/ppermute | solution.py:330
  27.9 7.4 %collective-permute-done.2.refs_4_ = bf16[64,3328]{1,0:T(8,128)(2,1)S(1)} collective-permute-done((bf16[64,3328]{1,0:T(8,128)(2,1)S(1)}, bf16[64,3328]{1,0:T(8,128)(2,1)S(1)}, u32[]{:S(2)}, u32[]{:S(2)}) %collective-permute-start.2) | collective-permute-done | bytes 426016 | tf_op jit(solution)/shard_map/ppermute | solution.py:330
  36.4 2.5 %collective-permute-start.7 = (bf16[64,1920]{1,0:T(8,128)(2,1)S(1)}, bf16[64,1920]{1,0:T(8,128)(2,1)S(1)}, u32[]{:S(2)}, u32[]{:S(2)}) collective-permute-start(bf16[64,1920]{1,0:T(8,128)(2,1)S(1)} %slice.52), channel_id=1, source_target_pairs={{0,16},{16,0},{1,17},{17,1},{2,18},{18,2},{3,19},{19,3},{4,20},{20... | collective-permute-start | bytes 737288 | tf_op jit(solution)/shard_map/ppermute | solution.py:339
  39.1 4.8 %collective-permute-done.1.refs_0_ = bf16[64,3328]{1,0:T(8,128)(2,1)S(1)} collective-permute-done((bf16[64,3328]{1,0:T(8,128)(2,1)S(1)}, bf16[64,3328]{1,0:T(8,128)(2,1)S(1)}, u32[]{:S(2)}, u32[]{:S(2)}) %collective-permute-start.1) | collective-permute-done | bytes 426016 | tf_op jit(solution)/shard_map/ppermute | solution.py:330
  45.9 2.1 %collective-permute-start.9 = (bf16[128,1920]{1,0:T(8,128)(2,1)S(1)}, bf16[128,1920]{1,0:T(8,128)(2,1)S(1)}, u32[]{:S(2)}, u32[]{:S(2)}) collective-permute-start(bf16[128,1920]{1,0:T(8,128)(2,1)S(1)} %pad_maximum_fusion.1), channel_id=1, source_target_pairs={{0,16},{16,0},{1,17},{17,1},{2,18},{18,2},{3,19},{19,3},{4,20},{20... | collective-permute-start | bytes 1474568 | tf_op jit(solution)/shard_map/ppermute | solution.py:339
  49.5 7.7 %shard_map.105 = bf16[512,512]{1,0:T(8,128)(2,1)} custom-call(s32[1]{0:T(128)} %bitcast.x_ref, bf16[512,512]{1,0:T(8,128)(2,1)S(1)} %copy-done.3, bf16[512,512]{1,0:T(8,128)(2,1)S(1)} %copy-done, bf16[512,512]{1,0:T(8,128)(2,1)S(1)} %copy-done.1, bf16[512,128]{1,0:T(8,128)(2,1)S(1)} %fusion.31.docs, ...), custom_call_target="tpu_custom_call" | custom-call | flops 1073741824 | bytes 3670016 | tf_op jit(solution)/shard_map/pallas_call | solution.py:287
  59.1 7.8 %collective-permute-done.9.refs_11_ = bf16[128,1920]{1,0:T(8,128)(2,1)S(1)} collective-permute-done((bf16[128,1920]{1,0:T(8,128)(2,1)S(1)}, bf16[128,1920]{1,0:T(8,128)(2,1)S(1)}, u32[]{:S(2)}, u32[]{:S(2)}) %collective-permute-start.9) | collective-permute-done | bytes 491552 | tf_op jit(solution)/shard_map/ppermute | solution.py:339
  68.3 2.0 %collective-permute-start.12 = (bf16[64,1920]{1,0:T(8,128)(2,1)}, bf16[64,1920]{1,0:T(8,128)(2,1)}, u32[]{:S(2)}, u32[]{:S(2)}) collective-permute-start(bf16[64,1920]{1,0:T(8,128)(2,1)} %slice.58), channel_id=1, source_target_pairs={{0,16},{16,0},{1,17},{17,1},{2,18},{18,2},{3,19},{19,3},{4,20},{20... | collective-permute-start | bytes 737288 | tf_op jit(solution)/shard_map/ppermute | solution.py:339
  70.4 1.8 collective-permute-done.11.refs_8_
  72.2 3.5 %collective-permute-done.12.refs_9_ = bf16[64,1920]{1,0:T(8,128)(2,1)} collective-permute-done((bf16[64,1920]{1,0:T(8,128)(2,1)}, bf16[64,1920]{1,0:T(8,128)(2,1)}, u32[]{:S(2)}, u32[]{:S(2)}) %collective-permute-start.12) | collective-permute-done | bytes 245792 | tf_op jit(solution)/shard_map/ppermute | solution.py:339
  79.6 6.5 %shard_map.106 = (bf16[256,5120]{1,0:T(8,128)(2,1)S(1)}, bf16[256,128]{1,0:T(8,128)(2,1)S(1)}, bf16[256,5248]{1,0:T(8,128)(2,1)S(1)}, bf16[8,64,64]{2,1,0:T(8,128)(2,1)S(1)}) custom-call(s32[2]{0:T(128)S(1)} %pad_add_fusion.s_ref, bf16[64,3328]{1,0:T(8,128)(2,1)S(1)} %collective-permute-done.1.refs_0_, bf16[64,3328]{1,0:T(8,128)(2,1)S(1)} %collective-permute-done.8.refs_1_, ...), custom_call_target="tpu_custom_call" | custom-call | flops 335544320 | bytes 10485760 | tf_op jit(solution)/shard_map/pallas_call | solution.py:187
  86.3 5.6 %fusion.6 = f32[256,768]{1,0:T(8,128)S(1)} fusion(bf16[256,5120]{1,0:T(8,128)(2,1)S(1)} %get-tuple-element.67, bf16[1,2,5120,768]{3,2,1,0:T(8,128)(2,1)} %param.16), kind=kOutput, calls=%fused_computation.6 | convolution fusion | flops 2013265920 | bytes 11272192 | tf_op jit(solution)/shard_map/dot_general | solution.py:509
  91.9 2.1 %copy-done.14 = bf16[1,2,5120,768]{3,2,1,0:T(8,128)(2,1)S(1)} copy-done((bf16[1,2,5120,768]{3,2,1,0:T(8,128)(2,1)S(1)}, bf16[1,2,5120,768]{3,2,1,0:T(8,128)(2,1)}, u32[]{:S(2)}) %copy-start.14) | copy-done | bytes 15728664
  94.0 2.2 %fusion.10 = f32[256,768]{1,0:T(8,128)S(1)} fusion(bf16[256,5120]{1,0:T(8,128)(2,1)S(1)} %get-tuple-element.67, bf16[1,2,5120,768]{3,2,1,0:T(8,128)(2,1)S(1)} %copy-done.14), kind=kOutput, calls=%fused_computation.10 | convolution fusion | flops 2013265920 | bytes 11272192 | tf_op jit(solution)/shard_map/dot_general | solution.py:508
  96.6 2.2 %fusion.25.near = bf16[256,5120]{1,0:T(8,128)(2,1)S(1)} fusion(bf16[256,768]{1,0:T(8,128)(2,1)S(1)} %multiply_convert_fusion.1, bf16[1,768,5120]{2,1,0:T(8,128)(2,1)S(1)} %bitcast.38, f32[256]{0:T(256)S(1)} %select_reduce_fusion.1), kind=kOutput, calls=%fused_computation.19 | convolution fusion | flops 2015887360 | bytes 10880000 | tf_op jit(solution)/shard_map/dot_general | solution.py:516
  98.9 2.2 %fusion.4 = f32[256,768]{1,0:T(8,128)S(1)} fusion(bf16[1,2,5120,768]{3,2,1,0:T(8,128)(2,1)S(1)} %copy-done.14, bf16[256,5248]{1,0:T(8,128)(2,1)S(1)} %collective-permute-done.13), kind=kOutput, calls=%fused_computation.4 | convolution fusion | flops 2013265920 | bytes 11272192 | tf_op jit(solution)/shard_map/dot_general | solution.py:509
  101.1 2.2 %fusion.8 = f32[256,768]{1,0:T(8,128)S(1)} fusion(bf16[1,2,5120,768]{3,2,1,0:T(8,128)(2,1)S(1)} %copy-done.14, bf16[256,5248]{1,0:T(8,128)(2,1)S(1)} %collective-permute-done.13), kind=kOutput, calls=%fused_computation.8 | convolution fusion | flops 2013265920 | bytes 11272192 | tf_op jit(solution)/shard_map/dot_general | solution.py:508
  103.5 2.5 %fusion.22 = bf16[256,5120]{1,0:T(8,128)(2,1)S(1)} fusion(bf16[256,768]{1,0:T(8,128)(2,1)S(1)} %multiply_convert_fusion, bf16[1,768,5120]{2,1,0:T(8,128)(2,1)S(1)} %bitcast.38, f32[256]{0:T(256)S(1)} %select_reduce_fusion), kind=kOutput, calls=%fused_computation.18 | convolution fusion | flops 2015887360 | bytes 10880000 | tf_op jit(solution)/shard_map/dot_general | solution.py:516
  106.8 2.7 %collective-permute-done.14.far = bf16[128,5120]{1,0:T(8,128)(2,1)S(1)} collective-permute-done((bf16[128,5120]{1,0:T(8,128)(2,1)S(1)}, bf16[128,5120]{1,0:T(8,128)(2,1)S(1)}, u32[]{:S(2)}, u32[]{:S(2)}) %collective-permute-start.14) | collective-permute-done | bytes 1310752 | tf_op jit(solution)/shard_map/ppermute | solution.py:336
  110.2 1.8 collective-permute-start.20
  113.3 8.1 %collective-permute-done.20.refs_0_ = bf16[128,1536]{1,0:T(8,128)(2,1)S(1)} collective-permute-done((bf16[128,1536]{1,0:T(8,128)(2,1)S(1)}, bf16[128,1536]{1,0:T(8,128)(2,1)S(1)}, u32[]{:S(2)}, u32[]{:S(2)}) %collective-permute-start.20) | collective-permute-done | bytes 393248 | tf_op jit(solution)/shard_map/ppermute | solution.py:339
  125.0 8.5 %collective-permute-done.21.refs_1_ = bf16[64,3584]{1,0:T(8,128)(2,1)S(1)} collective-permute-done((bf16[64,3584]{1,0:T(8,128)(2,1)S(1)}, bf16[64,3584]{1,0:T(8,128)(2,1)S(1)}, u32[]{:S(2)}, u32[]{:S(2)}) %collective-permute-start.21) | collective-permute-done | bytes 458784 | tf_op jit(solution)/shard_map/ppermute | solution.py:333
  133.8 6.3 %collective-permute-start.22 = (bf16[64,3584]{1,0:T(8,128)(2,1)S(1)}, bf16[64,3584]{1,0:T(8,128)(2,1)S(1)}, u32[]{:S(2)}, u32[]{:S(2)}) collective-permute-start(bf16[64,3584]{1,0:T(8,128)(2,1)S(1)} %shard_map.113), channel_id=1, source_target_pairs={{0,12},{1,13},{2,14},{3,15},{4,0},{5,1},{6,2},{7,3},{8,4},{9,5},{1... | collective-permute-start | bytes 1376264 | tf_op jit(solution)/shard_map/ppermute | solution.py:330
  143.6 7.1 %collective-permute-done.19.refs_0_ = bf16[128,1536]{1,0:T(8,128)(2,1)S(1)} collective-permute-done((bf16[128,1536]{1,0:T(8,128)(2,1)S(1)}, bf16[128,1536]{1,0:T(8,128)(2,1)S(1)}, u32[]{:S(2)}, u32[]{:S(2)}) %collective-permute-start.19) | collective-permute-done | bytes 393248 | tf_op jit(solution)/shard_map/ppermute | solution.py:339
  151.3 1.8 collective-permute-start.23
  156.6 6.2 %collective-permute-done.16.refs_0_ = bf16[128,1536]{1,0:T(8,128)(2,1)S(1)} collective-permute-done((bf16[128,1536]{1,0:T(8,128)(2,1)S(1)}, bf16[128,1536]{1,0:T(8,128)(2,1)S(1)}, u32[]{:S(2)}, u32[]{:S(2)}) %collective-permute-start.16) | collective-permute-done | bytes 393248 | tf_op jit(solution)/shard_map/ppermute | solution.py:339
  164.7 8.1 %collective-permute-done.24.refs_1_ = bf16[64,3584]{1,0:T(8,128)(2,1)S(1)} collective-permute-done((bf16[64,3584]{1,0:T(8,128)(2,1)S(1)}, bf16[64,3584]{1,0:T(8,128)(2,1)S(1)}, u32[]{:S(2)}, u32[]{:S(2)}) %collective-permute-start.24) | collective-permute-done | bytes 458784 | tf_op jit(solution)/shard_map/ppermute | solution.py:333
  173.2 1.8 collective-permute-done.26
  176.8 3.3 %collective-permute-done.27 = bf16[64,1024]{1,0:T(8,128)(2,1)S(1)} collective-permute-done((bf16[64,1024]{1,0:T(8,128)(2,1)S(1)}, bf16[64,1024]{1,0:T(8,128)(2,1)S(1)}, u32[]{:S(2)}, u32[]{:S(2)}) %collective-permute-start.27) | collective-permute-done | bytes 131104 | tf_op jit(solution)/shard_map/ppermute | solution.py:339
  (103 shorter events, 40.9 us)
Async XLA Ops:
  4.0 35.0 %copy-start.6 = (bf16[64,3328]{1,0:T(8,128)(2,1)}, bf16[64,3328]{1,0:T(8,128)(2,1)S(1)}, u32[]{:S(2)}) copy-start(bf16[64,3328]{1,0:T(8,128)(2,1)S(1)} %get-tuple-element.48.refs_6_) | copy-start | bytes 1277956
  6.1 43.3 %copy-start = (bf16[512,512]{1,0:T(8,128)(2,1)S(1)}, bf16[512,512]{1,0:T(8,128)(2,1)}, u32[]{:S(2)}) copy-start(bf16[512,512]{1,0:T(8,128)(2,1)} %k) | copy-start | bytes 1572868
  6.1 43.3 %copy-start.1 = (bf16[512,512]{1,0:T(8,128)(2,1)S(1)}, bf16[512,512]{1,0:T(8,128)(2,1)}, u32[]{:S(2)}) copy-start(bf16[512,512]{1,0:T(8,128)(2,1)} %v.1) | copy-start | bytes 1572868
  6.1 43.3 %copy-start.3 = (bf16[512,512]{1,0:T(8,128)(2,1)S(1)}, bf16[512,512]{1,0:T(8,128)(2,1)}, u32[]{:S(2)}) copy-start(bf16[512,512]{1,0:T(8,128)(2,1)} %q.1) | copy-start | bytes 1572868
  6.2 30.2 %collective-permute-start.6 = (bf16[512,1152]{1,0:T(8,128)(2,1)S(1)}, bf16[512,1152]{1,0:T(8,128)(2,1)S(1)}, u32[]{:S(2)}, u32[]{:S(2)}) collective-permute-start(bf16[512,1152]{1,0:T(8,128)(2,1)S(1)} %pad_maximum_fusion), channel_id=1, source_target_pairs={{0,16},{1,17},{2,18},{3,19},{4,20},{5,21},{6,22},{7,23},{8,24},{9,... | collective-permute-start | bytes 3538952 | tf_op jit(solution)/shard_map/ppermute | solution.py:480
  11.2 11.3 %collective-permute-start.3 = (bf16[64,3328]{1,0:T(8,128)(2,1)S(1)}, bf16[64,3328]{1,0:T(8,128)(2,1)S(1)}, u32[]{:S(2)}, u32[]{:S(2)}) collective-permute-start(bf16[64,3328]{1,0:T(8,128)(2,1)S(1)} %get-tuple-element.48.refs_6_), channel_id=1, source_target_pairs={{0,2},{1,3},{2,0},{3,1},{4,6},{5,7},{6,4},{7,5},{8,10},{9,11},{10,... | collective-permute-start | bytes 1277960 | tf_op jit(solution)/shard_map/ppermute | solution.py:333
  12.8 14.6 %collective-permute-start = (bf16[64,3328]{1,0:T(8,128)(2,1)S(1)}, bf16[64,3328]{1,0:T(8,128)(2,1)S(1)}, u32[]{:S(2)}, u32[]{:S(2)}) collective-permute-start(bf16[64,3328]{1,0:T(8,128)(2,1)S(1)} %get-tuple-element.48.refs_6_), channel_id=1, source_target_pairs={{0,4},{1,5},{2,6},{3,7},{4,8},{5,9},{6,10},{7,11},{8,12},{9,13},{1... | collective-permute-start | bytes 1277960 | tf_op jit(solution)/shard_map/ppermute | solution.py:330
  14.4 20.9 %collective-permute-start.2 = (bf16[64,3328]{1,0:T(8,128)(2,1)S(1)}, bf16[64,3328]{1,0:T(8,128)(2,1)S(1)}, u32[]{:S(2)}, u32[]{:S(2)}) collective-permute-start(bf16[64,3328]{1,0:T(8,128)(2,1)S(1)} %get-tuple-element.48.refs_6_), channel_id=1, source_target_pairs={{0,12},{1,13},{2,14},{3,15},{4,0},{5,1},{6,2},{7,3},{8,4},{9,5},{1... | collective-permute-start | bytes 1277960 | tf_op jit(solution)/shard_map/ppermute | solution.py:330
  27.4 8.4 %collective-permute-start.4 = (bf16[64,3328]{1,0:T(8,128)(2,1)S(1)}, bf16[64,3328]{1,0:T(8,128)(2,1)S(1)}, u32[]{:S(2)}, u32[]{:S(2)}) collective-permute-start(bf16[64,3328]{1,0:T(8,128)(2,1)S(1)} %collective-permute-done.refs_2_), channel_id=1, source_target_pairs={{0,2},{1,3},{2,0},{3,1},{4,6},{5,7},{6,4},{7,5},{8,10},{9,11},{10,... | collective-permute-start | bytes 1277960 | tf_op jit(solution)/shard_map/ppermute | solution.py:333
  27.9 16.1 %collective-permute-start.1 = (bf16[64,3328]{1,0:T(8,128)(2,1)S(1)}, bf16[64,3328]{1,0:T(8,128)(2,1)S(1)}, u32[]{:S(2)}, u32[]{:S(2)}) collective-permute-start(bf16[64,3328]{1,0:T(8,128)(2,1)S(1)} %collective-permute-done.refs_2_), channel_id=1, source_target_pairs={{0,4},{1,5},{2,6},{3,7},{4,8},{5,9},{6,10},{7,11},{8,12},{9,13},{1... | collective-permute-start | bytes 1277960 | tf_op jit(solution)/shard_map/ppermute | solution.py:330
  35.8 9.8 %collective-permute-start.5 = (bf16[64,3328]{1,0:T(8,128)(2,1)S(1)}, bf16[64,3328]{1,0:T(8,128)(2,1)S(1)}, u32[]{:S(2)}, u32[]{:S(2)}) collective-permute-start(bf16[64,3328]{1,0:T(8,128)(2,1)S(1)} %collective-permute-done.2.refs_4_), channel_id=1, source_target_pairs={{0,2},{1,3},{2,0},{3,1},{4,6},{5,7},{6,4},{7,5},{8,10},{9,11},{10,... | collective-permute-start | bytes 1277960 | tf_op jit(solution)/shard_map/ppermute | solution.py:333
  36.4 9.4 %collective-permute-start.7 = (bf16[64,1920]{1,0:T(8,128)(2,1)S(1)}, bf16[64,1920]{1,0:T(8,128)(2,1)S(1)}, u32[]{:S(2)}, u32[]{:S(2)}) collective-permute-start(bf16[64,1920]{1,0:T(8,128)(2,1)S(1)} %slice.52), channel_id=1, source_target_pairs={{0,16},{16,0},{1,17},{17,1},{2,18},{18,2},{3,19},{19,3},{4,20},{20... | collective-permute-start | bytes 737288 | tf_op jit(solution)/shard_map/ppermute | solution.py:339
  39.0 18.1 %collective-permute-start.10 = (bf16[128,1920]{1,0:T(8,128)(2,1)S(1)}, bf16[128,1920]{1,0:T(8,128)(2,1)S(1)}, u32[]{:S(2)}, u32[]{:S(2)}) collective-permute-start(bf16[128,1920]{1,0:T(8,128)(2,1)S(1)} %pad_maximum_fusion.2), channel_id=1, source_target_pairs={{0,16},{16,0},{1,17},{17,1},{2,18},{18,2},{3,19},{19,3},{4,20},{20... | collective-permute-start | bytes 1474568 | tf_op jit(solution)/shard_map/ppermute | solution.py:339
  45.9 21.0 %collective-permute-start.9 = (bf16[128,1920]{1,0:T(8,128)(2,1)S(1)}, bf16[128,1920]{1,0:T(8,128)(2,1)S(1)}, u32[]{:S(2)}, u32[]{:S(2)}) collective-permute-start(bf16[128,1920]{1,0:T(8,128)(2,1)S(1)} %pad_maximum_fusion.1), channel_id=1, source_target_pairs={{0,16},{16,0},{1,17},{17,1},{2,18},{18,2},{3,19},{19,3},{4,20},{20... | collective-permute-start | bytes 1474568 | tf_op jit(solution)/shard_map/ppermute | solution.py:339
  47.9 11.1 %collective-permute-start.8 = (bf16[64,3328]{1,0:T(8,128)(2,1)S(1)}, bf16[64,3328]{1,0:T(8,128)(2,1)S(1)}, u32[]{:S(2)}, u32[]{:S(2)}) collective-permute-start(bf16[64,3328]{1,0:T(8,128)(2,1)S(1)} %collective-permute-done.1.refs_0_), channel_id=1, source_target_pairs={{0,2},{1,3},{2,0},{3,1},{4,6},{5,7},{6,4},{7,5},{8,10},{9,11},{10,... | collective-permute-start | bytes 1277960 | tf_op jit(solution)/shard_map/ppermute | solution.py:333
  57.9 14.4 %collective-permute-start.11 = (bf16[64,1920]{1,0:T(8,128)(2,1)}, bf16[64,1920]{1,0:T(8,128)(2,1)}, u32[]{:S(2)}, u32[]{:S(2)}) collective-permute-start(bf16[64,1920]{1,0:T(8,128)(2,1)} %slice.57), channel_id=1, source_target_pairs={{0,16},{16,0},{1,17},{17,1},{2,18},{18,2},{3,19},{19,3},{4,20},{20... | collective-permute-start | bytes 737288 | tf_op jit(solution)/shard_map/ppermute | solution.py:339
  68.3 7.4 %collective-permute-start.12 = (bf16[64,1920]{1,0:T(8,128)(2,1)}, bf16[64,1920]{1,0:T(8,128)(2,1)}, u32[]{:S(2)}, u32[]{:S(2)}) collective-permute-start(bf16[64,1920]{1,0:T(8,128)(2,1)} %slice.58), channel_id=1, source_target_pairs={{0,16},{16,0},{1,17},{17,1},{2,18},{18,2},{3,19},{19,3},{4,20},{20... | collective-permute-start | bytes 737288 | tf_op jit(solution)/shard_map/ppermute | solution.py:339
  86.2 12.6 %collective-permute-start.13 = (bf16[256,5248]{1,0:T(8,128)(2,1)S(1)}, bf16[256,5248]{1,0:T(8,128)(2,1)S(1)}, u32[]{:S(2)}, u32[]{:S(2)}) collective-permute-start(bf16[256,5248]{1,0:T(8,128)(2,1)S(1)} %get-tuple-element.73), channel_id=1, source_target_pairs={{0,1},{1,0},{2,3},{3,2},{4,5},{5,4},{6,7},{7,6},{8,9},{9,8},{10,11... | collective-permute-start | bytes 8060936 | tf_op jit(solution)/shard_map/ppermute | solution.py:336
  106.2 3.2 %collective-permute-start.14 = (bf16[128,5120]{1,0:T(8,128)(2,1)S(1)}, bf16[128,5120]{1,0:T(8,128)(2,1)S(1)}, u32[]{:S(2)}, u32[]{:S(2)}) collective-permute-start(bf16[128,5120]{1,0:T(8,128)(2,1)S(1)} %get-tuple-element.97), channel_id=1, source_target_pairs={{0,1},{1,0},{2,3},{3,2},{4,5},{5,4},{6,7},{7,6},{8,9},{9,8},{10,11... | collective-permute-start | bytes 3932168 | tf_op jit(solution)/shard_map/ppermute | solution.py:336
  109.4 3.0 %collective-permute-start.15 = (bf16[128,5120]{1,0:T(8,128)(2,1)S(1)}, bf16[128,5120]{1,0:T(8,128)(2,1)S(1)}, u32[]{:S(2)}, u32[]{:S(2)}) collective-permute-start(bf16[128,5120]{1,0:T(8,128)(2,1)S(1)} %get-tuple-element.83), channel_id=1, source_target_pairs={{0,1},{1,0},{2,3},{3,2},{4,5},{5,4},{6,7},{7,6},{8,9},{9,8},{10,11... | collective-permute-start | bytes 3932168 | tf_op jit(solution)/shard_map/ppermute | solution.py:336
  110.2 11.2 %collective-permute-start.20 = (bf16[128,1536]{1,0:T(8,128)(2,1)S(1)}, bf16[128,1536]{1,0:T(8,128)(2,1)S(1)}, u32[]{:S(2)}, u32[]{:S(2)}) collective-permute-start(bf16[128,1536]{1,0:T(8,128)(2,1)S(1)} %shard_map.107), channel_id=1, source_target_pairs={{0,16},{16,0},{1,17},{17,1},{2,18},{18,2},{3,19},{19,3},{4,20},{20... | collective-permute-start | bytes 1179656 | tf_op jit(solution)/shard_map/ppermute | solution.py:339
  121.7 11.8 %collective-permute-start.21 = (bf16[64,3584]{1,0:T(8,128)(2,1)S(1)}, bf16[64,3584]{1,0:T(8,128)(2,1)S(1)}, u32[]{:S(2)}, u32[]{:S(2)}) collective-permute-start(bf16[64,3584]{1,0:T(8,128)(2,1)S(1)} %shard_map.112), channel_id=1, source_target_pairs={{0,2},{1,3},{2,0},{3,1},{4,6},{5,7},{6,4},{7,5},{8,10},{9,11},{10,... | collective-permute-start | bytes 1376264 | tf_op jit(solution)/shard_map/ppermute | solution.py:333
  123.3 16.8 %collective-permute-start.17 = (bf16[128,1536]{1,0:T(8,128)(2,1)S(1)}, bf16[128,1536]{1,0:T(8,128)(2,1)S(1)}, u32[]{:S(2)}, u32[]{:S(2)}) collective-permute-start(bf16[128,1536]{1,0:T(8,128)(2,1)S(1)} %shard_map.108), channel_id=1, source_target_pairs={{0,16},{16,0},{1,17},{17,1},{2,18},{18,2},{3,19},{19,3},{4,20},{20... | collective-permute-start | bytes 1179656 | tf_op jit(solution)/shard_map/ppermute | solution.py:339
  133.8 17.0 %collective-permute-start.22 = (bf16[64,3584]{1,0:T(8,128)(2,1)S(1)}, bf16[64,3584]{1,0:T(8,128)(2,1)S(1)}, u32[]{:S(2)}, u32[]{:S(2)}) collective-permute-start(bf16[64,3584]{1,0:T(8,128)(2,1)S(1)} %shard_map.113), channel_id=1, source_target_pairs={{0,12},{1,13},{2,14},{3,15},{4,0},{5,1},{6,2},{7,3},{8,4},{9,5},{1... | collective-permute-start | bytes 1376264 | tf_op jit(solution)/shard_map/ppermute | solution.py:330
  140.3 10.6 %collective-permute-start.18 = (bf16[64,3584]{1,0:T(8,128)(2,1)S(1)}, bf16[64,3584]{1,0:T(8,128)(2,1)S(1)}, u32[]{:S(2)}, u32[]{:S(2)}) collective-permute-start(bf16[64,3584]{1,0:T(8,128)(2,1)S(1)} %shard_map.111), channel_id=1, source_target_pairs={{0,2},{1,3},{2,0},{3,1},{4,6},{5,7},{6,4},{7,5},{8,10},{9,11},{10,... | collective-permute-start | bytes 1376264 | tf_op jit(solution)/shard_map/ppermute | solution.py:333
  141.9 8.8 %collective-permute-start.19 = (bf16[128,1536]{1,0:T(8,128)(2,1)S(1)}, bf16[128,1536]{1,0:T(8,128)(2,1)S(1)}, u32[]{:S(2)}, u32[]{:S(2)}) collective-permute-start(bf16[128,1536]{1,0:T(8,128)(2,1)S(1)} %shard_map.109), channel_id=1, source_target_pairs={{0,16},{16,0},{1,17},{17,1},{2,18},{18,2},{3,19},{19,3},{4,20},{20... | collective-permute-start | bytes 1179656 | tf_op jit(solution)/shard_map/ppermute | solution.py:339
  151.3 11.5 %collective-permute-start.23 = (bf16[64,3584]{1,0:T(8,128)(2,1)S(1)}, bf16[64,3584]{1,0:T(8,128)(2,1)S(1)}, u32[]{:S(2)}, u32[]{:S(2)}) collective-permute-start(bf16[64,3584]{1,0:T(8,128)(2,1)S(1)} %shard_map.114), channel_id=1, source_target_pairs={{0,12},{1,13},{2,14},{3,15},{4,0},{5,1},{6,2},{7,3},{8,4},{9,5},{1... | collective-permute-start | bytes 1376264 | tf_op jit(solution)/shard_map/ppermute | solution.py:330
  153.4 11.0 %collective-permute-start.25 = (bf16[64,3584]{1,0:T(8,128)(2,1)S(1)}, bf16[64,3584]{1,0:T(8,128)(2,1)S(1)}, u32[]{:S(2)}, u32[]{:S(2)}) collective-permute-start(bf16[64,3584]{1,0:T(8,128)(2,1)S(1)} %shard_map.117), channel_id=1, source_target_pairs={{0,2},{1,3},{2,0},{3,1},{4,6},{5,7},{6,4},{7,5},{8,10},{9,11},{10,... | collective-permute-start | bytes 1376264 | tf_op jit(solution)/shard_map/ppermute | solution.py:333
  154.9 7.9 %collective-permute-start.16 = (bf16[128,1536]{1,0:T(8,128)(2,1)S(1)}, bf16[128,1536]{1,0:T(8,128)(2,1)S(1)}, u32[]{:S(2)}, u32[]{:S(2)}) collective-permute-start(bf16[128,1536]{1,0:T(8,128)(2,1)S(1)} %shard_map.110), channel_id=1, source_target_pairs={{0,16},{16,0},{1,17},{17,1},{2,18},{18,2},{3,19},{19,3},{4,20},{20... | collective-permute-start | bytes 1179656 | tf_op jit(solution)/shard_map/ppermute | solution.py:339
  163.1 9.8 %collective-permute-start.24 = (bf16[64,3584]{1,0:T(8,128)(2,1)S(1)}, bf16[64,3584]{1,0:T(8,128)(2,1)S(1)}, u32[]{:S(2)}, u32[]{:S(2)}) collective-permute-start(bf16[64,3584]{1,0:T(8,128)(2,1)S(1)} %shard_map.115), channel_id=1, source_target_pairs={{0,2},{1,3},{2,0},{3,1},{4,6},{5,7},{6,4},{7,5},{8,10},{9,11},{10,... | collective-permute-start | bytes 1376264 | tf_op jit(solution)/shard_map/ppermute | solution.py:333
  164.6 10.3 %collective-permute-start.26 = (bf16[64,3584]{1,0:T(8,128)(2,1)S(1)}, bf16[64,3584]{1,0:T(8,128)(2,1)S(1)}, u32[]{:S(2)}, u32[]{:S(2)}) collective-permute-start(bf16[64,3584]{1,0:T(8,128)(2,1)S(1)} %shard_map.118), channel_id=1, source_target_pairs={{0,4},{1,5},{2,6},{3,7},{4,8},{5,9},{6,10},{7,11},{8,12},{9,13},{1... | collective-permute-start | bytes 1376264 | tf_op jit(solution)/shard_map/ppermute | solution.py:330
  175.1 5.0 %collective-permute-start.27 = (bf16[64,1024]{1,0:T(8,128)(2,1)S(1)}, bf16[64,1024]{1,0:T(8,128)(2,1)S(1)}, u32[]{:S(2)}, u32[]{:S(2)}) collective-permute-start(bf16[64,1024]{1,0:T(8,128)(2,1)S(1)} %slice.72), channel_id=1, source_target_pairs={{0,16},{16,0},{1,17},{17,1},{2,18},{18,2},{3,19},{19,3},{4,20},{20... | collective-permute-start | bytes 393224 | tf_op jit(solution)/shard_map/ppermute | solution.py:339
  (13 other events, 39.8 us)

commit v4 on v3

--- a/solution.py
+++ b/solution.py
@@ -53,7 +53,7 @@
     )
     return (summed / total[:, :, None]).reshape(rows, heads * HD).astype(BF16)
 
-SHARED = 1280
+SHARED = 2560
 OVER_X = 1536
 ORDER = [2, 1, 3, 0]
 
@@ -471,9 +471,12 @@
         block, theirs = prepare(tokens, expert_ids, route_weight, at_x, n_exp)
         cut = lambda a: a[:, SHARED : SHARED + split]
         both = lambda d: jnp.concatenate([cut(line[d]), cut(across[d])], axis=0)
-        line = {0: block, 1: z_shift(block, 1), 3: z_shift(block, -1)}
-        line[2] = z_shift(line[1], 1)
+        line = {0: block, 1: z_shift(block, 1)}
         across = {0: y_swap(block)}
+        line[1], again = after((line[1], block))
+        line[3] = z_shift(again, -1)
+        line[3], again = after((line[3], line[1]))
+        line[2] = z_shift(again, 1)
         block, segment_ids, k_input = after((block, segment_ids, k_input))
         docs = segment_ids[:, None] == jnp.arange(LANES, dtype=jnp.int32)
         docs = docs.astype(BF16)
@@ -537,7 +540,10 @@
         def over_y(i):
             return y_swap(sums(2 * i + 1, 1, False, [(got_x[i], 1)]))
 
-        got_y = [over_y(0), over_y(1)]
+        got_y = [over_y(0)]
+        turn = sums(3, 1, False, [(got_x[1], 1)])
+        got_y[0], turn = after((got_y[0], turn))
+        got_y.append(y_swap(turn))
         part = sums(0, 1, False, [(got_x[0], 0), (got_y[0], 0)])
         part = z_shift(part, -1)
         got_x[2], part = after((got_x[2], part))

time: 181 us -> 172 us (0.950)
  starting transfers between devices: 44.2 us -> 34.2 us
    ppermute x8, waiting for transfers between devices: 25.5 us -> 12.4 us  [y_swap(): return lax.ppermute(x, 'exp', pairs(lambda z, y, c: (z, 1 - y, c)))]
    ppermute x10, waiting for transfers between devices: 38 us -> 45 us  [x_swap(): return lax.ppermute(x, 'ctx', [(0, 1), (1, 0)])]
    ppermute x10, starting transfers between devices: 16.6 us -> 12.2 us  [x_swap(): return lax.ppermute(x, 'ctx', [(0, 1), (1, 0)])]
    ppermute x6, starting transfers between devices: 12.1 us -> 8.49 us  [z_shift(): return lax.ppermute(x, 'exp', pairs(lambda z, y, c: (z + d, y, c)))]
    ppermute x6, waiting for transfers between devices: 18.8 us -> 21.9 us  [z_shift(): return lax.ppermute(x, 'exp', pairs(lambda z, y, c: (z + d, y, c)))]
    ppermute x1, waiting for transfers between devices: 0.01 us -> 2.25 us  [pair_device(): lax.ppermute(jnp.concatenate([k_input, v_input, docs], axis=1), 'ctx', [(...]
    unnamed x34 -> x38, local copies, waits for them, and re-layouts: 9.97 us -> 10.1 us
  transfers between devices with their start and end apart: 28 -> 28, of which waited for: 21 -> 20; matrix products, arithmetic and copies ran while one was open for 7% -> 8% of each run, Pallas kernels for 6% -> 6%
where the time goes in v4:
time: 172 us; the launch traced here: 171 us
  waiting for transfers between devices  84.9 us (49%)
  starting transfers between devices  34.2 us (20%)
  Pallas kernels  18.5 us (11%)
  matrix products  16.9 us (10%)
  local copies, waits for them, and re-layouts  11.8 us (7%)
  other arithmetic  3.92 us (2%)
    ppermute x10, waiting for transfers between devices, x_swap(): return lax.ppermute(x, 'ctx', [(0, 1), (1, 0)])  45 us
    ppermute x6, waiting for transfers between devices, z_shift(): return lax.ppermute(x, 'exp', pairs(lambda z, y, c: (z + d, y, c)))  21.9 us
    ppermute x8, waiting for transfers between devices, y_swap(): return lax.ppermute(x, 'exp', pairs(lambda z, y, c: (z, 1 - y, c)))  12.4 us
    ppermute x10, starting transfers between devices, x_swap(): return lax.ppermute(x, 'ctx', [(0, 1), (1, 0)])  12.2 us
    unnamed x38, local copies, waits for them, and re-layouts  10.1 us
    ppermute x8, starting transfers between devices, y_swap(): return lax.ppermute(x, 'exp', pairs(lambda z, y, c: (z, 1 - y, c)))  9.02 us
    ppermute x6, starting transfers between devices, z_shift(): return lax.ppermute(x, 'exp', pairs(lambda z, y, c: (z + d, y, c)))  8.49 us
    dot_general x2, matrix products, expert(): up = jnp.dot(block, w_in[0, 1], preferred_element_type=F32)  7.79 us
  transfers between devices with their start and end apart: 28, of which 20 were waited for; matrix products, arithmetic and copies ran while one was open for 8% of the time, Pallas kernels for 6%

profile of v4, /device:TPU:0, one launch (start us, length us, event | category | flops | bytes accessed | tf_op | source)
XLA Modules:
  0.0 171.2 jit_solution(11672123200099972077)
XLA Ops:
  4.0 3.0 %collective-permute-start.3 = (bf16[64,3968]{1,0:T(8,128)(2,1)S(1)}, bf16[64,3968]{1,0:T(8,128)(2,1)S(1)}, u32[]{:S(2)}, u32[]{:S(2)}) collective-permute-start(bf16[64,3968]{1,0:T(8,128)(2,1)S(1)} %get-tuple-element.55.refs_6_), channel_id=1, source_target_pairs={{0,2},{1,3},{2,0},{3,1},{4,6},{5,7},{6,4},{7,5},{8,10},{9,11},{10,... | collective-permute-start | bytes 1523720 | tf_op jit(solution)/shard_map/ppermute | solution.py:333
  10.8 3.5 %collective-permute-start.6 = (bf16[512,1152]{1,0:T(8,128)(2,1)S(1)}, bf16[512,1152]{1,0:T(8,128)(2,1)S(1)}, u32[]{:S(2)}, u32[]{:S(2)}) collective-permute-start(bf16[512,1152]{1,0:T(8,128)(2,1)S(1)} %pad_maximum_fusion), channel_id=1, source_target_pairs={{0,16},{1,17},{2,18},{3,19},{4,20},{5,21},{6,22},{7,23},{8,24},{9,... | collective-permute-start | bytes 3538952 | tf_op jit(solution)/shard_map/ppermute | solution.py:483
  14.3 7.6 %collective-permute-done.refs_2_ = bf16[64,3968]{1,0:T(8,128)(2,1)S(1)} collective-permute-done((bf16[64,3968]{1,0:T(8,128)(2,1)S(1)}, bf16[64,3968]{1,0:T(8,128)(2,1)S(1)}, u32[]{:S(2)}, u32[]{:S(2)}) %collective-permute-start) | collective-permute-done | bytes 507936 | tf_op jit(solution)/shard_map/ppermute | solution.py:330
  21.8 1.7 %collective-permute-start.1 = (bf16[64,3968]{1,0:T(8,128)(2,1)S(1)}, bf16[64,3968]{1,0:T(8,128)(2,1)S(1)}, u32[]{:S(2)}, u32[]{:S(2)}) collective-permute-start(bf16[64,3968]{1,0:T(8,128)(2,1)S(1)} %get-tuple-element.55.refs_6_), channel_id=1, source_target_pairs={{0,12},{1,13},{2,14},{3,15},{4,0},{5,1},{6,2},{7,3},{8,4},{9,5},{1... | collective-permute-start | bytes 1523720 | tf_op jit(solution)/shard_map/ppermute | solution.py:330
  24.1 9.9 %collective-permute-done.1.refs_4_ = bf16[64,3968]{1,0:T(8,128)(2,1)S(1)} collective-permute-done((bf16[64,3968]{1,0:T(8,128)(2,1)S(1)}, bf16[64,3968]{1,0:T(8,128)(2,1)S(1)}, u32[]{:S(2)}, u32[]{:S(2)}) %collective-permute-start.1) | collective-permute-done | bytes 507936 | tf_op jit(solution)/shard_map/ppermute | solution.py:330
  36.6 2.2 %collective-permute-done.6.past_k.past_v.past_docs = bf16[512,1152]{1,0:T(8,128)(2,1)S(1)} collective-permute-done((bf16[512,1152]{1,0:T(8,128)(2,1)S(1)}, bf16[512,1152]{1,0:T(8,128)(2,1)S(1)}, u32[]{:S(2)}, u32[]{:S(2)}) %collective-permute-start.6) | collective-permute-done | bytes 1179680 | tf_op jit(solution)/shard_map/ppermute | solution.py:483
  38.9 2.5 %collective-permute-start.7 = (bf16[64,1280]{1,0:T(8,128)(2,1)S(1)}, bf16[64,1280]{1,0:T(8,128)(2,1)S(1)}, u32[]{:S(2)}, u32[]{:S(2)}) collective-permute-start(bf16[64,1280]{1,0:T(8,128)(2,1)S(1)} %slice.52), channel_id=1, source_target_pairs={{0,16},{16,0},{1,17},{17,1},{2,18},{18,2},{3,19},{19,3},{4,20},{20... | collective-permute-start | bytes 491528 | tf_op jit(solution)/shard_map/ppermute | solution.py:339
  41.5 5.0 %collective-permute-done.7.refs_13_ = bf16[64,1280]{1,0:T(8,128)(2,1)S(1)} collective-permute-done((bf16[64,1280]{1,0:T(8,128)(2,1)S(1)}, bf16[64,1280]{1,0:T(8,128)(2,1)S(1)}, u32[]{:S(2)}, u32[]{:S(2)}) %collective-permute-start.7) | collective-permute-done | bytes 163872 | tf_op jit(solution)/shard_map/ppermute | solution.py:339
  46.5 1.9 %collective-permute-done.2.refs_0_ = bf16[64,3968]{1,0:T(8,128)(2,1)S(1)} collective-permute-done((bf16[64,3968]{1,0:T(8,128)(2,1)S(1)}, bf16[64,3968]{1,0:T(8,128)(2,1)S(1)}, u32[]{:S(2)}, u32[]{:S(2)}) %collective-permute-start.2) | collective-permute-done | bytes 507936 | tf_op jit(solution)/shard_map/ppermute | solution.py:330
  48.4 1.6 collective-permute-start.8
  51.6 7.7 %shard_map.105 = bf16[512,512]{1,0:T(8,128)(2,1)} custom-call(s32[1]{0:T(128)} %bitcast.x_ref, bf16[512,512]{1,0:T(8,128)(2,1)S(1)} %copy-done.3, bf16[512,512]{1,0:T(8,128)(2,1)S(1)} %copy-done, bf16[512,512]{1,0:T(8,128)(2,1)S(1)} %copy-done.1, bf16[512,128]{1,0:T(8,128)(2,1)S(1)} %fusion.31.docs, ...), custom_call_target="tpu_custom_call" | custom-call | flops 1073741824 | bytes 3670016 | tf_op jit(solution)/shard_map/pallas_call | solution.py:287
  62.9 2.7 %collective-permute-done.11.refs_8_ = bf16[64,1280]{1,0:T(8,128)(2,1)} collective-permute-done((bf16[64,1280]{1,0:T(8,128)(2,1)}, bf16[64,1280]{1,0:T(8,128)(2,1)}, u32[]{:S(2)}, u32[]{:S(2)}) %collective-permute-start.11) | collective-permute-done | bytes 163872 | tf_op jit(solution)/shard_map/ppermute | solution.py:339
  65.6 1.8 %collective-permute-done.12.refs_9_ = bf16[64,1280]{1,0:T(8,128)(2,1)} collective-permute-done((bf16[64,1280]{1,0:T(8,128)(2,1)}, bf16[64,1280]{1,0:T(8,128)(2,1)}, u32[]{:S(2)}, u32[]{:S(2)}) %collective-permute-start.12) | collective-permute-done | bytes 163872 | tf_op jit(solution)/shard_map/ppermute | solution.py:339
  72.2 6.9 %shard_map.106 = (bf16[256,5120]{1,0:T(8,128)(2,1)S(1)}, bf16[256,128]{1,0:T(8,128)(2,1)S(1)}, bf16[256,5248]{1,0:T(8,128)(2,1)S(1)}, bf16[8,64,64]{2,1,0:T(8,128)(2,1)S(1)}) custom-call(s32[2]{0:T(128)S(1)} %pad_add_fusion.s_ref, bf16[64,3968]{1,0:T(8,128)(2,1)S(1)} %collective-permute-done.2.refs_0_, bf16[64,3968]{1,0:T(8,128)(2,1)S(1)} %collective-permute-done.8.refs_1_, ...), custom_call_target="tpu_custom_call" | custom-call | flops 335544320 | bytes 10485760 | tf_op jit(solution)/shard_map/pallas_call | solution.py:187
  79.2 5.6 %fusion.6 = f32[256,768]{1,0:T(8,128)S(1)} fusion(bf16[256,5120]{1,0:T(8,128)(2,1)S(1)} %get-tuple-element.77, bf16[1,2,5120,768]{3,2,1,0:T(8,128)(2,1)} %param.16), kind=kOutput, calls=%fused_computation.6 | convolution fusion | flops 2013265920 | bytes 11272192 | tf_op jit(solution)/shard_map/dot_general | solution.py:512
  84.8 2.1 %copy-done.16 = bf16[1,2,5120,768]{3,2,1,0:T(8,128)(2,1)S(1)} copy-done((bf16[1,2,5120,768]{3,2,1,0:T(8,128)(2,1)S(1)}, bf16[1,2,5120,768]{3,2,1,0:T(8,128)(2,1)}, u32[]{:S(2)}) %copy-start.16) | copy-done | bytes 15728664
  86.8 2.2 %fusion.10 = f32[256,768]{1,0:T(8,128)S(1)} fusion(bf16[256,5120]{1,0:T(8,128)(2,1)S(1)} %get-tuple-element.77, bf16[1,2,5120,768]{3,2,1,0:T(8,128)(2,1)S(1)} %copy-done.16), kind=kOutput, calls=%fused_computation.10 | convolution fusion | flops 2013265920 | bytes 11272192 | tf_op jit(solution)/shard_map/dot_general | solution.py:511
  89.4 2.2 %fusion.25.near = bf16[256,5120]{1,0:T(8,128)(2,1)S(1)} fusion(bf16[256,768]{1,0:T(8,128)(2,1)S(1)} %multiply_convert_fusion.1, bf16[1,768,5120]{2,1,0:T(8,128)(2,1)S(1)} %bitcast.38, f32[256]{0:T(256)S(1)} %select_reduce_fusion.1), kind=kOutput, calls=%fused_computation.19 | convolution fusion | flops 2015887360 | bytes 10880000 | tf_op jit(solution)/shard_map/dot_general | solution.py:519
  91.8 2.2 %fusion.4 = f32[256,768]{1,0:T(8,128)S(1)} fusion(bf16[1,2,5120,768]{3,2,1,0:T(8,128)(2,1)S(1)} %copy-done.16, bf16[256,5248]{1,0:T(8,128)(2,1)S(1)} %collective-permute-done.13), kind=kOutput, calls=%fused_computation.4 | convolution fusion | flops 2013265920 | bytes 11272192 | tf_op jit(solution)/shard_map/dot_general | solution.py:512
  94.0 2.2 %fusion.8 = f32[256,768]{1,0:T(8,128)S(1)} fusion(bf16[1,2,5120,768]{3,2,1,0:T(8,128)(2,1)S(1)} %copy-done.16, bf16[256,5248]{1,0:T(8,128)(2,1)S(1)} %collective-permute-done.13), kind=kOutput, calls=%fused_computation.8 | convolution fusion | flops 2013265920 | bytes 11272192 | tf_op jit(solution)/shard_map/dot_general | solution.py:511
  96.4 2.5 %fusion.22 = bf16[256,5120]{1,0:T(8,128)(2,1)S(1)} fusion(bf16[256,768]{1,0:T(8,128)(2,1)S(1)} %multiply_convert_fusion, bf16[1,768,5120]{2,1,0:T(8,128)(2,1)S(1)} %bitcast.38, f32[256]{0:T(256)S(1)} %select_reduce_fusion), kind=kOutput, calls=%fused_computation.18 | convolution fusion | flops 2015887360 | bytes 10880000 | tf_op jit(solution)/shard_map/dot_general | solution.py:519
  99.6 2.7 %collective-permute-done.14.far = bf16[128,5120]{1,0:T(8,128)(2,1)S(1)} collective-permute-done((bf16[128,5120]{1,0:T(8,128)(2,1)S(1)}, bf16[128,5120]{1,0:T(8,128)(2,1)S(1)}, u32[]{:S(2)}, u32[]{:S(2)}) %collective-permute-start.14) | collective-permute-done | bytes 1310752 | tf_op jit(solution)/shard_map/ppermute | solution.py:336
  106.1 8.1 %collective-permute-done.18.refs_0_ = bf16[128,1536]{1,0:T(8,128)(2,1)S(1)} collective-permute-done((bf16[128,1536]{1,0:T(8,128)(2,1)S(1)}, bf16[128,1536]{1,0:T(8,128)(2,1)S(1)}, u32[]{:S(2)}, u32[]{:S(2)}) %collective-permute-start.18) | collective-permute-done | bytes 393248 | tf_op jit(solution)/shard_map/ppermute | solution.py:339
  116.2 8.9 %collective-permute-done.17.refs_0_ = bf16[128,1536]{1,0:T(8,128)(2,1)S(1)} collective-permute-done((bf16[128,1536]{1,0:T(8,128)(2,1)S(1)}, bf16[128,1536]{1,0:T(8,128)(2,1)S(1)}, u32[]{:S(2)}, u32[]{:S(2)}) %collective-permute-start.17) | collective-permute-done | bytes 393248 | tf_op jit(solution)/shard_map/ppermute | solution.py:339
  126.6 2.4 %collective-permute-start.22 = (bf16[64,3584]{1,0:T(8,128)(2,1)S(1)}, bf16[64,3584]{1,0:T(8,128)(2,1)S(1)}, u32[]{:S(2)}, u32[]{:S(2)}) collective-permute-start(bf16[64,3584]{1,0:T(8,128)(2,1)S(1)} %shard_map.113), channel_id=1, source_target_pairs={{0,12},{1,13},{2,14},{3,15},{4,0},{5,1},{6,2},{7,3},{8,4},{9,5},{1... | collective-permute-start | bytes 1376264 | tf_op jit(solution)/shard_map/ppermute | solution.py:330
  131.1 7.6 %collective-permute-done.21.refs_0_ = bf16[128,1536]{1,0:T(8,128)(2,1)S(1)} collective-permute-done((bf16[128,1536]{1,0:T(8,128)(2,1)S(1)}, bf16[128,1536]{1,0:T(8,128)(2,1)S(1)}, u32[]{:S(2)}, u32[]{:S(2)}) %collective-permute-start.21) | collective-permute-done | bytes 393248 | tf_op jit(solution)/shard_map/ppermute | solution.py:339
  140.2 2.1 %collective-permute-start.23 = (bf16[64,3584]{1,0:T(8,128)(2,1)S(1)}, bf16[64,3584]{1,0:T(8,128)(2,1)S(1)}, u32[]{:S(2)}, u32[]{:S(2)}) collective-permute-start(bf16[64,3584]{1,0:T(8,128)(2,1)S(1)} %shard_map.114), channel_id=1, source_target_pairs={{0,12},{1,13},{2,14},{3,15},{4,0},{5,1},{6,2},{7,3},{8,4},{9,5},{1... | collective-permute-start | bytes 1376264 | tf_op jit(solution)/shard_map/ppermute | solution.py:330
  144.2 7.1 %collective-permute-done.16.refs_0_ = bf16[128,1536]{1,0:T(8,128)(2,1)S(1)} collective-permute-done((bf16[128,1536]{1,0:T(8,128)(2,1)S(1)}, bf16[128,1536]{1,0:T(8,128)(2,1)S(1)}, u32[]{:S(2)}, u32[]{:S(2)}) %collective-permute-start.16) | collective-permute-done | bytes 393248 | tf_op jit(solution)/shard_map/ppermute | solution.py:339
  151.5 1.7 %collective-permute-start.24 = (bf16[64,3584]{1,0:T(8,128)(2,1)S(1)}, bf16[64,3584]{1,0:T(8,128)(2,1)S(1)}, u32[]{:S(2)}, u32[]{:S(2)}) collective-permute-start(bf16[64,3584]{1,0:T(8,128)(2,1)S(1)} %shard_map.115), channel_id=1, source_target_pairs={{0,2},{1,3},{2,0},{3,1},{4,6},{5,7},{6,4},{7,5},{8,10},{9,11},{10,... | collective-permute-start | bytes 1376264 | tf_op jit(solution)/shard_map/ppermute | solution.py:333
  155.0 7.4 %collective-permute-done.24.refs_1_ = bf16[64,3584]{1,0:T(8,128)(2,1)S(1)} collective-permute-done((bf16[64,3584]{1,0:T(8,128)(2,1)S(1)}, bf16[64,3584]{1,0:T(8,128)(2,1)S(1)}, u32[]{:S(2)}, u32[]{:S(2)}) %collective-permute-start.24) | collective-permute-done | bytes 458784 | tf_op jit(solution)/shard_map/ppermute | solution.py:333
  162.7 2.5 %collective-permute-done.26 = bf16[64,3584]{1,0:T(8,128)(2,1)S(1)} collective-permute-done((bf16[64,3584]{1,0:T(8,128)(2,1)S(1)}, bf16[64,3584]{1,0:T(8,128)(2,1)S(1)}, u32[]{:S(2)}, u32[]{:S(2)}) %collective-permute-start.26) | collective-permute-done | bytes 458784 | tf_op jit(solution)/shard_map/ppermute | solution.py:330
  166.6 3.8 %collective-permute-done.27 = bf16[64,1024]{1,0:T(8,128)(2,1)S(1)} collective-permute-done((bf16[64,1024]{1,0:T(8,128)(2,1)S(1)}, bf16[64,1024]{1,0:T(8,128)(2,1)S(1)}, u32[]{:S(2)}, u32[]{:S(2)}) %collective-permute-start.27) | collective-permute-done | bytes 131104 | tf_op jit(solution)/shard_map/ppermute | solution.py:339
  (107 shorter events, 38.9 us)
Async XLA Ops:
  4.0 46.0 %copy-start.4 = (bf16[64,3968]{1,0:T(8,128)(2,1)}, bf16[64,3968]{1,0:T(8,128)(2,1)S(1)}, u32[]{:S(2)}) copy-start(bf16[64,3968]{1,0:T(8,128)(2,1)S(1)} %get-tuple-element.55.refs_6_) | copy-start | bytes 1523716
  4.0 19.6 %collective-permute-start.3 = (bf16[64,3968]{1,0:T(8,128)(2,1)S(1)}, bf16[64,3968]{1,0:T(8,128)(2,1)S(1)}, u32[]{:S(2)}, u32[]{:S(2)}) collective-permute-start(bf16[64,3968]{1,0:T(8,128)(2,1)S(1)} %get-tuple-element.55.refs_6_), channel_id=1, source_target_pairs={{0,2},{1,3},{2,0},{3,1},{4,6},{5,7},{6,4},{7,5},{8,10},{9,11},{10,... | collective-permute-start | bytes 1523720 | tf_op jit(solution)/shard_map/ppermute | solution.py:333
  6.9 14.9 %collective-permute-start = (bf16[64,3968]{1,0:T(8,128)(2,1)S(1)}, bf16[64,3968]{1,0:T(8,128)(2,1)S(1)}, u32[]{:S(2)}, u32[]{:S(2)}) collective-permute-start(bf16[64,3968]{1,0:T(8,128)(2,1)S(1)} %get-tuple-element.55.refs_6_), channel_id=1, source_target_pairs={{0,4},{1,5},{2,6},{3,7},{4,8},{5,9},{6,10},{7,11},{8,12},{9,13},{1... | collective-permute-start | bytes 1523720 | tf_op jit(solution)/shard_map/ppermute | solution.py:330
  9.3 42.2 %copy-start = (bf16[512,512]{1,0:T(8,128)(2,1)S(1)}, bf16[512,512]{1,0:T(8,128)(2,1)}, u32[]{:S(2)}) copy-start(bf16[512,512]{1,0:T(8,128)(2,1)} %k) | copy-start | bytes 1572868
  9.4 42.2 %copy-start.1 = (bf16[512,512]{1,0:T(8,128)(2,1)S(1)}, bf16[512,512]{1,0:T(8,128)(2,1)}, u32[]{:S(2)}) copy-start(bf16[512,512]{1,0:T(8,128)(2,1)} %v.1) | copy-start | bytes 1572868
  9.4 42.2 %copy-start.3 = (bf16[512,512]{1,0:T(8,128)(2,1)S(1)}, bf16[512,512]{1,0:T(8,128)(2,1)}, u32[]{:S(2)}) copy-start(bf16[512,512]{1,0:T(8,128)(2,1)} %q.1) | copy-start | bytes 1572868
  10.8 28.1 %collective-permute-start.6 = (bf16[512,1152]{1,0:T(8,128)(2,1)S(1)}, bf16[512,1152]{1,0:T(8,128)(2,1)S(1)}, u32[]{:S(2)}, u32[]{:S(2)}) collective-permute-start(bf16[512,1152]{1,0:T(8,128)(2,1)S(1)} %pad_maximum_fusion), channel_id=1, source_target_pairs={{0,16},{1,17},{2,18},{3,19},{4,20},{5,21},{6,22},{7,23},{8,24},{9,... | collective-permute-start | bytes 3538952 | tf_op jit(solution)/shard_map/ppermute | solution.py:483
  21.8 12.2 %collective-permute-start.1 = (bf16[64,3968]{1,0:T(8,128)(2,1)S(1)}, bf16[64,3968]{1,0:T(8,128)(2,1)S(1)}, u32[]{:S(2)}, u32[]{:S(2)}) collective-permute-start(bf16[64,3968]{1,0:T(8,128)(2,1)S(1)} %get-tuple-element.55.refs_6_), channel_id=1, source_target_pairs={{0,12},{1,13},{2,14},{3,15},{4,0},{5,1},{6,2},{7,3},{8,4},{9,5},{1... | collective-permute-start | bytes 1523720 | tf_op jit(solution)/shard_map/ppermute | solution.py:330
  23.6 11.8 %collective-permute-start.4 = (bf16[64,3968]{1,0:T(8,128)(2,1)S(1)}, bf16[64,3968]{1,0:T(8,128)(2,1)S(1)}, u32[]{:S(2)}, u32[]{:S(2)}) collective-permute-start(bf16[64,3968]{1,0:T(8,128)(2,1)S(1)} %collective-permute-done.refs_2_), channel_id=1, source_target_pairs={{0,2},{1,3},{2,0},{3,1},{4,6},{5,7},{6,4},{7,5},{8,10},{9,11},{10,... | collective-permute-start | bytes 1523720 | tf_op jit(solution)/shard_map/ppermute | solution.py:333
  35.4 11.1 %collective-permute-start.5 = (bf16[64,3968]{1,0:T(8,128)(2,1)S(1)}, bf16[64,3968]{1,0:T(8,128)(2,1)S(1)}, u32[]{:S(2)}, u32[]{:S(2)}) collective-permute-start(bf16[64,3968]{1,0:T(8,128)(2,1)S(1)} %collective-permute-done.1.refs_4_), channel_id=1, source_target_pairs={{0,2},{1,3},{2,0},{3,1},{4,6},{5,7},{6,4},{7,5},{8,10},{9,11},{10,... | collective-permute-start | bytes 1523720 | tf_op jit(solution)/shard_map/ppermute | solution.py:333
  35.9 12.4 %collective-permute-start.2 = (bf16[64,3968]{1,0:T(8,128)(2,1)S(1)}, bf16[64,3968]{1,0:T(8,128)(2,1)S(1)}, u32[]{:S(2)}, u32[]{:S(2)}) collective-permute-start(bf16[64,3968]{1,0:T(8,128)(2,1)S(1)} %collective-permute-done.refs_2_), channel_id=1, source_target_pairs={{0,4},{1,5},{2,6},{3,7},{4,8},{5,9},{6,10},{7,11},{8,12},{9,13},{1... | collective-permute-start | bytes 1523720 | tf_op jit(solution)/shard_map/ppermute | solution.py:330
  38.9 7.7 %collective-permute-start.7 = (bf16[64,1280]{1,0:T(8,128)(2,1)S(1)}, bf16[64,1280]{1,0:T(8,128)(2,1)S(1)}, u32[]{:S(2)}, u32[]{:S(2)}) collective-permute-start(bf16[64,1280]{1,0:T(8,128)(2,1)S(1)} %slice.52), channel_id=1, source_target_pairs={{0,16},{16,0},{1,17},{17,1},{2,18},{18,2},{3,19},{19,3},{4,20},{20... | collective-permute-start | bytes 491528 | tf_op jit(solution)/shard_map/ppermute | solution.py:339
  41.4 17.8 %collective-permute-start.10 = (bf16[128,1280]{1,0:T(8,128)(2,1)S(1)}, bf16[128,1280]{1,0:T(8,128)(2,1)S(1)}, u32[]{:S(2)}, u32[]{:S(2)}) collective-permute-start(bf16[128,1280]{1,0:T(8,128)(2,1)S(1)} %pad_maximum_fusion.2), channel_id=1, source_target_pairs={{0,16},{16,0},{1,17},{17,1},{2,18},{18,2},{3,19},{19,3},{4,20},{20... | collective-permute-start | bytes 983048 | tf_op jit(solution)/shard_map/ppermute | solution.py:339
  48.4 12.1 %collective-permute-start.8 = (bf16[64,3968]{1,0:T(8,128)(2,1)S(1)}, bf16[64,3968]{1,0:T(8,128)(2,1)S(1)}, u32[]{:S(2)}, u32[]{:S(2)}) collective-permute-start(bf16[64,3968]{1,0:T(8,128)(2,1)S(1)} %collective-permute-done.2.refs_0_), channel_id=1, source_target_pairs={{0,2},{1,3},{2,0},{3,1},{4,6},{5,7},{6,4},{7,5},{8,10},{9,11},{10,... | collective-permute-start | bytes 1523720 | tf_op jit(solution)/shard_map/ppermute | solution.py:333
  50.0 10.5 %collective-permute-start.9 = (bf16[128,1280]{1,0:T(8,128)(2,1)S(1)}, bf16[128,1280]{1,0:T(8,128)(2,1)S(1)}, u32[]{:S(2)}, u32[]{:S(2)}) collective-permute-start(bf16[128,1280]{1,0:T(8,128)(2,1)S(1)} %pad_maximum_fusion.1), channel_id=1, source_target_pairs={{0,16},{16,0},{1,17},{17,1},{2,18},{18,2},{3,19},{19,3},{4,20},{20... | collective-permute-start | bytes 983048 | tf_op jit(solution)/shard_map/ppermute | solution.py:339
  60.0 5.6 %collective-permute-start.11 = (bf16[64,1280]{1,0:T(8,128)(2,1)}, bf16[64,1280]{1,0:T(8,128)(2,1)}, u32[]{:S(2)}, u32[]{:S(2)}) collective-permute-start(bf16[64,1280]{1,0:T(8,128)(2,1)} %slice.57), channel_id=1, source_target_pairs={{0,16},{16,0},{1,17},{17,1},{2,18},{18,2},{3,19},{19,3},{4,20},{20... | collective-permute-start | bytes 491528 | tf_op jit(solution)/shard_map/ppermute | solution.py:339
  61.3 6.1 %collective-permute-start.12 = (bf16[64,1280]{1,0:T(8,128)(2,1)}, bf16[64,1280]{1,0:T(8,128)(2,1)}, u32[]{:S(2)}, u32[]{:S(2)}) collective-permute-start(bf16[64,1280]{1,0:T(8,128)(2,1)} %slice.58), channel_id=1, source_target_pairs={{0,16},{16,0},{1,17},{17,1},{2,18},{18,2},{3,19},{19,3},{4,20},{20... | collective-permute-start | bytes 491528 | tf_op jit(solution)/shard_map/ppermute | solution.py:339
  79.0 12.6 %collective-permute-start.13 = (bf16[256,5248]{1,0:T(8,128)(2,1)S(1)}, bf16[256,5248]{1,0:T(8,128)(2,1)S(1)}, u32[]{:S(2)}, u32[]{:S(2)}) collective-permute-start(bf16[256,5248]{1,0:T(8,128)(2,1)S(1)} %get-tuple-element.83), channel_id=1, source_target_pairs={{0,1},{1,0},{2,3},{3,2},{4,5},{5,4},{6,7},{7,6},{8,9},{9,8},{10,11... | collective-permute-start | bytes 8060936 | tf_op jit(solution)/shard_map/ppermute | solution.py:336
  99.1 3.2 %collective-permute-start.14 = (bf16[128,5120]{1,0:T(8,128)(2,1)S(1)}, bf16[128,5120]{1,0:T(8,128)(2,1)S(1)}, u32[]{:S(2)}, u32[]{:S(2)}) collective-permute-start(bf16[128,5120]{1,0:T(8,128)(2,1)S(1)} %get-tuple-element.109), channel_id=1, source_target_pairs={{0,1},{1,0},{2,3},{3,2},{4,5},{5,4},{6,7},{7,6},{8,9},{9,8},{10,11... | collective-permute-start | bytes 3932168 | tf_op jit(solution)/shard_map/ppermute | solution.py:336
  102.3 3.0 %collective-permute-start.15 = (bf16[128,5120]{1,0:T(8,128)(2,1)S(1)}, bf16[128,5120]{1,0:T(8,128)(2,1)S(1)}, u32[]{:S(2)}, u32[]{:S(2)}) collective-permute-start(bf16[128,5120]{1,0:T(8,128)(2,1)S(1)} %get-tuple-element.93), channel_id=1, source_target_pairs={{0,1},{1,0},{2,3},{3,2},{4,5},{5,4},{6,7},{7,6},{8,9},{9,8},{10,11... | collective-permute-start | bytes 3932168 | tf_op jit(solution)/shard_map/ppermute | solution.py:336
  103.0 11.2 %collective-permute-start.18 = (bf16[128,1536]{1,0:T(8,128)(2,1)S(1)}, bf16[128,1536]{1,0:T(8,128)(2,1)S(1)}, u32[]{:S(2)}, u32[]{:S(2)}) collective-permute-start(bf16[128,1536]{1,0:T(8,128)(2,1)S(1)} %shard_map.107), channel_id=1, source_target_pairs={{0,16},{16,0},{1,17},{17,1},{2,18},{18,2},{3,19},{19,3},{4,20},{20... | collective-permute-start | bytes 1179656 | tf_op jit(solution)/shard_map/ppermute | solution.py:339
  114.5 11.8 %collective-permute-start.19 = (bf16[64,3584]{1,0:T(8,128)(2,1)S(1)}, bf16[64,3584]{1,0:T(8,128)(2,1)S(1)}, u32[]{:S(2)}, u32[]{:S(2)}) collective-permute-start(bf16[64,3584]{1,0:T(8,128)(2,1)S(1)} %shard_map.111), channel_id=1, source_target_pairs={{0,2},{1,3},{2,0},{3,1},{4,6},{5,7},{6,4},{7,5},{8,10},{9,11},{10,... | collective-permute-start | bytes 1376264 | tf_op jit(solution)/shard_map/ppermute | solution.py:333
  115.1 10.0 %collective-permute-start.17 = (bf16[128,1536]{1,0:T(8,128)(2,1)S(1)}, bf16[128,1536]{1,0:T(8,128)(2,1)S(1)}, u32[]{:S(2)}, u32[]{:S(2)}) collective-permute-start(bf16[128,1536]{1,0:T(8,128)(2,1)S(1)} %shard_map.108), channel_id=1, source_target_pairs={{0,16},{16,0},{1,17},{17,1},{2,18},{18,2},{3,19},{19,3},{4,20},{20... | collective-permute-start | bytes 1179656 | tf_op jit(solution)/shard_map/ppermute | solution.py:339
  126.6 12.0 %collective-permute-start.22 = (bf16[64,3584]{1,0:T(8,128)(2,1)S(1)}, bf16[64,3584]{1,0:T(8,128)(2,1)S(1)}, u32[]{:S(2)}, u32[]{:S(2)}) collective-permute-start(bf16[64,3584]{1,0:T(8,128)(2,1)S(1)} %shard_map.113), channel_id=1, source_target_pairs={{0,12},{1,13},{2,14},{3,15},{4,0},{5,1},{6,2},{7,3},{8,4},{9,5},{1... | collective-permute-start | bytes 1376264 | tf_op jit(solution)/shard_map/ppermute | solution.py:330
  129.0 10.9 %collective-permute-start.20 = (bf16[64,3584]{1,0:T(8,128)(2,1)S(1)}, bf16[64,3584]{1,0:T(8,128)(2,1)S(1)}, u32[]{:S(2)}, u32[]{:S(2)}) collective-permute-start(bf16[64,3584]{1,0:T(8,128)(2,1)S(1)} %shard_map.112), channel_id=1, source_target_pairs={{0,2},{1,3},{2,0},{3,1},{4,6},{5,7},{6,4},{7,5},{8,10},{9,11},{10,... | collective-permute-start | bytes 1376264 | tf_op jit(solution)/shard_map/ppermute | solution.py:333
  129.6 9.0 %collective-permute-start.21 = (bf16[128,1536]{1,0:T(8,128)(2,1)S(1)}, bf16[128,1536]{1,0:T(8,128)(2,1)S(1)}, u32[]{:S(2)}, u32[]{:S(2)}) collective-permute-start(bf16[128,1536]{1,0:T(8,128)(2,1)S(1)} %shard_map.109), channel_id=1, source_target_pairs={{0,16},{16,0},{1,17},{17,1},{2,18},{18,2},{3,19},{19,3},{4,20},{20... | collective-permute-start | bytes 1179656 | tf_op jit(solution)/shard_map/ppermute | solution.py:339
  140.2 11.1 %collective-permute-start.23 = (bf16[64,3584]{1,0:T(8,128)(2,1)S(1)}, bf16[64,3584]{1,0:T(8,128)(2,1)S(1)}, u32[]{:S(2)}, u32[]{:S(2)}) collective-permute-start(bf16[64,3584]{1,0:T(8,128)(2,1)S(1)} %shard_map.114), channel_id=1, source_target_pairs={{0,12},{1,13},{2,14},{3,15},{4,0},{5,1},{6,2},{7,3},{8,4},{9,5},{1... | collective-permute-start | bytes 1376264 | tf_op jit(solution)/shard_map/ppermute | solution.py:330
  142.6 12.1 %collective-permute-start.25 = (bf16[64,3584]{1,0:T(8,128)(2,1)S(1)}, bf16[64,3584]{1,0:T(8,128)(2,1)S(1)}, u32[]{:S(2)}, u32[]{:S(2)}) collective-permute-start(bf16[64,3584]{1,0:T(8,128)(2,1)S(1)} %shard_map.117), channel_id=1, source_target_pairs={{0,2},{1,3},{2,0},{3,1},{4,6},{5,7},{6,4},{7,5},{8,10},{9,11},{10,... | collective-permute-start | bytes 1376264 | tf_op jit(solution)/shard_map/ppermute | solution.py:333
  143.1 8.2 %collective-permute-start.16 = (bf16[128,1536]{1,0:T(8,128)(2,1)S(1)}, bf16[128,1536]{1,0:T(8,128)(2,1)S(1)}, u32[]{:S(2)}, u32[]{:S(2)}) collective-permute-start(bf16[128,1536]{1,0:T(8,128)(2,1)S(1)} %shard_map.110), channel_id=1, source_target_pairs={{0,16},{16,0},{1,17},{17,1},{2,18},{18,2},{3,19},{19,3},{4,20},{20... | collective-permute-start | bytes 1179656 | tf_op jit(solution)/shard_map/ppermute | solution.py:339
  151.5 10.9 %collective-permute-start.24 = (bf16[64,3584]{1,0:T(8,128)(2,1)S(1)}, bf16[64,3584]{1,0:T(8,128)(2,1)S(1)}, u32[]{:S(2)}, u32[]{:S(2)}) collective-permute-start(bf16[64,3584]{1,0:T(8,128)(2,1)S(1)} %shard_map.115), channel_id=1, source_target_pairs={{0,2},{1,3},{2,0},{3,1},{4,6},{5,7},{6,4},{7,5},{8,10},{9,11},{10,... | collective-permute-start | bytes 1376264 | tf_op jit(solution)/shard_map/ppermute | solution.py:333
  154.9 10.3 %collective-permute-start.26 = (bf16[64,3584]{1,0:T(8,128)(2,1)S(1)}, bf16[64,3584]{1,0:T(8,128)(2,1)S(1)}, u32[]{:S(2)}, u32[]{:S(2)}) collective-permute-start(bf16[64,3584]{1,0:T(8,128)(2,1)S(1)} %shard_map.118), channel_id=1, source_target_pairs={{0,4},{1,5},{2,6},{3,7},{4,8},{5,9},{6,10},{7,11},{8,12},{9,13},{1... | collective-permute-start | bytes 1376264 | tf_op jit(solution)/shard_map/ppermute | solution.py:330
  165.4 5.0 %collective-permute-start.27 = (bf16[64,1024]{1,0:T(8,128)(2,1)S(1)}, bf16[64,1024]{1,0:T(8,128)(2,1)S(1)}, u32[]{:S(2)}, u32[]{:S(2)}) collective-permute-start(bf16[64,1024]{1,0:T(8,128)(2,1)S(1)} %slice.72), channel_id=1, source_target_pairs={{0,16},{16,0},{1,17},{17,1},{2,18},{18,2},{3,19},{19,3},{4,20},{20... | collective-permute-start | bytes 393224 | tf_op jit(solution)/shard_map/ppermute | solution.py:339
  (15 other events, 43.3 us)

commit v5 on v4

--- a/solution.py
+++ b/solution.py
@@ -54,8 +54,9 @@
     return (summed / total[:, :, None]).reshape(rows, heads * HD).astype(BF16)
 
 SHARED = 2560
-OVER_X = 1536
-ORDER = [2, 1, 3, 0]
+OVER_X = 1792
+FIRST = [1, 3, 0]
+LAST = [2]
 
 VMEM = pl.BlockSpec(memory_space=pltpu.VMEM)
 SMEM = pl.BlockSpec(memory_space=pltpu.SMEM)
@@ -125,7 +126,7 @@
     split = more[0].shape[1]
     edge = width - LANES
     features = edge + split
-    step = 4
+    step = count
     total = count + len(more)
 
     def body(s_ref, *refs):
@@ -499,14 +500,23 @@
         more[3] = [before]
         more[2].append(x_swap(cut(across[2])))
 
-        near, meta, sent, placing = pick(
-            [b for d in ORDER for b in (line[d], across[d])],
-            [a for d in ORDER for a in more[d]],
-            me,
-            at_x,
-            cap,
-        )
+        def place(group, extra):
+            return pick(
+                [b for d in group for b in (line[d], across[d])], extra, me, at_x, cap
+            )
+
+        early, early_meta, early_sent, early_placing = place(
+            FIRST, [a for d in FIRST for a in more[d]]
+        )
+        early_far = core_swap(early_sent)
+        more[2][1], early = after((more[2][1], early))
+        near, meta, sent, placing = place(LAST, more[2])
         far = core_swap(sent)
+        join = lambda *parts: jnp.concatenate(parts, axis=0)
+        placing = join(placing, early_placing)
+        near, meta = join(near, early), join(meta, early_meta)
+        far = join(far, early_far)
+
         def expert(block, meta):
             gate = jnp.dot(block, w_in[0, 0], preferred_element_type=F32)
             up = jnp.dot(block, w_in[0, 1], preferred_element_type=F32)

time: 172 us -> 162 us (0.942)
  waiting for transfers between devices: 84.9 us -> 75.4 us
  local copies, waits for them, and re-layouts: 11.8 us -> 7.45 us
  Pallas kernels: 18.5 us -> 20.9 us
    ppermute x10, waiting for transfers between devices: 45 us -> 34.2 us  [x_swap(): return lax.ppermute(x, 'ctx', [(0, 1), (1, 0)])]
    unnamed x38 -> x46, local copies, waits for them, and re-layouts: 10.1 us -> 5.2 us
    ppermute x6, waiting for transfers between devices: 21.9 us -> 25.2 us  [z_shift(): return lax.ppermute(x, 'exp', pairs(lambda z, y, c: (z + d, y, c)))]
    pallas_call x1 -> x2, Pallas kernels: 6.85 us -> 9.15 us  [pick(): call(body, (shape(count * cap, features), shape(count * cap, LANES), shap...]
  transfers between devices with their start and end apart: 28 -> 29, of which waited for: 20 -> 19; matrix products, arithmetic and copies ran while one was open for 8% -> 10% of each run, Pallas kernels for 6% -> 13%
where the time goes in v5:
time: 162 us; the launch traced here: 161 us
  waiting for transfers between devices  75.4 us (47%)
  starting transfers between devices  33.8 us (21%)
  Pallas kernels  20.9 us (13%)
  matrix products  17 us (10%)
  local copies, waits for them, and re-layouts  7.45 us (5%)
  other arithmetic  5.51 us (3%)
    ppermute x10, waiting for transfers between devices, x_swap(): return lax.ppermute(x, 'ctx', [(0, 1), (1, 0)])  34.2 us
    ppermute x6, waiting for transfers between devices, z_shift(): return lax.ppermute(x, 'exp', pairs(lambda z, y, c: (z + d, y, c)))  25.2 us
    ppermute x10, starting transfers between devices, x_swap(): return lax.ppermute(x, 'ctx', [(0, 1), (1, 0)])  12.1 us
    ppermute x8, waiting for transfers between devices, y_swap(): return lax.ppermute(x, 'exp', pairs(lambda z, y, c: (z, 1 - y, c)))  11.6 us
    ppermute x8, starting transfers between devices, y_swap(): return lax.ppermute(x, 'exp', pairs(lambda z, y, c: (z, 1 - y, c)))  10.4 us
    pallas_call x2, Pallas kernels, pick(): call(body, (shape(count * cap, features), shape(count * cap, LANES), shap...  9.15 us
    dot_general x2, matrix products, expert(): up = jnp.dot(block, w_in[0, 1], preferred_element_type=F32)  7.85 us
    pallas_call x1, Pallas kernels, attend_pair(): call(body, jax.ShapeDtypeStruct((rows, width), BF16), 8 * rows * rows * w...  7.68 us
  transfers between devices with their start and end apart: 29, of which 19 were waited for; matrix products, arithmetic and copies ran while one was open for 10% of the time, Pallas kernels for 13%

profile of v5, /device:TPU:0, one launch (start us, length us, event | category | flops | bytes accessed | tf_op | source)
XLA Modules:
  0.0 161.2 jit_solution(2578912152265038643)
XLA Ops:
  3.3 3.0 %collective-permute-start.3 = (bf16[64,3968]{1,0:T(8,128)(2,1)S(1)}, bf16[64,3968]{1,0:T(8,128)(2,1)S(1)}, u32[]{:S(2)}, u32[]{:S(2)}) collective-permute-start(bf16[64,3968]{1,0:T(8,128)(2,1)S(1)} %get-tuple-element.61.refs_4_), channel_id=1, source_target_pairs={{0,2},{1,3},{2,0},{3,1},{4,6},{5,7},{6,4},{7,5},{8,10},{9,11},{10,... | collective-permute-start | bytes 1523720 | tf_op jit(solution)/shard_map/ppermute | solution.py:334
  6.3 1.6 collective-permute-start
  10.1 3.5 %collective-permute-start.6 = (bf16[512,1152]{1,0:T(8,128)(2,1)S(1)}, bf16[512,1152]{1,0:T(8,128)(2,1)S(1)}, u32[]{:S(2)}, u32[]{:S(2)}) collective-permute-start(bf16[512,1152]{1,0:T(8,128)(2,1)S(1)} %pad_maximum_fusion.1), channel_id=1, source_target_pairs={{0,16},{1,17},{2,18},{3,19},{4,20},{5,21},{6,22},{7,23},{8,24},{9,... | collective-permute-start | bytes 3538952 | tf_op jit(solution)/shard_map/ppermute | solution.py:484
  13.6 7.6 %collective-permute-done.refs_0_ = bf16[64,3968]{1,0:T(8,128)(2,1)S(1)} collective-permute-done((bf16[64,3968]{1,0:T(8,128)(2,1)S(1)}, bf16[64,3968]{1,0:T(8,128)(2,1)S(1)}, u32[]{:S(2)}, u32[]{:S(2)}) %collective-permute-start) | collective-permute-done | bytes 507936 | tf_op jit(solution)/shard_map/ppermute | solution.py:331
  21.2 1.7 %collective-permute-start.1 = (bf16[64,3968]{1,0:T(8,128)(2,1)S(1)}, bf16[64,3968]{1,0:T(8,128)(2,1)S(1)}, u32[]{:S(2)}, u32[]{:S(2)}) collective-permute-start(bf16[64,3968]{1,0:T(8,128)(2,1)S(1)} %get-tuple-element.61.refs_4_), channel_id=1, source_target_pairs={{0,12},{1,13},{2,14},{3,15},{4,0},{5,1},{6,2},{7,3},{8,4},{9,5},{1... | collective-permute-start | bytes 1523720 | tf_op jit(solution)/shard_map/ppermute | solution.py:331
  23.5 9.9 %collective-permute-done.1.refs_2_ = bf16[64,3968]{1,0:T(8,128)(2,1)S(1)} collective-permute-done((bf16[64,3968]{1,0:T(8,128)(2,1)S(1)}, bf16[64,3968]{1,0:T(8,128)(2,1)S(1)}, u32[]{:S(2)}, u32[]{:S(2)}) %collective-permute-start.1) | collective-permute-done | bytes 507936 | tf_op jit(solution)/shard_map/ppermute | solution.py:331
  38.2 2.5 %collective-permute-start.7 = (bf16[64,1280]{1,0:T(8,128)(2,1)S(1)}, bf16[64,1280]{1,0:T(8,128)(2,1)S(1)}, u32[]{:S(2)}, u32[]{:S(2)}) collective-permute-start(bf16[64,1280]{1,0:T(8,128)(2,1)S(1)} %slice.52), channel_id=1, source_target_pairs={{0,16},{16,0},{1,17},{17,1},{2,18},{18,2},{3,19},{19,3},{4,20},{20... | collective-permute-start | bytes 491528 | tf_op jit(solution)/shard_map/ppermute | solution.py:340
  41.5 4.2 %collective-permute-done.7.refs_9_ = bf16[64,1280]{1,0:T(8,128)(2,1)S(1)} collective-permute-done((bf16[64,1280]{1,0:T(8,128)(2,1)S(1)}, bf16[64,1280]{1,0:T(8,128)(2,1)S(1)}, u32[]{:S(2)}, u32[]{:S(2)}) %collective-permute-start.7) | collective-permute-done | bytes 163872 | tf_op jit(solution)/shard_map/ppermute | solution.py:340
  45.7 2.1 %collective-permute-done.2.refs_0_ = bf16[64,3968]{1,0:T(8,128)(2,1)} collective-permute-done((bf16[64,3968]{1,0:T(8,128)(2,1)S(1)}, bf16[64,3968]{1,0:T(8,128)(2,1)}, u32[]{:S(2)}, u32[]{:S(2)}) %collective-permute-start.2) | collective-permute-done | bytes 507936 | tf_op jit(solution)/shard_map/ppermute | solution.py:331
  53.5 7.7 %shard_map.105 = bf16[512,512]{1,0:T(8,128)(2,1)} custom-call(s32[1]{0:T(128)} %bitcast.x_ref, bf16[512,512]{1,0:T(8,128)(2,1)S(1)} %copy-done.9, bf16[512,512]{1,0:T(8,128)(2,1)S(1)} %copy-done, bf16[512,512]{1,0:T(8,128)(2,1)S(1)} %copy-done.1, bf16[512,128]{1,0:T(8,128)(2,1)S(1)} %fusion.30.docs, ...), custom_call_target="tpu_custom_call" | custom-call | flops 1073741824 | bytes 3670016 | tf_op jit(solution)/shard_map/pallas_call | solution.py:288
  63.7 1.6 collective-permute-start.12
  65.4 6.5 %shard_map.106 = (bf16[192,5120]{1,0:T(8,128)(2,1)S(1)}, bf16[192,128]{1,0:T(8,128)(2,1)S(1)}, bf16[192,5248]{1,0:T(8,128)(2,1)S(1)}, bf16[6,64,64]{2,1,0:T(8,128)(2,1)S(1)}) custom-call(s32[2]{0:T(128)S(1)} %pad_add_fusion.s_ref, bf16[64,3968]{1,0:T(8,128)(2,1)S(1)} %collective-permute-done.refs_0_, bf16[64,3968]{1,0:T(8,128)(2,1)S(1)} %copy-done.5, ...), custom_call_target="tpu_custom_call" | custom-call | flops 251658240 | bytes 7864320 | tf_op jit(solution)/shard_map/pallas_call | solution.py:188
  72.0 2.6 %shard_map.107 = (bf16[64,5120]{1,0:T(8,128)(2,1)S(1)}, bf16[64,128]{1,0:T(8,128)(2,1)S(1)}, bf16[64,5248]{1,0:T(8,128)(2,1)S(1)}, bf16[2,64,64]{2,1,0:T(8,128)(2,1)S(1)}) custom-call(s32[2]{0:T(128)S(1)} %pad_add_fusion.s_ref, bf16[64,3968]{1,0:T(8,128)(2,1)} %collective-permute-done.2.refs_0_, bf16[64,3968]{1,0:T(8,128)(2,1)} %collective-permute-done.8.refs_1_, ...), custom_call_target="tpu_custom_call" | custom-call | flops 83886080 | bytes 2621440 | tf_op jit(solution)/shard_map/pallas_call | solution.py:188
  75.4 5.6 %fusion.6 = f32[256,768]{1,0:T(8,128)S(1)} fusion(bf16[256,5120]{1,0:T(8,128)(2,1)S(1)} %constant_dynamic-update-slice_fusion.2, bf16[1,2,5120,768]{3,2,1,0:T(8,128)(2,1)} %param.16), kind=kOutput, calls=%fused_computation.6 | convolution fusion | flops 2013265920 | bytes 11272192 | tf_op jit(solution)/shard_map/dot_general | solution.py:522
  81.1 2.2 %fusion.10 = f32[256,768]{1,0:T(8,128)S(1)} fusion(bf16[256,5120]{1,0:T(8,128)(2,1)S(1)} %constant_dynamic-update-slice_fusion.2, bf16[1,2,5120,768]{3,2,1,0:T(8,128)(2,1)S(1)} %bitcast.38), kind=kOutput, calls=%fused_computation.10 | convolution fusion | flops 2013265920 | bytes 11272192 | tf_op jit(solution)/shard_map/dot_general | solution.py:521
  83.6 2.3 %fusion.25.near = bf16[256,5120]{1,0:T(8,128)(2,1)S(1)} fusion(bf16[256,768]{1,0:T(8,128)(2,1)S(1)} %multiply_convert_fusion.1, bf16[1,768,5120]{2,1,0:T(8,128)(2,1)S(1)} %bitcast.40, f32[256]{0:T(256)S(1)} %select_reduce_fusion.1), kind=kOutput, calls=%fused_computation.19 | convolution fusion | flops 2015887360 | bytes 10880000 | tf_op jit(solution)/shard_map/dot_general | solution.py:529
  86.2 2.2 %fusion.4 = f32[256,768]{1,0:T(8,128)S(1)} fusion(bf16[1,2,5120,768]{3,2,1,0:T(8,128)(2,1)S(1)} %bitcast.38, bf16[256,5248]{1,0:T(8,128)(2,1)S(1)} %pad_maximum_fusion), kind=kOutput, calls=%fused_computation.4 | convolution fusion | flops 2013265920 | bytes 11272192 | tf_op jit(solution)/shard_map/dot_general | solution.py:522
  88.5 2.2 %fusion.8 = f32[256,768]{1,0:T(8,128)S(1)} fusion(bf16[1,2,5120,768]{3,2,1,0:T(8,128)(2,1)S(1)} %bitcast.38, bf16[256,5248]{1,0:T(8,128)(2,1)S(1)} %pad_maximum_fusion), kind=kOutput, calls=%fused_computation.8 | convolution fusion | flops 2013265920 | bytes 11272192 | tf_op jit(solution)/shard_map/dot_general | solution.py:521
  91.0 2.4 %fusion.22 = bf16[256,5120]{1,0:T(8,128)(2,1)S(1)} fusion(bf16[256,768]{1,0:T(8,128)(2,1)S(1)} %multiply_convert_fusion, bf16[1,768,5120]{2,1,0:T(8,128)(2,1)S(1)} %bitcast.40, f32[256]{0:T(256)S(1)} %select_reduce_fusion), kind=kOutput, calls=%fused_computation.18 | convolution fusion | flops 2015887360 | bytes 10880000 | tf_op jit(solution)/shard_map/dot_general | solution.py:529
  93.7 3.0 %collective-permute-done.15.far = bf16[128,5120]{1,0:T(8,128)(2,1)S(1)} collective-permute-done((bf16[128,5120]{1,0:T(8,128)(2,1)S(1)}, bf16[128,5120]{1,0:T(8,128)(2,1)S(1)}, u32[]{:S(2)}, u32[]{:S(2)}) %collective-permute-start.15) | collective-permute-done | bytes 1310752 | tf_op jit(solution)/shard_map/ppermute | solution.py:337
  98.3 1.6 collective-permute-start.18
  100.8 9.9 %collective-permute-done.19.refs_0_ = bf16[128,1792]{1,0:T(8,128)(2,1)S(1)} collective-permute-done((bf16[128,1792]{1,0:T(8,128)(2,1)S(1)}, bf16[128,1792]{1,0:T(8,128)(2,1)S(1)}, u32[]{:S(2)}, u32[]{:S(2)}) %collective-permute-start.19) | collective-permute-done | bytes 458784 | tf_op jit(solution)/shard_map/ppermute | solution.py:340
  112.1 8.5 %collective-permute-done.18.refs_0_ = bf16[128,1792]{1,0:T(8,128)(2,1)S(1)} collective-permute-done((bf16[128,1792]{1,0:T(8,128)(2,1)S(1)}, bf16[128,1792]{1,0:T(8,128)(2,1)S(1)}, u32[]{:S(2)}, u32[]{:S(2)}) %collective-permute-start.18) | collective-permute-done | bytes 458784 | tf_op jit(solution)/shard_map/ppermute | solution.py:340
  124.7 5.7 %collective-permute-done.22.refs_0_ = bf16[128,1792]{1,0:T(8,128)(2,1)S(1)} collective-permute-done((bf16[128,1792]{1,0:T(8,128)(2,1)S(1)}, bf16[128,1792]{1,0:T(8,128)(2,1)S(1)}, u32[]{:S(2)}, u32[]{:S(2)}) %collective-permute-start.22) | collective-permute-done | bytes 458784 | tf_op jit(solution)/shard_map/ppermute | solution.py:340
  132.5 2.1 %collective-permute-start.24 = (bf16[64,3328]{1,0:T(8,128)(2,1)S(1)}, bf16[64,3328]{1,0:T(8,128)(2,1)S(1)}, u32[]{:S(2)}, u32[]{:S(2)}) collective-permute-start(bf16[64,3328]{1,0:T(8,128)(2,1)S(1)} %shard_map.115), channel_id=1, source_target_pairs={{0,12},{1,13},{2,14},{3,15},{4,0},{5,1},{6,2},{7,3},{8,4},{9,5},{1... | collective-permute-start | bytes 1277960 | tf_op jit(solution)/shard_map/ppermute | solution.py:331
  136.4 3.3 %collective-permute-done.17.refs_0_ = bf16[128,1792]{1,0:T(8,128)(2,1)S(1)} collective-permute-done((bf16[128,1792]{1,0:T(8,128)(2,1)S(1)}, bf16[128,1792]{1,0:T(8,128)(2,1)S(1)}, u32[]{:S(2)}, u32[]{:S(2)}) %collective-permute-start.17) | collective-permute-done | bytes 458784 | tf_op jit(solution)/shard_map/ppermute | solution.py:340
  139.7 1.8 %collective-permute-done.24 = bf16[64,3328]{1,0:T(8,128)(2,1)S(1)} collective-permute-done((bf16[64,3328]{1,0:T(8,128)(2,1)S(1)}, bf16[64,3328]{1,0:T(8,128)(2,1)S(1)}, u32[]{:S(2)}, u32[]{:S(2)}) %collective-permute-start.24) | collective-permute-done | bytes 426016 | tf_op jit(solution)/shard_map/ppermute | solution.py:331
  143.1 1.8 %collective-permute-done.26.refs_1_ = bf16[64,3328]{1,0:T(8,128)(2,1)S(1)} collective-permute-done((bf16[64,3328]{1,0:T(8,128)(2,1)S(1)}, bf16[64,3328]{1,0:T(8,128)(2,1)S(1)}, u32[]{:S(2)}, u32[]{:S(2)}) %collective-permute-start.26) | collective-permute-done | bytes 426016 | tf_op jit(solution)/shard_map/ppermute | solution.py:334
  145.5 7.2 %collective-permute-done.25.refs_1_ = bf16[64,3328]{1,0:T(8,128)(2,1)S(1)} collective-permute-done((bf16[64,3328]{1,0:T(8,128)(2,1)S(1)}, bf16[64,3328]{1,0:T(8,128)(2,1)S(1)}, u32[]{:S(2)}, u32[]{:S(2)}) %collective-permute-start.25) | collective-permute-done | bytes 426016 | tf_op jit(solution)/shard_map/ppermute | solution.py:334
  152.9 2.2 %collective-permute-done.27 = bf16[64,3328]{1,0:T(8,128)(2,1)S(1)} collective-permute-done((bf16[64,3328]{1,0:T(8,128)(2,1)S(1)}, bf16[64,3328]{1,0:T(8,128)(2,1)S(1)}, u32[]{:S(2)}, u32[]{:S(2)}) %collective-permute-start.27) | collective-permute-done | bytes 426016 | tf_op jit(solution)/shard_map/ppermute | solution.py:331
  155.3 2.6 %collective-permute-start.28 = (bf16[64,768]{1,0:T(8,128)(2,1)S(1)}, bf16[64,768]{1,0:T(8,128)(2,1)S(1)}, u32[]{:S(2)}, u32[]{:S(2)}) collective-permute-start(bf16[64,768]{1,0:T(8,128)(2,1)S(1)} %slice.72), channel_id=1, source_target_pairs={{0,16},{16,0},{1,17},{17,1},{2,18},{18,2},{3,19},{19,3},{4,20},{20... | collective-permute-start | bytes 294920 | tf_op jit(solution)/shard_map/ppermute | solution.py:340
  157.8 2.6 %collective-permute-done.28 = bf16[64,768]{1,0:T(8,128)(2,1)S(1)} collective-permute-done((bf16[64,768]{1,0:T(8,128)(2,1)S(1)}, bf16[64,768]{1,0:T(8,128)(2,1)S(1)}, u32[]{:S(2)}, u32[]{:S(2)}) %collective-permute-start.28) | collective-permute-done | bytes 98336 | tf_op jit(solution)/shard_map/ppermute | solution.py:340
  (122 shorter events, 36.2 us)
Async XLA Ops:
  3.3 47.7 %copy-start.10 = (bf16[64,3968]{1,0:T(8,128)(2,1)}, bf16[64,3968]{1,0:T(8,128)(2,1)S(1)}, u32[]{:S(2)}) copy-start(bf16[64,3968]{1,0:T(8,128)(2,1)S(1)} %get-tuple-element.61.refs_4_) | copy-start | bytes 1523716
  3.3 19.7 %collective-permute-start.3 = (bf16[64,3968]{1,0:T(8,128)(2,1)S(1)}, bf16[64,3968]{1,0:T(8,128)(2,1)S(1)}, u32[]{:S(2)}, u32[]{:S(2)}) collective-permute-start(bf16[64,3968]{1,0:T(8,128)(2,1)S(1)} %get-tuple-element.61.refs_4_), channel_id=1, source_target_pairs={{0,2},{1,3},{2,0},{3,1},{4,6},{5,7},{6,4},{7,5},{8,10},{9,11},{10,... | collective-permute-start | bytes 1523720 | tf_op jit(solution)/shard_map/ppermute | solution.py:334
  6.3 14.9 %collective-permute-start = (bf16[64,3968]{1,0:T(8,128)(2,1)S(1)}, bf16[64,3968]{1,0:T(8,128)(2,1)S(1)}, u32[]{:S(2)}, u32[]{:S(2)}) collective-permute-start(bf16[64,3968]{1,0:T(8,128)(2,1)S(1)} %get-tuple-element.61.refs_4_), channel_id=1, source_target_pairs={{0,4},{1,5},{2,6},{3,7},{4,8},{5,9},{6,10},{7,11},{8,12},{9,13},{1... | collective-permute-start | bytes 1523720 | tf_op jit(solution)/shard_map/ppermute | solution.py:331
  8.7 43.7 %copy-start = (bf16[512,512]{1,0:T(8,128)(2,1)S(1)}, bf16[512,512]{1,0:T(8,128)(2,1)}, u32[]{:S(2)}) copy-start(bf16[512,512]{1,0:T(8,128)(2,1)} %k) | copy-start | bytes 1572868
  8.7 43.7 %copy-start.1 = (bf16[512,512]{1,0:T(8,128)(2,1)S(1)}, bf16[512,512]{1,0:T(8,128)(2,1)}, u32[]{:S(2)}) copy-start(bf16[512,512]{1,0:T(8,128)(2,1)} %v.1) | copy-start | bytes 1572868
  10.1 28.1 %collective-permute-start.6 = (bf16[512,1152]{1,0:T(8,128)(2,1)S(1)}, bf16[512,1152]{1,0:T(8,128)(2,1)S(1)}, u32[]{:S(2)}, u32[]{:S(2)}) collective-permute-start(bf16[512,1152]{1,0:T(8,128)(2,1)S(1)} %pad_maximum_fusion.1), channel_id=1, source_target_pairs={{0,16},{1,17},{2,18},{3,19},{4,20},{5,21},{6,22},{7,23},{8,24},{9,... | collective-permute-start | bytes 3538952 | tf_op jit(solution)/shard_map/ppermute | solution.py:484
  21.2 12.2 %collective-permute-start.1 = (bf16[64,3968]{1,0:T(8,128)(2,1)S(1)}, bf16[64,3968]{1,0:T(8,128)(2,1)S(1)}, u32[]{:S(2)}, u32[]{:S(2)}) collective-permute-start(bf16[64,3968]{1,0:T(8,128)(2,1)S(1)} %get-tuple-element.61.refs_4_), channel_id=1, source_target_pairs={{0,12},{1,13},{2,14},{3,15},{4,0},{5,1},{6,2},{7,3},{8,4},{9,5},{1... | collective-permute-start | bytes 1523720 | tf_op jit(solution)/shard_map/ppermute | solution.py:331
  23.0 11.8 %collective-permute-start.4 = (bf16[64,3968]{1,0:T(8,128)(2,1)S(1)}, bf16[64,3968]{1,0:T(8,128)(2,1)S(1)}, u32[]{:S(2)}, u32[]{:S(2)}) collective-permute-start(bf16[64,3968]{1,0:T(8,128)(2,1)S(1)} %collective-permute-done.refs_0_), channel_id=1, source_target_pairs={{0,2},{1,3},{2,0},{3,1},{4,6},{5,7},{6,4},{7,5},{8,10},{9,11},{10,... | collective-permute-start | bytes 1523720 | tf_op jit(solution)/shard_map/ppermute | solution.py:334
  34.8 10.9 %collective-permute-start.5 = (bf16[64,3968]{1,0:T(8,128)(2,1)S(1)}, bf16[64,3968]{1,0:T(8,128)(2,1)S(1)}, u32[]{:S(2)}, u32[]{:S(2)}) collective-permute-start(bf16[64,3968]{1,0:T(8,128)(2,1)S(1)} %collective-permute-done.1.refs_2_), channel_id=1, source_target_pairs={{0,2},{1,3},{2,0},{3,1},{4,6},{5,7},{6,4},{7,5},{8,10},{9,11},{10,... | collective-permute-start | bytes 1523720 | tf_op jit(solution)/shard_map/ppermute | solution.py:334
  35.3 12.5 %collective-permute-start.2 = (bf16[64,3968]{1,0:T(8,128)(2,1)S(1)}, bf16[64,3968]{1,0:T(8,128)(2,1)}, u32[]{:S(2)}, u32[]{:S(2)}) collective-permute-start(bf16[64,3968]{1,0:T(8,128)(2,1)S(1)} %collective-permute-done.refs_0_), channel_id=1, source_target_pairs={{0,4},{1,5},{2,6},{3,7},{4,8},{5,9},{6,10},{7,11},{8,12},{9,13},{1... | collective-permute-start | bytes 1523720 | tf_op jit(solution)/shard_map/ppermute | solution.py:331
  38.2 7.5 %collective-permute-start.7 = (bf16[64,1280]{1,0:T(8,128)(2,1)S(1)}, bf16[64,1280]{1,0:T(8,128)(2,1)S(1)}, u32[]{:S(2)}, u32[]{:S(2)}) collective-permute-start(bf16[64,1280]{1,0:T(8,128)(2,1)S(1)} %slice.52), channel_id=1, source_target_pairs={{0,16},{16,0},{1,17},{17,1},{2,18},{18,2},{3,19},{19,3},{4,20},{20... | collective-permute-start | bytes 491528 | tf_op jit(solution)/shard_map/ppermute | solution.py:340
  41.5 19.7 %collective-permute-start.10 = (bf16[128,1280]{1,0:T(8,128)(2,1)}, bf16[128,1280]{1,0:T(8,128)(2,1)}, u32[]{:S(2)}, u32[]{:S(2)}) collective-permute-start(bf16[128,1280]{1,0:T(8,128)(2,1)} %pad_maximum_fusion.3), channel_id=1, source_target_pairs={{0,16},{16,0},{1,17},{17,1},{2,18},{18,2},{3,19},{19,3},{4,20},{20... | collective-permute-start | bytes 983048 | tf_op jit(solution)/shard_map/ppermute | solution.py:340
  48.7 14.1 %collective-permute-start.8 = (bf16[64,3968]{1,0:T(8,128)(2,1)}, bf16[64,3968]{1,0:T(8,128)(2,1)}, u32[]{:S(2)}, u32[]{:S(2)}) collective-permute-start(bf16[64,3968]{1,0:T(8,128)(2,1)} %collective-permute-done.2.refs_0_), channel_id=1, source_target_pairs={{0,2},{1,3},{2,0},{3,1},{4,6},{5,7},{6,4},{7,5},{8,10},{9,11},{10,... | collective-permute-start | bytes 1523720 | tf_op jit(solution)/shard_map/ppermute | solution.py:334
  51.0 11.8 %collective-permute-start.9 = (bf16[128,1280]{1,0:T(8,128)(2,1)}, bf16[128,1280]{1,0:T(8,128)(2,1)}, u32[]{:S(2)}, u32[]{:S(2)}) collective-permute-start(bf16[128,1280]{1,0:T(8,128)(2,1)} %pad_maximum_fusion.2), channel_id=1, source_target_pairs={{0,16},{16,0},{1,17},{17,1},{2,18},{18,2},{3,19},{19,3},{4,20},{20... | collective-permute-start | bytes 983048 | tf_op jit(solution)/shard_map/ppermute | solution.py:340
  62.2 9.8 %collective-permute-start.11 = (bf16[64,1280]{1,0:T(8,128)(2,1)S(1)}, bf16[64,1280]{1,0:T(8,128)(2,1)S(1)}, u32[]{:S(2)}, u32[]{:S(2)}) collective-permute-start(bf16[64,1280]{1,0:T(8,128)(2,1)S(1)} %slice.57), channel_id=1, source_target_pairs={{0,16},{16,0},{1,17},{17,1},{2,18},{18,2},{3,19},{19,3},{4,20},{20... | collective-permute-start | bytes 491528 | tf_op jit(solution)/shard_map/ppermute | solution.py:340
  63.7 8.3 %collective-permute-start.12 = (bf16[64,1280]{1,0:T(8,128)(2,1)S(1)}, bf16[64,1280]{1,0:T(8,128)(2,1)S(1)}, u32[]{:S(2)}, u32[]{:S(2)}) collective-permute-start(bf16[64,1280]{1,0:T(8,128)(2,1)S(1)} %slice.58), channel_id=1, source_target_pairs={{0,16},{16,0},{1,17},{17,1},{2,18},{18,2},{3,19},{19,3},{4,20},{20... | collective-permute-start | bytes 491528 | tf_op jit(solution)/shard_map/ppermute | solution.py:340
  71.9 14.0 %collective-permute-start.14 = (bf16[192,5248]{1,0:T(8,128)(2,1)S(1)}, bf16[192,5248]{1,0:T(8,128)(2,1)S(1)}, u32[]{:S(2)}, u32[]{:S(2)}) collective-permute-start(bf16[192,5248]{1,0:T(8,128)(2,1)S(1)} %get-tuple-element.95), channel_id=1, source_target_pairs={{0,1},{1,0},{2,3},{3,2},{4,5},{5,4},{6,7},{7,6},{8,9},{9,8},{10,11... | collective-permute-start | bytes 6045704 | tf_op jit(solution)/shard_map/ppermute | solution.py:337
  74.6 11.3 %collective-permute-start.13 = (bf16[64,5248]{1,0:T(8,128)(2,1)S(1)}, bf16[64,5248]{1,0:T(8,128)(2,1)S(1)}, u32[]{:S(2)}, u32[]{:S(2)}) collective-permute-start(bf16[64,5248]{1,0:T(8,128)(2,1)S(1)} %get-tuple-element.94), channel_id=1, source_target_pairs={{0,1},{1,0},{2,3},{3,2},{4,5},{5,4},{6,7},{7,6},{8,9},{9,8},{10,11... | collective-permute-start | bytes 2015240 | tf_op jit(solution)/shard_map/ppermute | solution.py:337
  93.6 3.1 %collective-permute-start.15 = (bf16[128,5120]{1,0:T(8,128)(2,1)S(1)}, bf16[128,5120]{1,0:T(8,128)(2,1)S(1)}, u32[]{:S(2)}, u32[]{:S(2)}) collective-permute-start(bf16[128,5120]{1,0:T(8,128)(2,1)S(1)} %get-tuple-element.121), channel_id=1, source_target_pairs={{0,1},{1,0},{2,3},{3,2},{4,5},{5,4},{6,7},{7,6},{8,9},{9,8},{10,11... | collective-permute-start | bytes 3932168 | tf_op jit(solution)/shard_map/ppermute | solution.py:337
  96.7 3.2 %collective-permute-start.16 = (bf16[128,5120]{1,0:T(8,128)(2,1)S(1)}, bf16[128,5120]{1,0:T(8,128)(2,1)S(1)}, u32[]{:S(2)}, u32[]{:S(2)}) collective-permute-start(bf16[128,5120]{1,0:T(8,128)(2,1)S(1)} %get-tuple-element.105), channel_id=1, source_target_pairs={{0,1},{1,0},{2,3},{3,2},{4,5},{5,4},{6,7},{7,6},{8,9},{9,8},{10,11... | collective-permute-start | bytes 3932168 | tf_op jit(solution)/shard_map/ppermute | solution.py:337
  97.3 13.4 %collective-permute-start.19 = (bf16[128,1792]{1,0:T(8,128)(2,1)S(1)}, bf16[128,1792]{1,0:T(8,128)(2,1)S(1)}, u32[]{:S(2)}, u32[]{:S(2)}) collective-permute-start(bf16[128,1792]{1,0:T(8,128)(2,1)S(1)} %shard_map.108), channel_id=1, source_target_pairs={{0,16},{16,0},{1,17},{17,1},{2,18},{18,2},{3,19},{19,3},{4,20},{20... | collective-permute-start | bytes 1376264 | tf_op jit(solution)/shard_map/ppermute | solution.py:340
  98.3 22.2 %collective-permute-start.18 = (bf16[128,1792]{1,0:T(8,128)(2,1)S(1)}, bf16[128,1792]{1,0:T(8,128)(2,1)S(1)}, u32[]{:S(2)}, u32[]{:S(2)}) collective-permute-start(bf16[128,1792]{1,0:T(8,128)(2,1)S(1)} %shard_map.109), channel_id=1, source_target_pairs={{0,16},{16,0},{1,17},{17,1},{2,18},{18,2},{3,19},{19,3},{4,20},{20... | collective-permute-start | bytes 1376264 | tf_op jit(solution)/shard_map/ppermute | solution.py:340
  111.0 10.8 %collective-permute-start.20 = (bf16[64,3328]{1,0:T(8,128)(2,1)S(1)}, bf16[64,3328]{1,0:T(8,128)(2,1)S(1)}, u32[]{:S(2)}, u32[]{:S(2)}) collective-permute-start(bf16[64,3328]{1,0:T(8,128)(2,1)S(1)} %shard_map.112), channel_id=1, source_target_pairs={{0,2},{1,3},{2,0},{3,1},{4,6},{5,7},{6,4},{7,5},{8,10},{9,11},{10,... | collective-permute-start | bytes 1277960 | tf_op jit(solution)/shard_map/ppermute | solution.py:334
  111.5 18.8 %collective-permute-start.22 = (bf16[128,1792]{1,0:T(8,128)(2,1)S(1)}, bf16[128,1792]{1,0:T(8,128)(2,1)S(1)}, u32[]{:S(2)}, u32[]{:S(2)}) collective-permute-start(bf16[128,1792]{1,0:T(8,128)(2,1)S(1)} %shard_map.110), channel_id=1, source_target_pairs={{0,16},{16,0},{1,17},{17,1},{2,18},{18,2},{3,19},{19,3},{4,20},{20... | collective-permute-start | bytes 1376264 | tf_op jit(solution)/shard_map/ppermute | solution.py:340
  122.0 9.9 %collective-permute-start.23 = (bf16[64,3328]{1,0:T(8,128)(2,1)S(1)}, bf16[64,3328]{1,0:T(8,128)(2,1)S(1)}, u32[]{:S(2)}, u32[]{:S(2)}) collective-permute-start(bf16[64,3328]{1,0:T(8,128)(2,1)S(1)} %shard_map.114), channel_id=1, source_target_pairs={{0,12},{1,13},{2,14},{3,15},{4,0},{5,1},{6,2},{7,3},{8,4},{9,5},{1... | collective-permute-start | bytes 1277960 | tf_op jit(solution)/shard_map/ppermute | solution.py:331
  122.6 9.5 %collective-permute-start.21 = (bf16[64,3328]{1,0:T(8,128)(2,1)S(1)}, bf16[64,3328]{1,0:T(8,128)(2,1)S(1)}, u32[]{:S(2)}, u32[]{:S(2)}) collective-permute-start(bf16[64,3328]{1,0:T(8,128)(2,1)S(1)} %shard_map.113), channel_id=1, source_target_pairs={{0,2},{1,3},{2,0},{3,1},{4,6},{5,7},{6,4},{7,5},{8,10},{9,11},{10,... | collective-permute-start | bytes 1277960 | tf_op jit(solution)/shard_map/ppermute | solution.py:334
  124.1 15.6 %collective-permute-start.17 = (bf16[128,1792]{1,0:T(8,128)(2,1)S(1)}, bf16[128,1792]{1,0:T(8,128)(2,1)S(1)}, u32[]{:S(2)}, u32[]{:S(2)}) collective-permute-start(bf16[128,1792]{1,0:T(8,128)(2,1)S(1)} %shard_map.111), channel_id=1, source_target_pairs={{0,16},{16,0},{1,17},{17,1},{2,18},{18,2},{3,19},{19,3},{4,20},{20... | collective-permute-start | bytes 1376264 | tf_op jit(solution)/shard_map/ppermute | solution.py:340
  132.5 9.0 %collective-permute-start.24 = (bf16[64,3328]{1,0:T(8,128)(2,1)S(1)}, bf16[64,3328]{1,0:T(8,128)(2,1)S(1)}, u32[]{:S(2)}, u32[]{:S(2)}) collective-permute-start(bf16[64,3328]{1,0:T(8,128)(2,1)S(1)} %shard_map.115), channel_id=1, source_target_pairs={{0,12},{1,13},{2,14},{3,15},{4,0},{5,1},{6,2},{7,3},{8,4},{9,5},{1... | collective-permute-start | bytes 1277960 | tf_op jit(solution)/shard_map/ppermute | solution.py:331
  134.9 10.0 %collective-permute-start.26 = (bf16[64,3328]{1,0:T(8,128)(2,1)S(1)}, bf16[64,3328]{1,0:T(8,128)(2,1)S(1)}, u32[]{:S(2)}, u32[]{:S(2)}) collective-permute-start(bf16[64,3328]{1,0:T(8,128)(2,1)S(1)} %shard_map.118), channel_id=1, source_target_pairs={{0,2},{1,3},{2,0},{3,1},{4,6},{5,7},{6,4},{7,5},{8,10},{9,11},{10,... | collective-permute-start | bytes 1277960 | tf_op jit(solution)/shard_map/ppermute | solution.py:334
  141.7 10.9 %collective-permute-start.25 = (bf16[64,3328]{1,0:T(8,128)(2,1)S(1)}, bf16[64,3328]{1,0:T(8,128)(2,1)S(1)}, u32[]{:S(2)}, u32[]{:S(2)}) collective-permute-start(bf16[64,3328]{1,0:T(8,128)(2,1)S(1)} %shard_map.116), channel_id=1, source_target_pairs={{0,2},{1,3},{2,0},{3,1},{4,6},{5,7},{6,4},{7,5},{8,10},{9,11},{10,... | collective-permute-start | bytes 1277960 | tf_op jit(solution)/shard_map/ppermute | solution.py:334
  145.1 10.0 %collective-permute-start.27 = (bf16[64,3328]{1,0:T(8,128)(2,1)S(1)}, bf16[64,3328]{1,0:T(8,128)(2,1)S(1)}, u32[]{:S(2)}, u32[]{:S(2)}) collective-permute-start(bf16[64,3328]{1,0:T(8,128)(2,1)S(1)} %shard_map.119), channel_id=1, source_target_pairs={{0,4},{1,5},{2,6},{3,7},{4,8},{5,9},{6,10},{7,11},{8,12},{9,13},{1... | collective-permute-start | bytes 1277960 | tf_op jit(solution)/shard_map/ppermute | solution.py:331
  155.3 5.1 %collective-permute-start.28 = (bf16[64,768]{1,0:T(8,128)(2,1)S(1)}, bf16[64,768]{1,0:T(8,128)(2,1)S(1)}, u32[]{:S(2)}, u32[]{:S(2)}) collective-permute-start(bf16[64,768]{1,0:T(8,128)(2,1)S(1)} %slice.72), channel_id=1, source_target_pairs={{0,16},{16,0},{1,17},{17,1},{2,18},{18,2},{3,19},{19,3},{4,20},{20... | collective-permute-start | bytes 294920 | tf_op jit(solution)/shard_map/ppermute | solution.py:340
  (19 other events, 146.3 us)

commit v6 on v5

--- a/solution.py
+++ b/solution.py
@@ -62,6 +62,7 @@
 SMEM = pl.BlockSpec(memory_space=pltpu.SMEM)
 MIB = 1024 * 1024
 LANES = 128
+SUBLANES = 16
 
 
 def call(body, out_shape, flops, moved, room, **kw):
@@ -193,7 +194,7 @@
             shape(count * cap, features + LANES),
             shape(count, rows, 2 * cap),
         ),
-        4 * count * cap * rows * features,
+        40 * count * cap * rows * features,
         2 * count * (rows + 2 * cap) * features,
         20,
         in_specs=[SMEM] + [pl.BlockSpec(memory_space=pltpu.HBM)] * total,
@@ -253,20 +254,19 @@
     )(at_x.reshape(1), placing, near, far, *[a for a, _ in adds])
 
 
-def attend_pair(q_input, k_input, v_input, docs, past, at_x):
+def attend_pair(q_input, k_input, v_input, segment_ids, past, at_x):
     rows, width = q_input.shape
     scale = HD ** (-0.5)
     turn = (((1,), (1,)), ((), ()))
 
-    def body(x_ref, q, k, v, docs, past_k, past_v, past_docs, out, bias):
+    def body(x_ref, q, k, v, down, along, past_k, past_v, past_docs, out, bias):
         @pl.when(pl.program_id(0) == 0)
         def _():
             i = lax.broadcasted_iota(jnp.int32, (rows, rows), 0)
             j = lax.broadcasted_iota(jnp.int32, (rows, rows), 1)
-            same = lax.dot_general(docs[...], past_docs[...], turn, preferred_element_type=F32)
-            bias[:, :rows] = jnp.where((same > 0.5) & (x_ref[0] > 0), 0.0, -1e30)
-            same = lax.dot_general(docs[...], docs[...], turn, preferred_element_type=F32)
-            bias[:, rows:] = jnp.where((same > 0.5) & (j <= i), 0.0, -1e30)
+            same = down[...] == past_docs[:1, :].astype(F32)
+            bias[:, :rows] = jnp.where(same & (x_ref[0] > 0), 0.0, -1e30)
+            bias[:, rows:] = jnp.where((down[...] == along[...]) & (j <= i), 0.0, -1e30)
 
         query = q[...]
         early = lax.dot_general(query, past_k[...], turn, preferred_element_type=F32)
@@ -288,7 +288,7 @@
     return call(
         body,
         jax.ShapeDtypeStruct((rows, width), BF16),
-        8 * rows * rows * width,
+        48 * rows * rows * width,
         14 * rows * width,
         14,
         grid=(heads,),
@@ -297,14 +297,25 @@
             head,
             head,
             head,
-            pl.BlockSpec((rows, LANES), lambda h: (0, 0)),
+            pl.BlockSpec((rows, 1), lambda h: (0, 0)),
+            pl.BlockSpec((1, rows), lambda h: (0, 0)),
             head,
-            pl.BlockSpec((rows, HD), lambda h: (0, heads + h)),
-            pl.BlockSpec((rows, LANES), lambda h: (0, 2 * heads)),
+            pl.BlockSpec((rows, HD), lambda h: (1, h)),
+            pl.BlockSpec((SUBLANES, rows), lambda h: (2 * rows // SUBLANES, 0)),
         ],
         out_specs=head,
         scratch_shapes=[pltpu.VMEM((rows, 2 * rows), F32)],
-    )(at_x.reshape(1), q_input, k_input, v_input, docs, past, past, past)
+    )(
+        at_x.reshape(1),
+        q_input,
+        k_input,
+        v_input,
+        segment_ids.astype(F32)[:, None],
+        segment_ids.astype(F32)[None, :],
+        past,
+        past,
+        past,
+    )
 
 
 def spread(onehot):
@@ -461,6 +472,18 @@
     def pair_device(
         q_input, k_input, v_input, segment_ids, tokens, expert_ids, route_weight, w_in, w_down
     ):
+        if q_input.shape[0] != q_input.shape[1]:
+            return on_device(
+                q_input,
+                k_input,
+                v_input,
+                segment_ids,
+                tokens,
+                expert_ids,
+                route_weight,
+                w_in,
+                w_down,
+            )
         me = lax.axis_index("exp")
         at_x = lax.axis_index("ctx")
         rows, width = tokens.shape
@@ -478,10 +501,9 @@
         line[3] = z_shift(again, -1)
         line[3], again = after((line[3], line[1]))
         line[2] = z_shift(again, 1)
-        block, segment_ids, k_input = after((block, segment_ids, k_input))
-        docs = segment_ids[:, None] == jnp.arange(LANES, dtype=jnp.int32)
-        docs = docs.astype(BF16)
-        past = lax.ppermute(jnp.concatenate([k_input, v_input, docs], axis=1), "ctx", [(0, 1)])
+        block, k_input = after((block, k_input))
+        docs = jnp.broadcast_to(segment_ids.astype(BF16)[None, :], (SUBLANES, k_input.shape[1]))
+        past = lax.ppermute(jnp.concatenate([k_input, v_input, docs], axis=0), "ctx", [(0, 1)])
         line[1], across[0] = after((line[1], across[0]))
         across[1] = y_swap(line[1])
         line[3], across[1] = after((line[3], across[1]))
@@ -495,7 +517,7 @@
         line[2], before = after((line[2], more[1][0]))
         more[1] = [before]
         more[2] = [x_swap(cut(line[2]))]
-        attn_out = attend_pair(q_input, k_input, v_input, docs, past, at_x)
+        attn_out = attend_pair(q_input, k_input, v_input, segment_ids, past, at_x)
         across[2], before, attn_out = after((across[2], more[3][0], attn_out))
         more[3] = [before]
         more[2].append(x_swap(cut(across[2])))

time: 162 us -> 155 us (0.957)
  matrix products: 17 us -> 13.6 us
  starting transfers between devices: 33.8 us -> 30.7 us
  waiting for transfers between devices: 75.4 us -> 77.5 us
  local copies, waits for them, and re-layouts: 7.45 us -> 5.79 us
    ppermute x10, waiting for transfers between devices: 34.2 us -> 38.4 us  [x_swap(): return lax.ppermute(x, 'ctx', [(0, 1), (1, 0)])]
    dot_general x2, matrix products: 7.85 us -> 4.46 us  [expert(): up = jnp.dot(block, w_in[0, 1], preferred_element_type=F32)]
    ppermute x8, starting transfers between devices: 10.4 us -> 7.79 us  [y_swap(): return lax.ppermute(x, 'exp', pairs(lambda z, y, c: (z, 1 - y, c)))]
    ppermute x6, waiting for transfers between devices: 25.2 us -> 23.1 us  [z_shift(): return lax.ppermute(x, 'exp', pairs(lambda z, y, c: (z + d, y, c)))]
    ppermute x10, starting transfers between devices: 12.1 us -> 10.2 us  [x_swap(): return lax.ppermute(x, 'ctx', [(0, 1), (1, 0)])]
    unnamed x46 -> x34, local copies, waits for them, and re-layouts: 5.2 us -> 3.36 us
  transfers between devices with their start and end apart: 29 -> 29, of which waited for: 19 -> 19; matrix products, arithmetic and copies ran while one was open for 10% -> 8% of each run, Pallas kernels for 13% -> 13%
where the time goes in v6:
time: 155 us
  waiting for transfers between devices  77.5 us (50%)
  starting transfers between devices  30.7 us (20%)
  Pallas kernels  20.9 us (13%)
  matrix products  13.6 us (9%)
  local copies, waits for them, and re-layouts  5.79 us (4%)
  other arithmetic  4.99 us (3%)
    ppermute x10, waiting for transfers between devices, x_swap(): return lax.ppermute(x, 'ctx', [(0, 1), (1, 0)])  38.4 us
    ppermute x6, waiting for transfers between devices, z_shift(): return lax.ppermute(x, 'exp', pairs(lambda z, y, c: (z + d, y, c)))  23.1 us
    ppermute x8, waiting for transfers between devices, y_swap(): return lax.ppermute(x, 'exp', pairs(lambda z, y, c: (z, 1 - y, c)))  13 us
    ppermute x10, starting transfers between devices, x_swap(): return lax.ppermute(x, 'ctx', [(0, 1), (1, 0)])  10.2 us
    pallas_call x2, Pallas kernels, pick(): call(body, (shape(count * cap, features), shape(count * cap, LANES), shap...  8.46 us
    pallas_call x1, Pallas kernels, attend_pair(): call(body, jax.ShapeDtypeStruct((rows, width), BF16), 48 * rows * rows *...  8.4 us
    ppermute x8, starting transfers between devices, y_swap(): return lax.ppermute(x, 'exp', pairs(lambda z, y, c: (z, 1 - y, c)))  7.79 us
    ppermute x6, starting transfers between devices, z_shift(): return lax.ppermute(x, 'exp', pairs(lambda z, y, c: (z + d, y, c)))  7.5 us
  transfers between devices with their start and end apart: 29, of which 19 were waited for; matrix products, arithmetic and copies ran while one was open for 8% of the time, Pallas kernels for 13%

profile of v6, /device:TPU:0, one launch (start us, length us, event | category | flops | bytes accessed | tf_op | source)
XLA Modules:
  0.0 154.6 jit_solution(3628422310584631848)
XLA Ops:
  3.3 3.0 %collective-permute-start.3 = (bf16[64,3968]{1,0:T(8,128)(2,1)S(1)}, bf16[64,3968]{1,0:T(8,128)(2,1)S(1)}, u32[]{:S(2)}, u32[]{:S(2)}) collective-permute-start(bf16[64,3968]{1,0:T(8,128)(2,1)S(1)} %get-tuple-element.60.refs_4_), channel_id=1, source_target_pairs={{0,2},{1,3},{2,0},{3,1},{4,6},{5,7},{6,4},{7,5},{8,10},{9,11},{10,... | collective-permute-start | bytes 1523720 | tf_op jit(solution)/shard_map/ppermute | solution.py:345
  6.3 1.6 %collective-permute-start = (bf16[64,3968]{1,0:T(8,128)(2,1)S(1)}, bf16[64,3968]{1,0:T(8,128)(2,1)S(1)}, u32[]{:S(2)}, u32[]{:S(2)}) collective-permute-start(bf16[64,3968]{1,0:T(8,128)(2,1)S(1)} %get-tuple-element.60.refs_4_), channel_id=1, source_target_pairs={{0,4},{1,5},{2,6},{3,7},{4,8},{5,9},{6,10},{7,11},{8,12},{9,13},{1... | collective-permute-start | bytes 1523720 | tf_op jit(solution)/shard_map/ppermute | solution.py:342
  8.7 2.4 %pad_maximum_fusion.1 = bf16[1040,512]{1,0:T(8,128)(2,1)} fusion(bf16[16,512]{1,0:T(8,128)(2,1)S(1)} %broadcast_in_dim.28, bf16[512,512]{1,0:T(8,128)(2,1)} %v.1, bf16[512,512]{1,0:T(8,128)(2,1)} %k), kind=kLoop, calls=%fused_computation.23 | loop fusion | flops 3194880 | bytes 2129920 | tf_op jit(solution)/shard_map/concatenate | solution.py:506
  11.0 4.4 %collective-permute-start.6 = (bf16[1040,512]{1,0:T(8,128)(2,1)}, bf16[1040,512]{1,0:T(8,128)(2,1)}, u32[]{:S(2)}, u32[]{:S(2)}) collective-permute-start(bf16[1040,512]{1,0:T(8,128)(2,1)} %pad_maximum_fusion.1), channel_id=1, source_target_pairs={{0,16},{1,17},{2,18},{3,19},{4,20},{5,21},{6,22},{7,23},{8,24},{9,... | collective-permute-start | bytes 3194888 | tf_op jit(solution)/shard_map/ppermute | solution.py:506
  15.4 5.8 %collective-permute-done.refs_0_ = bf16[64,3968]{1,0:T(8,128)(2,1)S(1)} collective-permute-done((bf16[64,3968]{1,0:T(8,128)(2,1)S(1)}, bf16[64,3968]{1,0:T(8,128)(2,1)S(1)}, u32[]{:S(2)}, u32[]{:S(2)}) %collective-permute-start) | collective-permute-done | bytes 507936 | tf_op jit(solution)/shard_map/ppermute | solution.py:342
  21.2 1.7 %collective-permute-start.1 = (bf16[64,3968]{1,0:T(8,128)(2,1)S(1)}, bf16[64,3968]{1,0:T(8,128)(2,1)S(1)}, u32[]{:S(2)}, u32[]{:S(2)}) collective-permute-start(bf16[64,3968]{1,0:T(8,128)(2,1)S(1)} %get-tuple-element.60.refs_4_), channel_id=1, source_target_pairs={{0,12},{1,13},{2,14},{3,15},{4,0},{5,1},{6,2},{7,3},{8,4},{9,5},{1... | collective-permute-start | bytes 1523720 | tf_op jit(solution)/shard_map/ppermute | solution.py:342
  23.5 9.9 %collective-permute-done.1.refs_2_ = bf16[64,3968]{1,0:T(8,128)(2,1)S(1)} collective-permute-done((bf16[64,3968]{1,0:T(8,128)(2,1)S(1)}, bf16[64,3968]{1,0:T(8,128)(2,1)S(1)}, u32[]{:S(2)}, u32[]{:S(2)}) %collective-permute-start.1) | collective-permute-done | bytes 507936 | tf_op jit(solution)/shard_map/ppermute | solution.py:342
  40.2 5.0 %collective-permute-done.7.refs_9_ = bf16[64,1280]{1,0:T(8,128)(2,1)S(1)} collective-permute-done((bf16[64,1280]{1,0:T(8,128)(2,1)S(1)}, bf16[64,1280]{1,0:T(8,128)(2,1)S(1)}, u32[]{:S(2)}, u32[]{:S(2)}) %collective-permute-start.7) | collective-permute-done | bytes 163872 | tf_op jit(solution)/shard_map/ppermute | solution.py:351
  46.6 1.9 %collective-permute-done.2.refs_0_ = bf16[64,3968]{1,0:T(8,128)(2,1)S(1)} collective-permute-done((bf16[64,3968]{1,0:T(8,128)(2,1)S(1)}, bf16[64,3968]{1,0:T(8,128)(2,1)S(1)}, u32[]{:S(2)}, u32[]{:S(2)}) %collective-permute-start.2) | collective-permute-done | bytes 507936 | tf_op jit(solution)/shard_map/ppermute | solution.py:342
  49.5 1.9 %collective-permute-start.9 = (bf16[128,1280]{1,0:T(8,128)(2,1)S(1)}, bf16[128,1280]{1,0:T(8,128)(2,1)S(1)}, u32[]{:S(2)}, u32[]{:S(2)}) collective-permute-start(bf16[128,1280]{1,0:T(8,128)(2,1)S(1)} %pad_maximum_fusion.2), channel_id=1, source_target_pairs={{0,16},{16,0},{1,17},{17,1},{2,18},{18,2},{3,19},{19,3},{4,20},{20... | collective-permute-start | bytes 983048 | tf_op jit(solution)/shard_map/ppermute | solution.py:351
  53.0 8.4 %shard_map.105 = bf16[512,512]{1,0:T(8,128)(2,1)} custom-call(s32[1]{0:T(128)} %bitcast.x_ref, bf16[512,512]{1,0:T(8,128)(2,1)S(1)} %copy-done.7, bf16[512,512]{1,0:T(8,128)(2,1)S(1)} %copy-done.1, bf16[512,512]{1,0:T(8,128)(2,1)S(1)} %copy-done.2, f32[512,1]{1,0:T(8,128)S(1)} %copy.11.down, f32[1,512]{1,0:T(1,128)S(1)} %bitcast.38, ...), custom_call_target="tpu_custom_call" | custom-call | flops 6442450944 | bytes 3670016 | tf_op jit(solution)/shard_map/pallas_call | solution.py:288
  61.7 1.9 %collective-permute-start.12 = (bf16[64,1280]{1,0:T(8,128)(2,1)S(1)}, bf16[64,1280]{1,0:T(8,128)(2,1)S(1)}, u32[]{:S(2)}, u32[]{:S(2)}) collective-permute-start(bf16[64,1280]{1,0:T(8,128)(2,1)S(1)} %slice.58), channel_id=1, source_target_pairs={{0,16},{16,0},{1,17},{17,1},{2,18},{18,2},{3,19},{19,3},{4,20},{20... | collective-permute-start | bytes 491528 | tf_op jit(solution)/shard_map/ppermute | solution.py:351
  63.6 5.8 %shard_map.106 = (bf16[192,5120]{1,0:T(8,128)(2,1)S(1)}, bf16[192,128]{1,0:T(8,128)(2,1)S(1)}, bf16[192,5248]{1,0:T(8,128)(2,1)S(1)}, bf16[6,64,64]{2,1,0:T(8,128)(2,1)S(1)}) custom-call(s32[2]{0:T(128)S(1)} %pad_add_fusion.s_ref, bf16[64,3968]{1,0:T(8,128)(2,1)S(1)} %collective-permute-done.refs_0_, bf16[64,3968]{1,0:T(8,128)(2,1)S(1)} %copy-done.4, ...), custom_call_target="tpu_custom_call" | custom-call | flops 2516582400 | bytes 7864320 | tf_op jit(solution)/shard_map/pallas_call | solution.py:189
  69.4 2.7 %shard_map.107 = (bf16[64,5120]{1,0:T(8,128)(2,1)S(1)}, bf16[64,128]{1,0:T(8,128)(2,1)S(1)}, bf16[64,5248]{1,0:T(8,128)(2,1)S(1)}, bf16[2,64,64]{2,1,0:T(8,128)(2,1)S(1)}) custom-call(s32[2]{0:T(128)S(1)} %pad_add_fusion.s_ref, bf16[64,3968]{1,0:T(8,128)(2,1)S(1)} %collective-permute-done.2.refs_0_, bf16[64,3968]{1,0:T(8,128)(2,1)S(1)} %collective-permute-done.8.refs_1_, ...), custom_call_target="tpu_custom_call" | custom-call | flops 838860800 | bytes 2621440 | tf_op jit(solution)/shard_map/pallas_call | solution.py:189
  72.9 2.2 %fusion.6 = f32[256,768]{1,0:T(8,128)S(1)} fusion(bf16[256,5120]{1,0:T(8,128)(2,1)S(1)} %constant_dynamic-update-slice_fusion.2, bf16[1,2,5120,768]{3,2,1,0:T(8,128)(2,1)S(1)} %bitcast.42), kind=kOutput, calls=%fused_computation.6 | convolution fusion | flops 2013265920 | bytes 11272192 | tf_op jit(solution)/shard_map/dot_general | solution.py:544
  75.2 2.2 %fusion.10 = f32[256,768]{1,0:T(8,128)S(1)} fusion(bf16[256,5120]{1,0:T(8,128)(2,1)S(1)} %constant_dynamic-update-slice_fusion.2, bf16[1,2,5120,768]{3,2,1,0:T(8,128)(2,1)S(1)} %bitcast.42), kind=kOutput, calls=%fused_computation.10 | convolution fusion | flops 2013265920 | bytes 11272192 | tf_op jit(solution)/shard_map/dot_general | solution.py:543
  77.8 2.3 %fusion.25.near = bf16[256,5120]{1,0:T(8,128)(2,1)S(1)} fusion(bf16[256,768]{1,0:T(8,128)(2,1)S(1)} %multiply_convert_fusion.1, bf16[1,768,5120]{2,1,0:T(8,128)(2,1)S(1)} %bitcast.44, f32[256]{0:T(256)S(1)} %select_reduce_fusion.1), kind=kOutput, calls=%fused_computation.19 | convolution fusion | flops 2015887360 | bytes 10880000 | tf_op jit(solution)/shard_map/dot_general | solution.py:551
  80.3 2.2 %fusion.4 = f32[256,768]{1,0:T(8,128)S(1)} fusion(bf16[1,2,5120,768]{3,2,1,0:T(8,128)(2,1)S(1)} %bitcast.42, bf16[256,5248]{1,0:T(8,128)(2,1)S(1)} %pad_maximum_fusion), kind=kOutput, calls=%fused_computation.4 | convolution fusion | flops 2013265920 | bytes 11272192 | tf_op jit(solution)/shard_map/dot_general | solution.py:544
  82.6 2.2 %fusion.8 = f32[256,768]{1,0:T(8,128)S(1)} fusion(bf16[1,2,5120,768]{3,2,1,0:T(8,128)(2,1)S(1)} %bitcast.42, bf16[256,5248]{1,0:T(8,128)(2,1)S(1)} %pad_maximum_fusion), kind=kOutput, calls=%fused_computation.8 | convolution fusion | flops 2013265920 | bytes 11272192 | tf_op jit(solution)/shard_map/dot_general | solution.py:543
  85.1 2.4 %fusion.22 = bf16[256,5120]{1,0:T(8,128)(2,1)S(1)} fusion(bf16[256,768]{1,0:T(8,128)(2,1)S(1)} %multiply_convert_fusion, bf16[1,768,5120]{2,1,0:T(8,128)(2,1)S(1)} %bitcast.44, f32[256]{0:T(256)S(1)} %select_reduce_fusion), kind=kOutput, calls=%fused_computation.18 | convolution fusion | flops 2015887360 | bytes 10880000 | tf_op jit(solution)/shard_map/dot_general | solution.py:551
  87.8 3.0 %collective-permute-done.15.far = bf16[128,5120]{1,0:T(8,128)(2,1)S(1)} collective-permute-done((bf16[128,5120]{1,0:T(8,128)(2,1)S(1)}, bf16[128,5120]{1,0:T(8,128)(2,1)S(1)}, u32[]{:S(2)}, u32[]{:S(2)}) %collective-permute-start.15) | collective-permute-done | bytes 1310752 | tf_op jit(solution)/shard_map/ppermute | solution.py:348
  92.1 1.9 %collective-permute-start.18 = (bf16[128,1792]{1,0:T(8,128)(2,1)S(1)}, bf16[128,1792]{1,0:T(8,128)(2,1)S(1)}, u32[]{:S(2)}, u32[]{:S(2)}) collective-permute-start(bf16[128,1792]{1,0:T(8,128)(2,1)S(1)} %shard_map.109), channel_id=1, source_target_pairs={{0,16},{16,0},{1,17},{17,1},{2,18},{18,2},{3,19},{19,3},{4,20},{20... | collective-permute-start | bytes 1376264 | tf_op jit(solution)/shard_map/ppermute | solution.py:351
  94.9 9.9 %collective-permute-done.19.refs_0_ = bf16[128,1792]{1,0:T(8,128)(2,1)S(1)} collective-permute-done((bf16[128,1792]{1,0:T(8,128)(2,1)S(1)}, bf16[128,1792]{1,0:T(8,128)(2,1)S(1)}, u32[]{:S(2)}, u32[]{:S(2)}) %collective-permute-start.19) | collective-permute-done | bytes 458784 | tf_op jit(solution)/shard_map/ppermute | solution.py:351
  106.3 8.4 %collective-permute-done.18.refs_0_ = bf16[128,1792]{1,0:T(8,128)(2,1)S(1)} collective-permute-done((bf16[128,1792]{1,0:T(8,128)(2,1)S(1)}, bf16[128,1792]{1,0:T(8,128)(2,1)S(1)}, u32[]{:S(2)}, u32[]{:S(2)}) %collective-permute-start.18) | collective-permute-done | bytes 458784 | tf_op jit(solution)/shard_map/ppermute | solution.py:351
  118.0 6.5 %collective-permute-done.22.refs_0_ = bf16[128,1792]{1,0:T(8,128)(2,1)S(1)} collective-permute-done((bf16[128,1792]{1,0:T(8,128)(2,1)S(1)}, bf16[128,1792]{1,0:T(8,128)(2,1)S(1)}, u32[]{:S(2)}, u32[]{:S(2)}) %collective-permute-start.22) | collective-permute-done | bytes 458784 | tf_op jit(solution)/shard_map/ppermute | solution.py:351
  126.5 2.1 %collective-permute-start.24 = (bf16[64,3328]{1,0:T(8,128)(2,1)S(1)}, bf16[64,3328]{1,0:T(8,128)(2,1)S(1)}, u32[]{:S(2)}, u32[]{:S(2)}) collective-permute-start(bf16[64,3328]{1,0:T(8,128)(2,1)S(1)} %shard_map.115), channel_id=1, source_target_pairs={{0,12},{1,13},{2,14},{3,15},{4,0},{5,1},{6,2},{7,3},{8,4},{9,5},{1... | collective-permute-start | bytes 1277960 | tf_op jit(solution)/shard_map/ppermute | solution.py:342
  129.5 4.3 %collective-permute-done.17.refs_0_ = bf16[128,1792]{1,0:T(8,128)(2,1)S(1)} collective-permute-done((bf16[128,1792]{1,0:T(8,128)(2,1)S(1)}, bf16[128,1792]{1,0:T(8,128)(2,1)S(1)}, u32[]{:S(2)}, u32[]{:S(2)}) %collective-permute-start.17) | collective-permute-done | bytes 458784 | tf_op jit(solution)/shard_map/ppermute | solution.py:351
  133.8 1.8 %collective-permute-done.24 = bf16[64,3328]{1,0:T(8,128)(2,1)S(1)} collective-permute-done((bf16[64,3328]{1,0:T(8,128)(2,1)S(1)}, bf16[64,3328]{1,0:T(8,128)(2,1)S(1)}, u32[]{:S(2)}, u32[]{:S(2)}) %collective-permute-start.24) | collective-permute-done | bytes 426016 | tf_op jit(solution)/shard_map/ppermute | solution.py:342
  136.4 2.4 %collective-permute-done.26.refs_1_ = bf16[64,3328]{1,0:T(8,128)(2,1)S(1)} collective-permute-done((bf16[64,3328]{1,0:T(8,128)(2,1)S(1)}, bf16[64,3328]{1,0:T(8,128)(2,1)S(1)}, u32[]{:S(2)}, u32[]{:S(2)}) %collective-permute-start.26) | collective-permute-done | bytes 426016 | tf_op jit(solution)/shard_map/ppermute | solution.py:345
  140.0 6.7 %collective-permute-done.25.refs_1_ = bf16[64,3328]{1,0:T(8,128)(2,1)S(1)} collective-permute-done((bf16[64,3328]{1,0:T(8,128)(2,1)S(1)}, bf16[64,3328]{1,0:T(8,128)(2,1)S(1)}, u32[]{:S(2)}, u32[]{:S(2)}) %collective-permute-start.25) | collective-permute-done | bytes 426016 | tf_op jit(solution)/shard_map/ppermute | solution.py:345
  146.9 2.1 %collective-permute-done.27 = bf16[64,3328]{1,0:T(8,128)(2,1)S(1)} collective-permute-done((bf16[64,3328]{1,0:T(8,128)(2,1)S(1)}, bf16[64,3328]{1,0:T(8,128)(2,1)S(1)}, u32[]{:S(2)}, u32[]{:S(2)}) %collective-permute-start.27) | collective-permute-done | bytes 426016 | tf_op jit(solution)/shard_map/ppermute | solution.py:342
  149.6 4.3 %collective-permute-done.28 = bf16[64,768]{1,0:T(8,128)(2,1)S(1)} collective-permute-done((bf16[64,768]{1,0:T(8,128)(2,1)S(1)}, bf16[64,768]{1,0:T(8,128)(2,1)S(1)}, u32[]{:S(2)}, u32[]{:S(2)}) %collective-permute-start.28) | collective-permute-done | bytes 98336 | tf_op jit(solution)/shard_map/ppermute | solution.py:351
  (112 shorter events, 30.2 us)
Async XLA Ops:
  3.3 32.8 %copy-start.8 = (bf16[64,3968]{1,0:T(8,128)(2,1)}, bf16[64,3968]{1,0:T(8,128)(2,1)S(1)}, u32[]{:S(2)}) copy-start(bf16[64,3968]{1,0:T(8,128)(2,1)S(1)} %get-tuple-element.60.refs_4_) | copy-start | bytes 1523716
  3.3 19.7 %collective-permute-start.3 = (bf16[64,3968]{1,0:T(8,128)(2,1)S(1)}, bf16[64,3968]{1,0:T(8,128)(2,1)S(1)}, u32[]{:S(2)}, u32[]{:S(2)}) collective-permute-start(bf16[64,3968]{1,0:T(8,128)(2,1)S(1)} %get-tuple-element.60.refs_4_), channel_id=1, source_target_pairs={{0,2},{1,3},{2,0},{3,1},{4,6},{5,7},{6,4},{7,5},{8,10},{9,11},{10,... | collective-permute-start | bytes 1523720 | tf_op jit(solution)/shard_map/ppermute | solution.py:345
  6.3 14.9 %collective-permute-start = (bf16[64,3968]{1,0:T(8,128)(2,1)S(1)}, bf16[64,3968]{1,0:T(8,128)(2,1)S(1)}, u32[]{:S(2)}, u32[]{:S(2)}) collective-permute-start(bf16[64,3968]{1,0:T(8,128)(2,1)S(1)} %get-tuple-element.60.refs_4_), channel_id=1, source_target_pairs={{0,4},{1,5},{2,6},{3,7},{4,8},{5,9},{6,10},{7,11},{8,12},{9,13},{1... | collective-permute-start | bytes 1523720 | tf_op jit(solution)/shard_map/ppermute | solution.py:342
  8.7 44.2 %copy-start.1 = (bf16[512,512]{1,0:T(8,128)(2,1)S(1)}, bf16[512,512]{1,0:T(8,128)(2,1)}, u32[]{:S(2)}) copy-start(bf16[512,512]{1,0:T(8,128)(2,1)} %k) | copy-start | bytes 1572868
  8.7 44.2 %copy-start.2 = (bf16[512,512]{1,0:T(8,128)(2,1)S(1)}, bf16[512,512]{1,0:T(8,128)(2,1)}, u32[]{:S(2)}) copy-start(bf16[512,512]{1,0:T(8,128)(2,1)} %v.1) | copy-start | bytes 1572868
  11.0 26.9 %collective-permute-start.6 = (bf16[1040,512]{1,0:T(8,128)(2,1)}, bf16[1040,512]{1,0:T(8,128)(2,1)}, u32[]{:S(2)}, u32[]{:S(2)}) collective-permute-start(bf16[1040,512]{1,0:T(8,128)(2,1)} %pad_maximum_fusion.1), channel_id=1, source_target_pairs={{0,16},{1,17},{2,18},{3,19},{4,20},{5,21},{6,22},{7,23},{8,24},{9,... | collective-permute-start | bytes 3194888 | tf_op jit(solution)/shard_map/ppermute | solution.py:506
  21.2 12.2 %collective-permute-start.1 = (bf16[64,3968]{1,0:T(8,128)(2,1)S(1)}, bf16[64,3968]{1,0:T(8,128)(2,1)S(1)}, u32[]{:S(2)}, u32[]{:S(2)}) collective-permute-start(bf16[64,3968]{1,0:T(8,128)(2,1)S(1)} %get-tuple-element.60.refs_4_), channel_id=1, source_target_pairs={{0,12},{1,13},{2,14},{3,15},{4,0},{5,1},{6,2},{7,3},{8,4},{9,5},{1... | collective-permute-start | bytes 1523720 | tf_op jit(solution)/shard_map/ppermute | solution.py:342
  23.0 11.8 %collective-permute-start.4 = (bf16[64,3968]{1,0:T(8,128)(2,1)S(1)}, bf16[64,3968]{1,0:T(8,128)(2,1)S(1)}, u32[]{:S(2)}, u32[]{:S(2)}) collective-permute-start(bf16[64,3968]{1,0:T(8,128)(2,1)S(1)} %collective-permute-done.refs_0_), channel_id=1, source_target_pairs={{0,2},{1,3},{2,0},{3,1},{4,6},{5,7},{6,4},{7,5},{8,10},{9,11},{10,... | collective-permute-start | bytes 1523720 | tf_op jit(solution)/shard_map/ppermute | solution.py:345
  35.6 11.0 %collective-permute-start.5 = (bf16[64,3968]{1,0:T(8,128)(2,1)S(1)}, bf16[64,3968]{1,0:T(8,128)(2,1)}, u32[]{:S(2)}, u32[]{:S(2)}) collective-permute-start(bf16[64,3968]{1,0:T(8,128)(2,1)S(1)} %collective-permute-done.1.refs_2_), channel_id=1, source_target_pairs={{0,2},{1,3},{2,0},{3,1},{4,6},{5,7},{6,4},{7,5},{8,10},{9,11},{10,... | collective-permute-start | bytes 1523720 | tf_op jit(solution)/shard_map/ppermute | solution.py:345
  36.1 12.4 %collective-permute-start.2 = (bf16[64,3968]{1,0:T(8,128)(2,1)S(1)}, bf16[64,3968]{1,0:T(8,128)(2,1)S(1)}, u32[]{:S(2)}, u32[]{:S(2)}) collective-permute-start(bf16[64,3968]{1,0:T(8,128)(2,1)S(1)} %collective-permute-done.refs_0_), channel_id=1, source_target_pairs={{0,4},{1,5},{2,6},{3,7},{4,8},{5,9},{6,10},{7,11},{8,12},{9,13},{1... | collective-permute-start | bytes 1523720 | tf_op jit(solution)/shard_map/ppermute | solution.py:342
  38.0 7.2 %collective-permute-start.7 = (bf16[64,1280]{1,0:T(8,128)(2,1)S(1)}, bf16[64,1280]{1,0:T(8,128)(2,1)S(1)}, u32[]{:S(2)}, u32[]{:S(2)}) collective-permute-start(bf16[64,1280]{1,0:T(8,128)(2,1)S(1)} %slice.52), channel_id=1, source_target_pairs={{0,16},{16,0},{1,17},{17,1},{2,18},{18,2},{3,19},{19,3},{4,20},{20... | collective-permute-start | bytes 491528 | tf_op jit(solution)/shard_map/ppermute | solution.py:351
  39.5 21.8 %collective-permute-start.10 = (bf16[128,1280]{1,0:T(8,128)(2,1)S(1)}, bf16[128,1280]{1,0:T(8,128)(2,1)S(1)}, u32[]{:S(2)}, u32[]{:S(2)}) collective-permute-start(bf16[128,1280]{1,0:T(8,128)(2,1)S(1)} %pad_maximum_fusion.3), channel_id=1, source_target_pairs={{0,16},{16,0},{1,17},{17,1},{2,18},{18,2},{3,19},{19,3},{4,20},{20... | collective-permute-start | bytes 983048 | tf_op jit(solution)/shard_map/ppermute | solution.py:351
  49.5 12.2 %collective-permute-start.9 = (bf16[128,1280]{1,0:T(8,128)(2,1)S(1)}, bf16[128,1280]{1,0:T(8,128)(2,1)S(1)}, u32[]{:S(2)}, u32[]{:S(2)}) collective-permute-start(bf16[128,1280]{1,0:T(8,128)(2,1)S(1)} %pad_maximum_fusion.2), channel_id=1, source_target_pairs={{0,16},{16,0},{1,17},{17,1},{2,18},{18,2},{3,19},{19,3},{4,20},{20... | collective-permute-start | bytes 983048 | tf_op jit(solution)/shard_map/ppermute | solution.py:351
  51.4 10.3 %collective-permute-start.8 = (bf16[64,3968]{1,0:T(8,128)(2,1)S(1)}, bf16[64,3968]{1,0:T(8,128)(2,1)S(1)}, u32[]{:S(2)}, u32[]{:S(2)}) collective-permute-start(bf16[64,3968]{1,0:T(8,128)(2,1)S(1)} %collective-permute-done.2.refs_0_), channel_id=1, source_target_pairs={{0,2},{1,3},{2,0},{3,1},{4,6},{5,7},{6,4},{7,5},{8,10},{9,11},{10,... | collective-permute-start | bytes 1523720 | tf_op jit(solution)/shard_map/ppermute | solution.py:345
  61.4 8.0 %collective-permute-start.11 = (bf16[64,1280]{1,0:T(8,128)(2,1)S(1)}, bf16[64,1280]{1,0:T(8,128)(2,1)S(1)}, u32[]{:S(2)}, u32[]{:S(2)}) collective-permute-start(bf16[64,1280]{1,0:T(8,128)(2,1)S(1)} %slice.57), channel_id=1, source_target_pairs={{0,16},{16,0},{1,17},{17,1},{2,18},{18,2},{3,19},{19,3},{4,20},{20... | collective-permute-start | bytes 491528 | tf_op jit(solution)/shard_map/ppermute | solution.py:351
  61.7 7.7 %collective-permute-start.12 = (bf16[64,1280]{1,0:T(8,128)(2,1)S(1)}, bf16[64,1280]{1,0:T(8,128)(2,1)S(1)}, u32[]{:S(2)}, u32[]{:S(2)}) collective-permute-start(bf16[64,1280]{1,0:T(8,128)(2,1)S(1)} %slice.58), channel_id=1, source_target_pairs={{0,16},{16,0},{1,17},{17,1},{2,18},{18,2},{3,19},{19,3},{4,20},{20... | collective-permute-start | bytes 491528 | tf_op jit(solution)/shard_map/ppermute | solution.py:351
  69.3 10.7 %collective-permute-start.14 = (bf16[192,5248]{1,0:T(8,128)(2,1)S(1)}, bf16[192,5248]{1,0:T(8,128)(2,1)S(1)}, u32[]{:S(2)}, u32[]{:S(2)}) collective-permute-start(bf16[192,5248]{1,0:T(8,128)(2,1)S(1)} %get-tuple-element.93), channel_id=1, source_target_pairs={{0,1},{1,0},{2,3},{3,2},{4,5},{5,4},{6,7},{7,6},{8,9},{9,8},{10,11... | collective-permute-start | bytes 6045704 | tf_op jit(solution)/shard_map/ppermute | solution.py:348
  72.2 7.9 %collective-permute-start.13 = (bf16[64,5248]{1,0:T(8,128)(2,1)S(1)}, bf16[64,5248]{1,0:T(8,128)(2,1)S(1)}, u32[]{:S(2)}, u32[]{:S(2)}) collective-permute-start(bf16[64,5248]{1,0:T(8,128)(2,1)S(1)} %get-tuple-element.92), channel_id=1, source_target_pairs={{0,1},{1,0},{2,3},{3,2},{4,5},{5,4},{6,7},{7,6},{8,9},{9,8},{10,11... | collective-permute-start | bytes 2015240 | tf_op jit(solution)/shard_map/ppermute | solution.py:348
  87.7 3.1 %collective-permute-start.15 = (bf16[128,5120]{1,0:T(8,128)(2,1)S(1)}, bf16[128,5120]{1,0:T(8,128)(2,1)S(1)}, u32[]{:S(2)}, u32[]{:S(2)}) collective-permute-start(bf16[128,5120]{1,0:T(8,128)(2,1)S(1)} %get-tuple-element.119), channel_id=1, source_target_pairs={{0,1},{1,0},{2,3},{3,2},{4,5},{5,4},{6,7},{7,6},{8,9},{9,8},{10,11... | collective-permute-start | bytes 3932168 | tf_op jit(solution)/shard_map/ppermute | solution.py:348
  90.8 3.2 %collective-permute-start.16 = (bf16[128,5120]{1,0:T(8,128)(2,1)S(1)}, bf16[128,5120]{1,0:T(8,128)(2,1)S(1)}, u32[]{:S(2)}, u32[]{:S(2)}) collective-permute-start(bf16[128,5120]{1,0:T(8,128)(2,1)S(1)} %get-tuple-element.103), channel_id=1, source_target_pairs={{0,1},{1,0},{2,3},{3,2},{4,5},{5,4},{6,7},{7,6},{8,9},{9,8},{10,11... | collective-permute-start | bytes 3932168 | tf_op jit(solution)/shard_map/ppermute | solution.py:348
  91.4 13.4 %collective-permute-start.19 = (bf16[128,1792]{1,0:T(8,128)(2,1)S(1)}, bf16[128,1792]{1,0:T(8,128)(2,1)S(1)}, u32[]{:S(2)}, u32[]{:S(2)}) collective-permute-start(bf16[128,1792]{1,0:T(8,128)(2,1)S(1)} %shard_map.108), channel_id=1, source_target_pairs={{0,16},{16,0},{1,17},{17,1},{2,18},{18,2},{3,19},{19,3},{4,20},{20... | collective-permute-start | bytes 1376264 | tf_op jit(solution)/shard_map/ppermute | solution.py:351
  92.1 22.5 %collective-permute-start.18 = (bf16[128,1792]{1,0:T(8,128)(2,1)S(1)}, bf16[128,1792]{1,0:T(8,128)(2,1)S(1)}, u32[]{:S(2)}, u32[]{:S(2)}) collective-permute-start(bf16[128,1792]{1,0:T(8,128)(2,1)S(1)} %shard_map.109), channel_id=1, source_target_pairs={{0,16},{16,0},{1,17},{17,1},{2,18},{18,2},{3,19},{19,3},{4,20},{20... | collective-permute-start | bytes 1376264 | tf_op jit(solution)/shard_map/ppermute | solution.py:351
  105.1 10.8 %collective-permute-start.20 = (bf16[64,3328]{1,0:T(8,128)(2,1)S(1)}, bf16[64,3328]{1,0:T(8,128)(2,1)S(1)}, u32[]{:S(2)}, u32[]{:S(2)}) collective-permute-start(bf16[64,3328]{1,0:T(8,128)(2,1)S(1)} %shard_map.112), channel_id=1, source_target_pairs={{0,2},{1,3},{2,0},{3,1},{4,6},{5,7},{6,4},{7,5},{8,10},{9,11},{10,... | collective-permute-start | bytes 1277960 | tf_op jit(solution)/shard_map/ppermute | solution.py:345
  105.7 18.8 %collective-permute-start.22 = (bf16[128,1792]{1,0:T(8,128)(2,1)S(1)}, bf16[128,1792]{1,0:T(8,128)(2,1)S(1)}, u32[]{:S(2)}, u32[]{:S(2)}) collective-permute-start(bf16[128,1792]{1,0:T(8,128)(2,1)S(1)} %shard_map.110), channel_id=1, source_target_pairs={{0,16},{16,0},{1,17},{17,1},{2,18},{18,2},{3,19},{19,3},{4,20},{20... | collective-permute-start | bytes 1376264 | tf_op jit(solution)/shard_map/ppermute | solution.py:351
  116.1 9.9 %collective-permute-start.23 = (bf16[64,3328]{1,0:T(8,128)(2,1)S(1)}, bf16[64,3328]{1,0:T(8,128)(2,1)S(1)}, u32[]{:S(2)}, u32[]{:S(2)}) collective-permute-start(bf16[64,3328]{1,0:T(8,128)(2,1)S(1)} %shard_map.114), channel_id=1, source_target_pairs={{0,12},{1,13},{2,14},{3,15},{4,0},{5,1},{6,2},{7,3},{8,4},{9,5},{1... | collective-permute-start | bytes 1277960 | tf_op jit(solution)/shard_map/ppermute | solution.py:342
  116.6 9.5 %collective-permute-start.21 = (bf16[64,3328]{1,0:T(8,128)(2,1)S(1)}, bf16[64,3328]{1,0:T(8,128)(2,1)S(1)}, u32[]{:S(2)}, u32[]{:S(2)}) collective-permute-start(bf16[64,3328]{1,0:T(8,128)(2,1)S(1)} %shard_map.113), channel_id=1, source_target_pairs={{0,2},{1,3},{2,0},{3,1},{4,6},{5,7},{6,4},{7,5},{8,10},{9,11},{10,... | collective-permute-start | bytes 1277960 | tf_op jit(solution)/shard_map/ppermute | solution.py:345
  117.2 16.6 %collective-permute-start.17 = (bf16[128,1792]{1,0:T(8,128)(2,1)S(1)}, bf16[128,1792]{1,0:T(8,128)(2,1)S(1)}, u32[]{:S(2)}, u32[]{:S(2)}) collective-permute-start(bf16[128,1792]{1,0:T(8,128)(2,1)S(1)} %shard_map.111), channel_id=1, source_target_pairs={{0,16},{16,0},{1,17},{17,1},{2,18},{18,2},{3,19},{19,3},{4,20},{20... | collective-permute-start | bytes 1376264 | tf_op jit(solution)/shard_map/ppermute | solution.py:351
  126.5 9.1 %collective-permute-start.24 = (bf16[64,3328]{1,0:T(8,128)(2,1)S(1)}, bf16[64,3328]{1,0:T(8,128)(2,1)S(1)}, u32[]{:S(2)}, u32[]{:S(2)}) collective-permute-start(bf16[64,3328]{1,0:T(8,128)(2,1)S(1)} %shard_map.115), channel_id=1, source_target_pairs={{0,12},{1,13},{2,14},{3,15},{4,0},{5,1},{6,2},{7,3},{8,4},{9,5},{1... | collective-permute-start | bytes 1277960 | tf_op jit(solution)/shard_map/ppermute | solution.py:342
  128.9 9.9 %collective-permute-start.26 = (bf16[64,3328]{1,0:T(8,128)(2,1)S(1)}, bf16[64,3328]{1,0:T(8,128)(2,1)S(1)}, u32[]{:S(2)}, u32[]{:S(2)}) collective-permute-start(bf16[64,3328]{1,0:T(8,128)(2,1)S(1)} %shard_map.118), channel_id=1, source_target_pairs={{0,2},{1,3},{2,0},{3,1},{4,6},{5,7},{6,4},{7,5},{8,10},{9,11},{10,... | collective-permute-start | bytes 1277960 | tf_op jit(solution)/shard_map/ppermute | solution.py:345
  135.9 10.8 %collective-permute-start.25 = (bf16[64,3328]{1,0:T(8,128)(2,1)S(1)}, bf16[64,3328]{1,0:T(8,128)(2,1)S(1)}, u32[]{:S(2)}, u32[]{:S(2)}) collective-permute-start(bf16[64,3328]{1,0:T(8,128)(2,1)S(1)} %shard_map.116), channel_id=1, source_target_pairs={{0,2},{1,3},{2,0},{3,1},{4,6},{5,7},{6,4},{7,5},{8,10},{9,11},{10,... | collective-permute-start | bytes 1277960 | tf_op jit(solution)/shard_map/ppermute | solution.py:345
  139.1 10.0 %collective-permute-start.27 = (bf16[64,3328]{1,0:T(8,128)(2,1)S(1)}, bf16[64,3328]{1,0:T(8,128)(2,1)S(1)}, u32[]{:S(2)}, u32[]{:S(2)}) collective-permute-start(bf16[64,3328]{1,0:T(8,128)(2,1)S(1)} %shard_map.119), channel_id=1, source_target_pairs={{0,4},{1,5},{2,6},{3,7},{4,8},{5,9},{6,10},{7,11},{8,12},{9,13},{1... | collective-permute-start | bytes 1277960 | tf_op jit(solution)/shard_map/ppermute | solution.py:342
  149.2 4.7 %collective-permute-start.28 = (bf16[64,768]{1,0:T(8,128)(2,1)S(1)}, bf16[64,768]{1,0:T(8,128)(2,1)S(1)}, u32[]{:S(2)}, u32[]{:S(2)}) collective-permute-start(bf16[64,768]{1,0:T(8,128)(2,1)S(1)} %slice.72), channel_id=1, source_target_pairs={{0,16},{16,0},{1,17},{17,1},{2,18},{18,2},{3,19},{19,3},{4,20},{20... | collective-permute-start | bytes 294920 | tf_op jit(solution)/shard_map/ppermute | solution.py:351
  (13 other events, 117.2 us)

commit v7 on v6

--- a/solution.py
+++ b/solution.py
@@ -516,11 +516,10 @@
         more[3] = [x_swap(both(3))]
         line[2], before = after((line[2], more[1][0]))
         more[1] = [before]
-        more[2] = [x_swap(cut(line[2]))]
         attn_out = attend_pair(q_input, k_input, v_input, segment_ids, past, at_x)
         across[2], before, attn_out = after((across[2], more[3][0], attn_out))
         more[3] = [before]
-        more[2].append(x_swap(cut(across[2])))
+        more[2] = [x_swap(both(2))]
 
         def place(group, extra):
             return pick(
@@ -531,7 +530,7 @@
             FIRST, [a for d in FIRST for a in more[d]]
         )
         early_far = core_swap(early_sent)
-        more[2][1], early = after((more[2][1], early))
+        more[2][0], early = after((more[2][0], early))
         near, meta, sent, placing = place(LAST, more[2])
         far = core_swap(sent)
         join = lambda *parts: jnp.concatenate(parts, axis=0)

time: 155 us -> 152 us (0.981)
  waiting for transfers between devices: 77.5 us -> 73.5 us
  starting transfers between devices: 30.7 us -> 33.4 us
    ppermute x8, starting transfers between devices: 7.79 us -> 10.5 us  [y_swap(): return lax.ppermute(x, 'exp', pairs(lambda z, y, c: (z, 1 - y, c)))]
    ppermute x10 -> x9, waiting for transfers between devices: 38.4 us -> 36.9 us  [x_swap(): return lax.ppermute(x, 'ctx', [(0, 1), (1, 0)])]
    unnamed x34 -> x30, local copies, waits for them, and re-layouts: 3.36 us -> 2.56 us
    ppermute x10 -> x9, starting transfers between devices: 10.2 us -> 9.77 us  [x_swap(): return lax.ppermute(x, 'ctx', [(0, 1), (1, 0)])]
  transfers between devices with their start and end apart: 29 -> 28, of which waited for: 19 -> 20; matrix products, arithmetic and copies ran while one was open for 8% -> 8% of each run, Pallas kernels for 13% -> 13%
where the time goes in v7:
time: 152 us
  waiting for transfers between devices  73.5 us (48%)
  starting transfers between devices  33.4 us (22%)
  Pallas kernels  20.2 us (13%)
  matrix products  13.6 us (9%)
  local copies, waits for them, and re-layouts  5.01 us (3%)
  other arithmetic  5.01 us (3%)
    ppermute x9, waiting for transfers between devices, x_swap(): return lax.ppermute(x, 'ctx', [(0, 1), (1, 0)])  36.9 us
    ppermute x6, waiting for transfers between devices, z_shift(): return lax.ppermute(x, 'exp', pairs(lambda z, y, c: (z + d, y, c)))  22.2 us
    ppermute x8, waiting for transfers between devices, y_swap(): return lax.ppermute(x, 'exp', pairs(lambda z, y, c: (z, 1 - y, c)))  11.7 us
    ppermute x8, starting transfers between devices, y_swap(): return lax.ppermute(x, 'exp', pairs(lambda z, y, c: (z, 1 - y, c)))  10.5 us
    ppermute x9, starting transfers between devices, x_swap(): return lax.ppermute(x, 'ctx', [(0, 1), (1, 0)])  9.77 us
    pallas_call x1, Pallas kernels, attend_pair(): call(body, jax.ShapeDtypeStruct((rows, width), BF16), 48 * rows * rows *...  8.4 us
    pallas_call x2, Pallas kernels, pick(): call(body, (shape(count * cap, features), shape(count * cap, LANES), shap...  7.79 us
    ppermute x6, starting transfers between devices, z_shift(): return lax.ppermute(x, 'exp', pairs(lambda z, y, c: (z + d, y, c)))  7.68 us
  transfers between devices with their start and end apart: 28, of which 20 were waited for; matrix products, arithmetic and copies ran while one was open for 8% of the time, Pallas kernels for 13%

profile of v7, /device:TPU:0, one launch (start us, length us, event | category | flops | bytes accessed | tf_op | source)
XLA Modules:
  0.0 152.0 jit_solution(7505194309775291426)
XLA Ops:
  3.3 3.0 %collective-permute-start.3 = (bf16[64,3968]{1,0:T(8,128)(2,1)S(1)}, bf16[64,3968]{1,0:T(8,128)(2,1)S(1)}, u32[]{:S(2)}, u32[]{:S(2)}) collective-permute-start(bf16[64,3968]{1,0:T(8,128)(2,1)S(1)} %get-tuple-element.60.refs_4_), channel_id=1, source_target_pairs={{0,2},{1,3},{2,0},{3,1},{4,6},{5,7},{6,4},{7,5},{8,10},{9,11},{10,... | collective-permute-start | bytes 1523720 | tf_op jit(solution)/shard_map/ppermute | solution.py:345
  6.3 1.6 %collective-permute-start = (bf16[64,3968]{1,0:T(8,128)(2,1)S(1)}, bf16[64,3968]{1,0:T(8,128)(2,1)S(1)}, u32[]{:S(2)}, u32[]{:S(2)}) collective-permute-start(bf16[64,3968]{1,0:T(8,128)(2,1)S(1)} %get-tuple-element.60.refs_4_), channel_id=1, source_target_pairs={{0,4},{1,5},{2,6},{3,7},{4,8},{5,9},{6,10},{7,11},{8,12},{9,13},{1... | collective-permute-start | bytes 1523720 | tf_op jit(solution)/shard_map/ppermute | solution.py:342
  8.7 2.4 %pad_maximum_fusion.1 = bf16[1040,512]{1,0:T(8,128)(2,1)} fusion(bf16[16,512]{1,0:T(8,128)(2,1)S(1)} %broadcast_in_dim.28, bf16[512,512]{1,0:T(8,128)(2,1)} %v.1, bf16[512,512]{1,0:T(8,128)(2,1)} %k), kind=kLoop, calls=%fused_computation.23 | loop fusion | flops 3194880 | bytes 2129920 | tf_op jit(solution)/shard_map/concatenate | solution.py:506
  11.0 4.4 %collective-permute-start.6 = (bf16[1040,512]{1,0:T(8,128)(2,1)}, bf16[1040,512]{1,0:T(8,128)(2,1)}, u32[]{:S(2)}, u32[]{:S(2)}) collective-permute-start(bf16[1040,512]{1,0:T(8,128)(2,1)} %pad_maximum_fusion.1), channel_id=1, source_target_pairs={{0,16},{1,17},{2,18},{3,19},{4,20},{5,21},{6,22},{7,23},{8,24},{9,... | collective-permute-start | bytes 3194888 | tf_op jit(solution)/shard_map/ppermute | solution.py:506
  15.4 5.8 %collective-permute-done.refs_0_ = bf16[64,3968]{1,0:T(8,128)(2,1)S(1)} collective-permute-done((bf16[64,3968]{1,0:T(8,128)(2,1)S(1)}, bf16[64,3968]{1,0:T(8,128)(2,1)S(1)}, u32[]{:S(2)}, u32[]{:S(2)}) %collective-permute-start) | collective-permute-done | bytes 507936 | tf_op jit(solution)/shard_map/ppermute | solution.py:342
  21.2 1.7 %collective-permute-start.1 = (bf16[64,3968]{1,0:T(8,128)(2,1)S(1)}, bf16[64,3968]{1,0:T(8,128)(2,1)S(1)}, u32[]{:S(2)}, u32[]{:S(2)}) collective-permute-start(bf16[64,3968]{1,0:T(8,128)(2,1)S(1)} %get-tuple-element.60.refs_4_), channel_id=1, source_target_pairs={{0,12},{1,13},{2,14},{3,15},{4,0},{5,1},{6,2},{7,3},{8,4},{9,5},{1... | collective-permute-start | bytes 1523720 | tf_op jit(solution)/shard_map/ppermute | solution.py:342
  23.5 9.9 %collective-permute-done.1.refs_2_ = bf16[64,3968]{1,0:T(8,128)(2,1)S(1)} collective-permute-done((bf16[64,3968]{1,0:T(8,128)(2,1)S(1)}, bf16[64,3968]{1,0:T(8,128)(2,1)S(1)}, u32[]{:S(2)}, u32[]{:S(2)}) %collective-permute-start.1) | collective-permute-done | bytes 507936 | tf_op jit(solution)/shard_map/ppermute | solution.py:342
  37.3 2.2 %collective-permute-start.7 = (bf16[64,1280]{1,0:T(8,128)(2,1)S(1)}, bf16[64,1280]{1,0:T(8,128)(2,1)S(1)}, u32[]{:S(2)}, u32[]{:S(2)}) collective-permute-start(bf16[64,1280]{1,0:T(8,128)(2,1)S(1)} %slice.52), channel_id=1, source_target_pairs={{0,16},{16,0},{1,17},{17,1},{2,18},{18,2},{3,19},{19,3},{4,20},{20... | collective-permute-start | bytes 491528 | tf_op jit(solution)/shard_map/ppermute | solution.py:351
  39.6 5.0 %collective-permute-done.7.refs_9_ = bf16[64,1280]{1,0:T(8,128)(2,1)S(1)} collective-permute-done((bf16[64,1280]{1,0:T(8,128)(2,1)S(1)}, bf16[64,1280]{1,0:T(8,128)(2,1)S(1)}, u32[]{:S(2)}, u32[]{:S(2)}) %collective-permute-start.7) | collective-permute-done | bytes 163872 | tf_op jit(solution)/shard_map/ppermute | solution.py:351
  45.9 1.9 %collective-permute-done.2.refs_0_ = bf16[64,3968]{1,0:T(8,128)(2,1)S(1)} collective-permute-done((bf16[64,3968]{1,0:T(8,128)(2,1)S(1)}, bf16[64,3968]{1,0:T(8,128)(2,1)S(1)}, u32[]{:S(2)}, u32[]{:S(2)}) %collective-permute-start.2) | collective-permute-done | bytes 507936 | tf_op jit(solution)/shard_map/ppermute | solution.py:342
  48.8 1.8 %collective-permute-start.9 = (bf16[128,1280]{1,0:T(8,128)(2,1)S(1)}, bf16[128,1280]{1,0:T(8,128)(2,1)S(1)}, u32[]{:S(2)}, u32[]{:S(2)}) collective-permute-start(bf16[128,1280]{1,0:T(8,128)(2,1)S(1)} %pad_maximum_fusion.2), channel_id=1, source_target_pairs={{0,16},{16,0},{1,17},{17,1},{2,18},{18,2},{3,19},{19,3},{4,20},{20... | collective-permute-start | bytes 983048 | tf_op jit(solution)/shard_map/ppermute | solution.py:351
  50.6 1.5 collective-permute-start.8
  52.2 8.4 %shard_map.105 = bf16[512,512]{1,0:T(8,128)(2,1)} custom-call(s32[1]{0:T(128)} %bitcast.x_ref, bf16[512,512]{1,0:T(8,128)(2,1)S(1)} %copy-done.5, bf16[512,512]{1,0:T(8,128)(2,1)S(1)} %copy-done.1, bf16[512,512]{1,0:T(8,128)(2,1)S(1)} %copy-done.2, f32[512,1]{1,0:T(8,128)S(1)} %copy.11.down, f32[1,512]{1,0:T(1,128)S(1)} %bitcast.38, ...), custom_call_target="tpu_custom_call" | custom-call | flops 6442450944 | bytes 3670016 | tf_op jit(solution)/shard_map/pallas_call | solution.py:288
  61.1 5.4 %shard_map.106 = (bf16[192,5120]{1,0:T(8,128)(2,1)S(1)}, bf16[192,128]{1,0:T(8,128)(2,1)S(1)}, bf16[192,5248]{1,0:T(8,128)(2,1)S(1)}, bf16[6,64,64]{2,1,0:T(8,128)(2,1)S(1)}) custom-call(s32[2]{0:T(128)S(1)} %pad_add_fusion.s_ref, bf16[64,3968]{1,0:T(8,128)(2,1)S(1)} %collective-permute-done.refs_0_, bf16[64,3968]{1,0:T(8,128)(2,1)} %collective-permute-done.4.refs_1_, ...), custom_call_target="tpu_custom_call" | custom-call | flops 2516582400 | bytes 7864320 | tf_op jit(solution)/shard_map/pallas_call | solution.py:189
  67.8 2.4 %shard_map.107 = (bf16[64,5120]{1,0:T(8,128)(2,1)S(1)}, bf16[64,128]{1,0:T(8,128)(2,1)S(1)}, bf16[64,5248]{1,0:T(8,128)(2,1)S(1)}, bf16[2,64,64]{2,1,0:T(8,128)(2,1)S(1)}) custom-call(s32[2]{0:T(128)S(1)} %pad_add_fusion.s_ref, bf16[64,3968]{1,0:T(8,128)(2,1)S(1)} %collective-permute-done.2.refs_0_, bf16[64,3968]{1,0:T(8,128)(2,1)S(1)} %collective-permute-done.8.refs_1_, ...), custom_call_target="tpu_custom_call" | custom-call | flops 838860800 | bytes 2621440 | tf_op jit(solution)/shard_map/pallas_call | solution.py:189
  70.5 2.2 %fusion.6 = f32[256,768]{1,0:T(8,128)S(1)} fusion(bf16[256,5120]{1,0:T(8,128)(2,1)S(1)} %constant_dynamic-update-slice_fusion.2, bf16[1,2,5120,768]{3,2,1,0:T(8,128)(2,1)S(1)} %bitcast.42), kind=kOutput, calls=%fused_computation.6 | convolution fusion | flops 2013265920 | bytes 11272192 | tf_op jit(solution)/shard_map/dot_general | solution.py:543
  72.7 2.2 %fusion.10 = f32[256,768]{1,0:T(8,128)S(1)} fusion(bf16[256,5120]{1,0:T(8,128)(2,1)S(1)} %constant_dynamic-update-slice_fusion.2, bf16[1,2,5120,768]{3,2,1,0:T(8,128)(2,1)S(1)} %bitcast.42), kind=kOutput, calls=%fused_computation.10 | convolution fusion | flops 2013265920 | bytes 11272192 | tf_op jit(solution)/shard_map/dot_general | solution.py:542
  75.3 2.3 %fusion.25.near = bf16[256,5120]{1,0:T(8,128)(2,1)S(1)} fusion(bf16[256,768]{1,0:T(8,128)(2,1)S(1)} %multiply_convert_fusion.1, bf16[1,768,5120]{2,1,0:T(8,128)(2,1)S(1)} %bitcast.44, f32[256]{0:T(256)S(1)} %select_reduce_fusion.1), kind=kOutput, calls=%fused_computation.19 | convolution fusion | flops 2015887360 | bytes 10880000 | tf_op jit(solution)/shard_map/dot_general | solution.py:550
  77.9 2.2 %fusion.4 = f32[256,768]{1,0:T(8,128)S(1)} fusion(bf16[1,2,5120,768]{3,2,1,0:T(8,128)(2,1)S(1)} %bitcast.42, bf16[256,5248]{1,0:T(8,128)(2,1)S(1)} %pad_maximum_fusion), kind=kOutput, calls=%fused_computation.4 | convolution fusion | flops 2013265920 | bytes 11272192 | tf_op jit(solution)/shard_map/dot_general | solution.py:543
  80.2 2.2 %fusion.8 = f32[256,768]{1,0:T(8,128)S(1)} fusion(bf16[1,2,5120,768]{3,2,1,0:T(8,128)(2,1)S(1)} %bitcast.42, bf16[256,5248]{1,0:T(8,128)(2,1)S(1)} %pad_maximum_fusion), kind=kOutput, calls=%fused_computation.8 | convolution fusion | flops 2013265920 | bytes 11272192 | tf_op jit(solution)/shard_map/dot_general | solution.py:542
  82.7 2.4 %fusion.22 = bf16[256,5120]{1,0:T(8,128)(2,1)S(1)} fusion(bf16[256,768]{1,0:T(8,128)(2,1)S(1)} %multiply_convert_fusion, bf16[1,768,5120]{2,1,0:T(8,128)(2,1)S(1)} %bitcast.44, f32[256]{0:T(256)S(1)} %select_reduce_fusion), kind=kOutput, calls=%fused_computation.18 | convolution fusion | flops 2015887360 | bytes 10880000 | tf_op jit(solution)/shard_map/dot_general | solution.py:550
  85.8 2.7 %collective-permute-done.14.far = bf16[128,5120]{1,0:T(8,128)(2,1)S(1)} collective-permute-done((bf16[128,5120]{1,0:T(8,128)(2,1)S(1)}, bf16[128,5120]{1,0:T(8,128)(2,1)S(1)}, u32[]{:S(2)}, u32[]{:S(2)}) %collective-permute-start.14) | collective-permute-done | bytes 1310752 | tf_op jit(solution)/shard_map/ppermute | solution.py:348
  92.8 10.0 %collective-permute-done.18.refs_0_ = bf16[128,1792]{1,0:T(8,128)(2,1)S(1)} collective-permute-done((bf16[128,1792]{1,0:T(8,128)(2,1)S(1)}, bf16[128,1792]{1,0:T(8,128)(2,1)S(1)}, u32[]{:S(2)}, u32[]{:S(2)}) %collective-permute-start.18) | collective-permute-done | bytes 458784 | tf_op jit(solution)/shard_map/ppermute | solution.py:351
  104.8 7.8 %collective-permute-done.17.refs_0_ = bf16[128,1792]{1,0:T(8,128)(2,1)S(1)} collective-permute-done((bf16[128,1792]{1,0:T(8,128)(2,1)S(1)}, bf16[128,1792]{1,0:T(8,128)(2,1)S(1)}, u32[]{:S(2)}, u32[]{:S(2)}) %collective-permute-start.17) | collective-permute-done | bytes 458784 | tf_op jit(solution)/shard_map/ppermute | solution.py:351
  116.6 5.8 %collective-permute-done.21.refs_0_ = bf16[128,1792]{1,0:T(8,128)(2,1)S(1)} collective-permute-done((bf16[128,1792]{1,0:T(8,128)(2,1)S(1)}, bf16[128,1792]{1,0:T(8,128)(2,1)S(1)}, u32[]{:S(2)}, u32[]{:S(2)}) %collective-permute-start.21) | collective-permute-done | bytes 458784 | tf_op jit(solution)/shard_map/ppermute | solution.py:351
  123.9 2.1 %collective-permute-start.23 = (bf16[64,3328]{1,0:T(8,128)(2,1)S(1)}, bf16[64,3328]{1,0:T(8,128)(2,1)S(1)}, u32[]{:S(2)}, u32[]{:S(2)}) collective-permute-start(bf16[64,3328]{1,0:T(8,128)(2,1)S(1)} %shard_map.115), channel_id=1, source_target_pairs={{0,12},{1,13},{2,14},{3,15},{4,0},{5,1},{6,2},{7,3},{8,4},{9,5},{1... | collective-permute-start | bytes 1277960 | tf_op jit(solution)/shard_map/ppermute | solution.py:342
  127.7 3.8 %collective-permute-done.16.refs_0_ = bf16[128,1792]{1,0:T(8,128)(2,1)S(1)} collective-permute-done((bf16[128,1792]{1,0:T(8,128)(2,1)S(1)}, bf16[128,1792]{1,0:T(8,128)(2,1)S(1)}, u32[]{:S(2)}, u32[]{:S(2)}) %collective-permute-start.16) | collective-permute-done | bytes 458784 | tf_op jit(solution)/shard_map/ppermute | solution.py:351
  131.5 1.6 %collective-permute-done.23 = bf16[64,3328]{1,0:T(8,128)(2,1)S(1)} collective-permute-done((bf16[64,3328]{1,0:T(8,128)(2,1)S(1)}, bf16[64,3328]{1,0:T(8,128)(2,1)S(1)}, u32[]{:S(2)}, u32[]{:S(2)}) %collective-permute-start.23) | collective-permute-done | bytes 426016 | tf_op jit(solution)/shard_map/ppermute | solution.py:342
  134.4 1.7 %collective-permute-done.25.refs_1_ = bf16[64,3328]{1,0:T(8,128)(2,1)S(1)} collective-permute-done((bf16[64,3328]{1,0:T(8,128)(2,1)S(1)}, bf16[64,3328]{1,0:T(8,128)(2,1)S(1)}, u32[]{:S(2)}, u32[]{:S(2)}) %collective-permute-start.25) | collective-permute-done | bytes 426016 | tf_op jit(solution)/shard_map/ppermute | solution.py:345
  137.5 6.6 %collective-permute-done.24.refs_1_ = bf16[64,3328]{1,0:T(8,128)(2,1)S(1)} collective-permute-done((bf16[64,3328]{1,0:T(8,128)(2,1)S(1)}, bf16[64,3328]{1,0:T(8,128)(2,1)S(1)}, u32[]{:S(2)}, u32[]{:S(2)}) %collective-permute-start.24) | collective-permute-done | bytes 426016 | tf_op jit(solution)/shard_map/ppermute | solution.py:345
  144.3 2.0 %collective-permute-done.26 = bf16[64,3328]{1,0:T(8,128)(2,1)S(1)} collective-permute-done((bf16[64,3328]{1,0:T(8,128)(2,1)S(1)}, bf16[64,3328]{1,0:T(8,128)(2,1)S(1)}, u32[]{:S(2)}, u32[]{:S(2)}) %collective-permute-start.26) | collective-permute-done | bytes 426016 | tf_op jit(solution)/shard_map/ppermute | solution.py:342
  147.8 3.4 %collective-permute-done.27 = bf16[64,768]{1,0:T(8,128)(2,1)S(1)} collective-permute-done((bf16[64,768]{1,0:T(8,128)(2,1)S(1)}, bf16[64,768]{1,0:T(8,128)(2,1)S(1)}, u32[]{:S(2)}, u32[]{:S(2)}) %collective-permute-start.27) | collective-permute-done | bytes 98336 | tf_op jit(solution)/shard_map/ppermute | solution.py:351
  (107 shorter events, 32.3 us)
Async XLA Ops:
  3.3 31.6 %copy-start.6 = (bf16[64,3968]{1,0:T(8,128)(2,1)}, bf16[64,3968]{1,0:T(8,128)(2,1)S(1)}, u32[]{:S(2)}) copy-start(bf16[64,3968]{1,0:T(8,128)(2,1)S(1)} %get-tuple-element.60.refs_4_) | copy-start | bytes 1523716
  3.3 19.7 %collective-permute-start.3 = (bf16[64,3968]{1,0:T(8,128)(2,1)S(1)}, bf16[64,3968]{1,0:T(8,128)(2,1)S(1)}, u32[]{:S(2)}, u32[]{:S(2)}) collective-permute-start(bf16[64,3968]{1,0:T(8,128)(2,1)S(1)} %get-tuple-element.60.refs_4_), channel_id=1, source_target_pairs={{0,2},{1,3},{2,0},{3,1},{4,6},{5,7},{6,4},{7,5},{8,10},{9,11},{10,... | collective-permute-start | bytes 1523720 | tf_op jit(solution)/shard_map/ppermute | solution.py:345
  6.3 14.9 %collective-permute-start = (bf16[64,3968]{1,0:T(8,128)(2,1)S(1)}, bf16[64,3968]{1,0:T(8,128)(2,1)S(1)}, u32[]{:S(2)}, u32[]{:S(2)}) collective-permute-start(bf16[64,3968]{1,0:T(8,128)(2,1)S(1)} %get-tuple-element.60.refs_4_), channel_id=1, source_target_pairs={{0,4},{1,5},{2,6},{3,7},{4,8},{5,9},{6,10},{7,11},{8,12},{9,13},{1... | collective-permute-start | bytes 1523720 | tf_op jit(solution)/shard_map/ppermute | solution.py:342
  8.7 43.4 %copy-start.1 = (bf16[512,512]{1,0:T(8,128)(2,1)S(1)}, bf16[512,512]{1,0:T(8,128)(2,1)}, u32[]{:S(2)}) copy-start(bf16[512,512]{1,0:T(8,128)(2,1)} %k) | copy-start | bytes 1572868
  8.7 43.4 %copy-start.2 = (bf16[512,512]{1,0:T(8,128)(2,1)S(1)}, bf16[512,512]{1,0:T(8,128)(2,1)}, u32[]{:S(2)}) copy-start(bf16[512,512]{1,0:T(8,128)(2,1)} %v.1) | copy-start | bytes 1572868
  11.0 26.2 %collective-permute-start.6 = (bf16[1040,512]{1,0:T(8,128)(2,1)}, bf16[1040,512]{1,0:T(8,128)(2,1)}, u32[]{:S(2)}, u32[]{:S(2)}) collective-permute-start(bf16[1040,512]{1,0:T(8,128)(2,1)} %pad_maximum_fusion.1), channel_id=1, source_target_pairs={{0,16},{1,17},{2,18},{3,19},{4,20},{5,21},{6,22},{7,23},{8,24},{9,... | collective-permute-start | bytes 3194888 | tf_op jit(solution)/shard_map/ppermute | solution.py:506
  21.2 12.2 %collective-permute-start.1 = (bf16[64,3968]{1,0:T(8,128)(2,1)S(1)}, bf16[64,3968]{1,0:T(8,128)(2,1)S(1)}, u32[]{:S(2)}, u32[]{:S(2)}) collective-permute-start(bf16[64,3968]{1,0:T(8,128)(2,1)S(1)} %get-tuple-element.60.refs_4_), channel_id=1, source_target_pairs={{0,12},{1,13},{2,14},{3,15},{4,0},{5,1},{6,2},{7,3},{8,4},{9,5},{1... | collective-permute-start | bytes 1523720 | tf_op jit(solution)/shard_map/ppermute | solution.py:342
  23.0 11.9 %collective-permute-start.4 = (bf16[64,3968]{1,0:T(8,128)(2,1)S(1)}, bf16[64,3968]{1,0:T(8,128)(2,1)}, u32[]{:S(2)}, u32[]{:S(2)}) collective-permute-start(bf16[64,3968]{1,0:T(8,128)(2,1)S(1)} %collective-permute-done.refs_0_), channel_id=1, source_target_pairs={{0,2},{1,3},{2,0},{3,1},{4,6},{5,7},{6,4},{7,5},{8,10},{9,11},{10,... | collective-permute-start | bytes 1523720 | tf_op jit(solution)/shard_map/ppermute | solution.py:345
  34.9 11.0 %collective-permute-start.5 = (bf16[64,3968]{1,0:T(8,128)(2,1)S(1)}, bf16[64,3968]{1,0:T(8,128)(2,1)}, u32[]{:S(2)}, u32[]{:S(2)}) collective-permute-start(bf16[64,3968]{1,0:T(8,128)(2,1)S(1)} %collective-permute-done.1.refs_2_), channel_id=1, source_target_pairs={{0,2},{1,3},{2,0},{3,1},{4,6},{5,7},{6,4},{7,5},{8,10},{9,11},{10,... | collective-permute-start | bytes 1523720 | tf_op jit(solution)/shard_map/ppermute | solution.py:345
  35.4 12.4 %collective-permute-start.2 = (bf16[64,3968]{1,0:T(8,128)(2,1)S(1)}, bf16[64,3968]{1,0:T(8,128)(2,1)S(1)}, u32[]{:S(2)}, u32[]{:S(2)}) collective-permute-start(bf16[64,3968]{1,0:T(8,128)(2,1)S(1)} %collective-permute-done.refs_0_), channel_id=1, source_target_pairs={{0,4},{1,5},{2,6},{3,7},{4,8},{5,9},{6,10},{7,11},{8,12},{9,13},{1... | collective-permute-start | bytes 1523720 | tf_op jit(solution)/shard_map/ppermute | solution.py:342
  37.3 7.4 %collective-permute-start.7 = (bf16[64,1280]{1,0:T(8,128)(2,1)S(1)}, bf16[64,1280]{1,0:T(8,128)(2,1)S(1)}, u32[]{:S(2)}, u32[]{:S(2)}) collective-permute-start(bf16[64,1280]{1,0:T(8,128)(2,1)S(1)} %slice.52), channel_id=1, source_target_pairs={{0,16},{16,0},{1,17},{17,1},{2,18},{18,2},{3,19},{19,3},{4,20},{20... | collective-permute-start | bytes 491528 | tf_op jit(solution)/shard_map/ppermute | solution.py:351
  39.5 21.0 %collective-permute-start.10 = (bf16[128,1280]{1,0:T(8,128)(2,1)S(1)}, bf16[128,1280]{1,0:T(8,128)(2,1)S(1)}, u32[]{:S(2)}, u32[]{:S(2)}) collective-permute-start(bf16[128,1280]{1,0:T(8,128)(2,1)S(1)} %pad_maximum_fusion.3), channel_id=1, source_target_pairs={{0,16},{16,0},{1,17},{17,1},{2,18},{18,2},{3,19},{19,3},{4,20},{20... | collective-permute-start | bytes 983048 | tf_op jit(solution)/shard_map/ppermute | solution.py:351
  48.8 11.8 %collective-permute-start.9 = (bf16[128,1280]{1,0:T(8,128)(2,1)S(1)}, bf16[128,1280]{1,0:T(8,128)(2,1)S(1)}, u32[]{:S(2)}, u32[]{:S(2)}) collective-permute-start(bf16[128,1280]{1,0:T(8,128)(2,1)S(1)} %pad_maximum_fusion.2), channel_id=1, source_target_pairs={{0,16},{16,0},{1,17},{17,1},{2,18},{18,2},{3,19},{19,3},{4,20},{20... | collective-permute-start | bytes 983048 | tf_op jit(solution)/shard_map/ppermute | solution.py:351
  50.6 10.0 %collective-permute-start.8 = (bf16[64,3968]{1,0:T(8,128)(2,1)S(1)}, bf16[64,3968]{1,0:T(8,128)(2,1)S(1)}, u32[]{:S(2)}, u32[]{:S(2)}) collective-permute-start(bf16[64,3968]{1,0:T(8,128)(2,1)S(1)} %collective-permute-done.2.refs_0_), channel_id=1, source_target_pairs={{0,2},{1,3},{2,0},{3,1},{4,6},{5,7},{6,4},{7,5},{8,10},{9,11},{10,... | collective-permute-start | bytes 1523720 | tf_op jit(solution)/shard_map/ppermute | solution.py:345
  52.1 18.3 %slice-start = ((s8[15728640]{0:T(1024)(128)(4,1)}), s8[4194304]{0:T(1024)(128)(4,1)S(1)}, s32[]{:S(2)}) async-start(s8[15728640]{0:T(1024)(128)(4,1)} %bitcast.41), calls=%async_computation | async-start | bytes 8388608
  60.7 7.1 %collective-permute-start.11 = (bf16[128,1280]{1,0:T(8,128)(2,1)S(1)}, bf16[128,1280]{1,0:T(8,128)(2,1)S(1)}, u32[]{:S(2)}, u32[]{:S(2)}) collective-permute-start(bf16[128,1280]{1,0:T(8,128)(2,1)S(1)} %pad_maximum_fusion.4), channel_id=1, source_target_pairs={{0,16},{16,0},{1,17},{17,1},{2,18},{18,2},{3,19},{19,3},{4,20},{20... | collective-permute-start | bytes 983048 | tf_op jit(solution)/shard_map/ppermute | solution.py:351
  66.6 11.1 %collective-permute-start.13 = (bf16[192,5248]{1,0:T(8,128)(2,1)S(1)}, bf16[192,5248]{1,0:T(8,128)(2,1)S(1)}, u32[]{:S(2)}, u32[]{:S(2)}) collective-permute-start(bf16[192,5248]{1,0:T(8,128)(2,1)S(1)} %get-tuple-element.93), channel_id=1, source_target_pairs={{0,1},{1,0},{2,3},{3,2},{4,5},{5,4},{6,7},{7,6},{8,9},{9,8},{10,11... | collective-permute-start | bytes 6045704 | tf_op jit(solution)/shard_map/ppermute | solution.py:348
  70.2 7.4 %collective-permute-start.12 = (bf16[64,5248]{1,0:T(8,128)(2,1)S(1)}, bf16[64,5248]{1,0:T(8,128)(2,1)S(1)}, u32[]{:S(2)}, u32[]{:S(2)}) collective-permute-start(bf16[64,5248]{1,0:T(8,128)(2,1)S(1)} %get-tuple-element.92), channel_id=1, source_target_pairs={{0,1},{1,0},{2,3},{3,2},{4,5},{5,4},{6,7},{7,6},{8,9},{9,8},{10,11... | collective-permute-start | bytes 2015240 | tf_op jit(solution)/shard_map/ppermute | solution.py:348
  85.3 3.2 %collective-permute-start.14 = (bf16[128,5120]{1,0:T(8,128)(2,1)S(1)}, bf16[128,5120]{1,0:T(8,128)(2,1)S(1)}, u32[]{:S(2)}, u32[]{:S(2)}) collective-permute-start(bf16[128,5120]{1,0:T(8,128)(2,1)S(1)} %get-tuple-element.119), channel_id=1, source_target_pairs={{0,1},{1,0},{2,3},{3,2},{4,5},{5,4},{6,7},{7,6},{8,9},{9,8},{10,11... | collective-permute-start | bytes 3932168 | tf_op jit(solution)/shard_map/ppermute | solution.py:348
  88.5 3.4 %collective-permute-start.15 = (bf16[128,5120]{1,0:T(8,128)(2,1)S(1)}, bf16[128,5120]{1,0:T(8,128)(2,1)S(1)}, u32[]{:S(2)}, u32[]{:S(2)}) collective-permute-start(bf16[128,5120]{1,0:T(8,128)(2,1)S(1)} %get-tuple-element.103), channel_id=1, source_target_pairs={{0,1},{1,0},{2,3},{3,2},{4,5},{5,4},{6,7},{7,6},{8,9},{9,8},{10,11... | collective-permute-start | bytes 3932168 | tf_op jit(solution)/shard_map/ppermute | solution.py:348
  89.3 13.4 %collective-permute-start.18 = (bf16[128,1792]{1,0:T(8,128)(2,1)S(1)}, bf16[128,1792]{1,0:T(8,128)(2,1)S(1)}, u32[]{:S(2)}, u32[]{:S(2)}) collective-permute-start(bf16[128,1792]{1,0:T(8,128)(2,1)S(1)} %shard_map.108), channel_id=1, source_target_pairs={{0,16},{16,0},{1,17},{17,1},{2,18},{18,2},{3,19},{19,3},{4,20},{20... | collective-permute-start | bytes 1376264 | tf_op jit(solution)/shard_map/ppermute | solution.py:351
  90.5 22.1 %collective-permute-start.17 = (bf16[128,1792]{1,0:T(8,128)(2,1)S(1)}, bf16[128,1792]{1,0:T(8,128)(2,1)S(1)}, u32[]{:S(2)}, u32[]{:S(2)}) collective-permute-start(bf16[128,1792]{1,0:T(8,128)(2,1)S(1)} %shard_map.109), channel_id=1, source_target_pairs={{0,16},{16,0},{1,17},{17,1},{2,18},{18,2},{3,19},{19,3},{4,20},{20... | collective-permute-start | bytes 1376264 | tf_op jit(solution)/shard_map/ppermute | solution.py:351
  103.0 10.3 %collective-permute-start.19 = (bf16[64,3328]{1,0:T(8,128)(2,1)S(1)}, bf16[64,3328]{1,0:T(8,128)(2,1)S(1)}, u32[]{:S(2)}, u32[]{:S(2)}) collective-permute-start(bf16[64,3328]{1,0:T(8,128)(2,1)S(1)} %shard_map.112), channel_id=1, source_target_pairs={{0,2},{1,3},{2,0},{3,1},{4,6},{5,7},{6,4},{7,5},{8,10},{9,11},{10,... | collective-permute-start | bytes 1277960 | tf_op jit(solution)/shard_map/ppermute | solution.py:345
  104.1 18.3 %collective-permute-start.21 = (bf16[128,1792]{1,0:T(8,128)(2,1)S(1)}, bf16[128,1792]{1,0:T(8,128)(2,1)S(1)}, u32[]{:S(2)}, u32[]{:S(2)}) collective-permute-start(bf16[128,1792]{1,0:T(8,128)(2,1)S(1)} %shard_map.110), channel_id=1, source_target_pairs={{0,16},{16,0},{1,17},{17,1},{2,18},{18,2},{3,19},{19,3},{4,20},{20... | collective-permute-start | bytes 1376264 | tf_op jit(solution)/shard_map/ppermute | solution.py:351
  113.6 9.8 %collective-permute-start.22 = (bf16[64,3328]{1,0:T(8,128)(2,1)S(1)}, bf16[64,3328]{1,0:T(8,128)(2,1)S(1)}, u32[]{:S(2)}, u32[]{:S(2)}) collective-permute-start(bf16[64,3328]{1,0:T(8,128)(2,1)S(1)} %shard_map.114), channel_id=1, source_target_pairs={{0,12},{1,13},{2,14},{3,15},{4,0},{5,1},{6,2},{7,3},{8,4},{9,5},{1... | collective-permute-start | bytes 1277960 | tf_op jit(solution)/shard_map/ppermute | solution.py:342
  114.1 9.5 %collective-permute-start.20 = (bf16[64,3328]{1,0:T(8,128)(2,1)S(1)}, bf16[64,3328]{1,0:T(8,128)(2,1)S(1)}, u32[]{:S(2)}, u32[]{:S(2)}) collective-permute-start(bf16[64,3328]{1,0:T(8,128)(2,1)S(1)} %shard_map.113), channel_id=1, source_target_pairs={{0,2},{1,3},{2,0},{3,1},{4,6},{5,7},{6,4},{7,5},{8,10},{9,11},{10,... | collective-permute-start | bytes 1277960 | tf_op jit(solution)/shard_map/ppermute | solution.py:345
  115.4 16.0 %collective-permute-start.16 = (bf16[128,1792]{1,0:T(8,128)(2,1)S(1)}, bf16[128,1792]{1,0:T(8,128)(2,1)S(1)}, u32[]{:S(2)}, u32[]{:S(2)}) collective-permute-start(bf16[128,1792]{1,0:T(8,128)(2,1)S(1)} %shard_map.111), channel_id=1, source_target_pairs={{0,16},{16,0},{1,17},{17,1},{2,18},{18,2},{3,19},{19,3},{4,20},{20... | collective-permute-start | bytes 1376264 | tf_op jit(solution)/shard_map/ppermute | solution.py:351
  123.9 9.1 %collective-permute-start.23 = (bf16[64,3328]{1,0:T(8,128)(2,1)S(1)}, bf16[64,3328]{1,0:T(8,128)(2,1)S(1)}, u32[]{:S(2)}, u32[]{:S(2)}) collective-permute-start(bf16[64,3328]{1,0:T(8,128)(2,1)S(1)} %shard_map.115), channel_id=1, source_target_pairs={{0,12},{1,13},{2,14},{3,15},{4,0},{5,1},{6,2},{7,3},{8,4},{9,5},{1... | collective-permute-start | bytes 1277960 | tf_op jit(solution)/shard_map/ppermute | solution.py:342
  126.3 9.8 %collective-permute-start.25 = (bf16[64,3328]{1,0:T(8,128)(2,1)S(1)}, bf16[64,3328]{1,0:T(8,128)(2,1)S(1)}, u32[]{:S(2)}, u32[]{:S(2)}) collective-permute-start(bf16[64,3328]{1,0:T(8,128)(2,1)S(1)} %shard_map.118), channel_id=1, source_target_pairs={{0,2},{1,3},{2,0},{3,1},{4,6},{5,7},{6,4},{7,5},{8,10},{9,11},{10,... | collective-permute-start | bytes 1277960 | tf_op jit(solution)/shard_map/ppermute | solution.py:345
  133.3 10.8 %collective-permute-start.24 = (bf16[64,3328]{1,0:T(8,128)(2,1)S(1)}, bf16[64,3328]{1,0:T(8,128)(2,1)S(1)}, u32[]{:S(2)}, u32[]{:S(2)}) collective-permute-start(bf16[64,3328]{1,0:T(8,128)(2,1)S(1)} %shard_map.116), channel_id=1, source_target_pairs={{0,2},{1,3},{2,0},{3,1},{4,6},{5,7},{6,4},{7,5},{8,10},{9,11},{10,... | collective-permute-start | bytes 1277960 | tf_op jit(solution)/shard_map/ppermute | solution.py:345
  136.4 10.0 %collective-permute-start.26 = (bf16[64,3328]{1,0:T(8,128)(2,1)S(1)}, bf16[64,3328]{1,0:T(8,128)(2,1)S(1)}, u32[]{:S(2)}, u32[]{:S(2)}) collective-permute-start(bf16[64,3328]{1,0:T(8,128)(2,1)S(1)} %shard_map.119), channel_id=1, source_target_pairs={{0,4},{1,5},{2,6},{3,7},{4,8},{5,9},{6,10},{7,11},{8,12},{9,13},{1... | collective-permute-start | bytes 1277960 | tf_op jit(solution)/shard_map/ppermute | solution.py:342
  146.5 4.7 %collective-permute-start.27 = (bf16[64,768]{1,0:T(8,128)(2,1)S(1)}, bf16[64,768]{1,0:T(8,128)(2,1)S(1)}, u32[]{:S(2)}, u32[]{:S(2)}) collective-permute-start(bf16[64,768]{1,0:T(8,128)(2,1)S(1)} %slice.72), channel_id=1, source_target_pairs={{0,16},{16,0},{1,17},{17,1},{2,18},{18,2},{3,19},{19,3},{4,20},{20... | collective-permute-start | bytes 294920 | tf_op jit(solution)/shard_map/ppermute | solution.py:351
  (10 other events, 80.8 us)
